TPU v7x, 32 devices: a whole 2x2x4 slice. The times are simulated.
32 devices in a mesh: rep: 4 (over x, core), grp: 8 (over z, y).
Axes of the slice: x: 2, y: 2, z: 4, core: 2. Of those that a mesh axis runs over, the one named last changes fastest.
Arguments:
- tokens: bfloat16 [4, 1024, 2048], P('rep', 'grp'), may hold values from -6 to 6
- q_weight: bfloat16 [2048, 2048], P('grp'), may hold values from -0.125 to 0.125
- k_weight: bfloat16 [2048, 2048], P('grp'), may hold values from -0.125 to 0.125
- v_weight: bfloat16 [2048, 2048], P('grp'), may hold values from -0.125 to 0.125
- o_weight: bfloat16 [2048, 2048], P('grp'), may hold values from -0.125 to 0.125
- gate_weight: bfloat16 [2048, 8192], P('grp'), may hold values from -0.125 to 0.125
- up_weight: bfloat16 [2048, 8192], P('grp'), may hold values from -0.125 to 0.125
- down_weight: bfloat16 [8192, 2048], P(None, 'grp'), may hold values from -0.0625 to 0.0625
- q_gain: bfloat16 [2048], P('grp'), may hold values from 0.5 to 1.5
- k_gain: bfloat16 [2048], P('grp'), may hold values from 0.5 to 1.5
- attn_gain: bfloat16 [2048], P('grp'), may hold values from 0.5 to 1.5
- mlp_gain: bfloat16 [2048], P('grp'), may hold values from 0.5 to 1.5
- cotangent: bfloat16 [4, 1024, 2048], P('rep', 'grp'), may hold values from -6 to 6
Outputs:
- outputs: bfloat16 [4, 1024, 2048], P('rep', 'grp')
- d_tokens: bfloat16 [4, 1024, 2048], P('rep', 'grp')
- q_grad: float32 [2048, 2048], P('grp')
- k_grad: float32 [2048, 2048], P('grp')
- v_grad: float32 [2048, 2048], P('grp')
- o_grad: float32 [2048, 2048], P('grp')
- gate_grad: float32 [2048, 8192], P('grp')
- up_grad: float32 [2048, 8192], P('grp')
- down_grad: float32 [8192, 2048], P(None, 'grp')
- q_gain_grad: float32 [2048], P('grp')
- k_gain_grad: float32 [2048], P('grp')
- attn_gain_grad: float32 [2048], P('grp')
- mlp_gain_grad: float32 [2048], P('grp')
All inputs are finite; a program needn't handle non-finite values.
Results may differ from a plain program's by a relative error of at most 0.017.
Values may be sent and summed in bfloat16 or wider, within the bound.
No kernel may reach another device: no remote copies, remote signals or barrier semaphores. Data moves between devices by JAX's collectives and lax.ppermute only.
A program may use at most 640 MiB of HBM per device.

v0:
```python
import jax
import jax.numpy as jnp
from jax import lax
from jax.sharding import PartitionSpec as P

HEADS = 16
HEAD = 128


EPS = 1e-06
THETA = 500000.0
GROUPED = 4


def rms_scale(values, gains):
    return values * lax.rsqrt(jnp.mean(values * values, axis=-1, keepdims=True) + EPS) * gains


def rotary(values, places):
    count = values.shape[0]
    heads = values.reshape(count, HEADS, HEAD)
    freqs = THETA ** (-2.0 * jnp.arange(HEAD // 2, dtype=jnp.float32) / HEAD)
    angles = places[:, None] * freqs[None, :]
    cosine = jnp.cos(angles)[:, None, :]
    sine = jnp.sin(angles)[:, None, :]
    first = heads[..., : HEAD // 2]
    second = heads[..., HEAD // 2 :]
    turned = jnp.concatenate(
        [first * cosine - second * sine, second * cosine + first * sine], axis=-1
    )
    return turned.reshape(count, HEADS * HEAD)


def swiglu(gates, uppers):
    return jax.nn.silu(gates) * uppers


def dot_plain(left, right):
    return jnp.dot(left, right, preferred_element_type=jnp.float32)


def dot_right_t(left, right):
    return lax.dot_general(
        left, right, (((1,), (1,)), ((), ())), preferred_element_type=jnp.float32
    )


def dot_left_t(left, right):
    return lax.dot_general(
        left, right, (((0,), (0,)), ((), ())), preferred_element_type=jnp.float32
    )


def head_slice(matrix, index):
    piece = lax.dynamic_slice_in_dim(matrix, index * GROUPED * HEAD, GROUPED * HEAD, 1)
    return piece.reshape(matrix.shape[0], GROUPED, HEAD)


def heads_back(stacked, count):
    return jnp.moveaxis(stacked, 0, 1).reshape(count, HEADS * HEAD)


def on_device(
    tokens,
    q_weight,
    k_weight,
    v_weight,
    o_weight,
    gate_weight,
    up_weight,
    down_weight,
    q_gain,
    k_gain,
    attn_gain,
    mlp_gain,
    cotangent,
):
    inputs = tokens[0]
    rows = inputs.shape[0]
    width = inputs.shape[1]
    hidden_width = gate_weight.shape[1]
    groups = lax.axis_size("grp")
    length = rows * groups
    query_places = lax.axis_index("grp") * rows + jnp.arange(rows, dtype=jnp.int32)
    places = query_places.astype(jnp.float32)
    scale = HEAD ** (-0.5)
    group_ids = jnp.arange(HEADS // GROUPED, dtype=jnp.int32)
    wq_fwd, wk_fwd, wv_fwd, wo_gathered, gq_bf, gk_bf, ga_bf = (
        lax.all_gather(q_weight, "grp", axis=0, tiled=True),
        lax.all_gather(k_weight, "grp", axis=0, tiled=True),
        lax.all_gather(v_weight, "grp", axis=0, tiled=True),
        lax.all_gather(o_weight, "grp", axis=0, tiled=True),
        lax.all_gather(q_gain, "grp", axis=0, tiled=True),
        lax.all_gather(k_gain, "grp", axis=0, tiled=True),
        lax.all_gather(attn_gain, "grp", axis=0, tiled=True),
    )
    gq_full = gq_bf.astype(jnp.float32)
    gk_full = gk_bf.astype(jnp.float32)
    ga_full = ga_bf.astype(jnp.float32)
    q_proj = dot_plain(inputs, wq_fwd)
    k_proj = dot_plain(inputs, wk_fwd)
    v_proj = dot_plain(inputs, wv_fwd)

    def turn_query(values, gains):
        return rotary(rms_scale(values, gains), places)

    queries = turn_query(q_proj, gq_full).astype(jnp.bfloat16)
    keys_own = turn_query(k_proj, gk_full).astype(jnp.bfloat16)
    values_own = v_proj.astype(jnp.bfloat16)
    keys_all, values_all = (
        lax.all_gather(keys_own, "grp", axis=0, tiled=True),
        lax.all_gather(values_own, "grp", axis=0, tiled=True),
    )
    allowed = jnp.arange(length, dtype=jnp.int32)[None, :] <= query_places[:, None]

    def forward_group(index):
        scores = (
            jnp.einsum(
                "qhd,khd->hqk",
                head_slice(queries, index),
                head_slice(keys_all, index),
                preferred_element_type=jnp.float32,
            )
            * scale
        )
        scores = jnp.where(allowed[None], scores, -1e30)
        top_score = jnp.max(scores, axis=-1, keepdims=True)
        weights = jnp.exp(scores - top_score)
        totals = jnp.sum(weights, axis=-1, keepdims=True)
        probs = (weights / totals).astype(jnp.bfloat16)
        mixed = jnp.einsum(
            "hqk,khd->qhd", probs, head_slice(values_all, index), preferred_element_type=jnp.float32
        )
        return (mixed, (top_score + jnp.log(totals))[..., 0])

    mixed_all, log_totals = lax.map(forward_group, group_ids)
    log_totals = log_totals.reshape(HEADS, rows)
    attn_bf = heads_back(mixed_all, rows).astype(jnp.bfloat16)
    a_proj = dot_plain(attn_bf, wo_gathered)
    middle = inputs.astype(jnp.float32) + rms_scale(a_proj, ga_full)
    middle_bf = middle.astype(jnp.bfloat16)
    wg_fwd, wu_fwd, gm_bf = (
        lax.all_gather(gate_weight, "grp", axis=0, tiled=True),
        lax.all_gather(up_weight, "grp", axis=0, tiled=True),
        lax.all_gather(mlp_gain, "grp", axis=0, tiled=True),
    )
    gm_full = gm_bf.astype(jnp.float32)
    gates = dot_plain(middle_bf, wg_fwd)
    uppers = dot_plain(middle_bf, wu_fwd)
    hidden = swiglu(gates, uppers).astype(jnp.bfloat16)
    y_proj = dot_plain(hidden, lax.all_gather(down_weight, "grp", axis=1, tiled=True))
    outputs = (middle + rms_scale(y_proj, gm_full)).astype(jnp.bfloat16)
    grad_out = cotangent[0].astype(jnp.float32)
    unused_y, pull_mlp = jax.vjp(rms_scale, y_proj, gm_full)
    dy_proj, d_mlp_gain = pull_mlp(grad_out)
    dy_bf = dy_proj.astype(jnp.bfloat16)
    down_full = lax.all_gather(down_weight, "grp", axis=1, tiled=True)
    d_hidden = dot_right_t(dy_bf, down_full)
    unused_h, pull_act = jax.vjp(swiglu, gates, uppers)
    d_gates, d_uppers = pull_act(d_hidden)
    dg_bf = d_gates.astype(jnp.bfloat16)
    du_bf = d_uppers.astype(jnp.bfloat16)
    block = dot_right_t(
        dg_bf, lax.all_gather(gate_weight, "grp", axis=0, tiled=True)
    ) + dot_right_t(du_bf, lax.all_gather(up_weight, "grp", axis=0, tiled=True))
    d_middle = grad_out + block
    unused_a, pull_attn = jax.vjp(rms_scale, a_proj, ga_full)
    da_proj, d_attn_gain = pull_attn(d_middle)
    da_bf = da_proj.astype(jnp.bfloat16)
    wq_full, wk_full, wv_full, wo_full = (
        lax.all_gather(q_weight, "grp", axis=0, tiled=True),
        lax.all_gather(k_weight, "grp", axis=0, tiled=True),
        lax.all_gather(v_weight, "grp", axis=0, tiled=True),
        lax.all_gather(o_weight, "grp", axis=0, tiled=True),
    )
    d_attn_bf = dot_right_t(da_bf, wo_full).astype(jnp.bfloat16)

    def query_group(index):
        query_g = head_slice(queries, index)
        key_g = head_slice(keys_all, index)
        dout_g = head_slice(d_attn_bf, index)
        lse_g = lax.dynamic_slice_in_dim(log_totals, index * GROUPED, GROUPED, 0)
        scores = (
            jnp.einsum("qhd,khd->hqk", query_g, key_g, preferred_element_type=jnp.float32) * scale
        )
        scores = jnp.where(allowed[None], scores, -1e30)
        probs = jnp.exp(scores - lse_g[..., None])
        d_probs = jnp.einsum(
            "qhd,khd->hqk",
            dout_g,
            head_slice(values_all, index),
            preferred_element_type=jnp.float32,
        )
        deltas = jnp.sum(probs * d_probs, axis=-1, keepdims=True)
        ds_bf = (probs * (d_probs - deltas)).astype(jnp.bfloat16)
        d_query = (
            jnp.einsum("hqk,khd->qhd", ds_bf, key_g, preferred_element_type=jnp.float32) * scale
        )
        return (d_query, deltas[..., 0])

    d_query_all, delta_all = lax.map(query_group, group_ids)
    d_queries = heads_back(d_query_all, rows)
    delta_all = delta_all.reshape(HEADS, rows)
    key_places = jnp.arange(rows * lax.axis_size("grp"), dtype=jnp.int32)
    permit = key_places[None, :] <= query_places[:, None]

    def key_group(index):
        query_g = head_slice(queries, index)
        dout_g = head_slice(d_attn_bf, index)
        lse_g = lax.dynamic_slice_in_dim(log_totals, index * GROUPED, GROUPED, 0)
        delta_g = lax.dynamic_slice_in_dim(delta_all, index * GROUPED, GROUPED, 0)
        scores = (
            jnp.einsum(
                "qhd,khd->hqk",
                query_g,
                head_slice(keys_all, index),
                preferred_element_type=jnp.float32,
            )
            * scale
        )
        scores = jnp.where(permit[None], scores, -1e30)
        probs = jnp.exp(scores - lse_g[..., None])
        d_value = jnp.einsum(
            "hqk,qhd->khd", probs.astype(jnp.bfloat16), dout_g, preferred_element_type=jnp.float32
        )
        d_probs = jnp.einsum(
            "qhd,khd->hqk",
            dout_g,
            head_slice(values_all, index),
            preferred_element_type=jnp.float32,
        )
        ds_bf = (probs * (d_probs - delta_g[..., None])).astype(jnp.bfloat16)
        d_key = (
            jnp.einsum("hqk,qhd->khd", ds_bf, query_g, preferred_element_type=jnp.float32) * scale
        )
        return (d_key, d_value)

    d_key_all, d_value_all = lax.map(key_group, group_ids)
    key_grads = lax.psum_scatter(
        jnp.concatenate(
            [
                heads_back(d_key_all, rows * lax.axis_size("grp")),
                heads_back(d_value_all, rows * lax.axis_size("grp")),
            ],
            axis=1,
        ),
        "grp",
        scatter_dimension=0,
        tiled=True,
    )
    dv_bf = key_grads[:, width:].astype(jnp.bfloat16)
    unused_q, pull_query = jax.vjp(turn_query, q_proj, gq_full)
    dq_proj, d_q_gain = pull_query(d_queries)
    unused_k, pull_key = jax.vjp(turn_query, k_proj, gk_full)
    dk_proj, d_k_gain = pull_key(key_grads[:, :width])
    dq_bf = dq_proj.astype(jnp.bfloat16)
    dk_bf = dk_proj.astype(jnp.bfloat16)
    d_inputs = (
        d_middle
        + dot_right_t(dq_bf, wq_full)
        + dot_right_t(dk_bf, wk_full)
        + dot_right_t(dv_bf, wv_full)
    )
    owned_rows = width // groups

    def attn_terms(start, count):
        return jnp.concatenate(
            [
                dot_left_t(inputs, dq_bf),
                dot_left_t(inputs, dk_bf),
                dot_left_t(inputs, dv_bf),
                dot_left_t(attn_bf, da_bf),
                dot_left_t(dy_bf, hidden),
            ],
            axis=1,
        )

    def mlp_terms(start, count):
        return jnp.concatenate([dot_left_t(middle_bf, dg_bf), dot_left_t(middle_bf, du_bf)], axis=1)

    def spread(term_fn):
        return lax.psum_scatter(
            term_fn(jnp.int32(0), owned_rows * lax.axis_size("grp")),
            "grp",
            scatter_dimension=0,
            tiled=True,
        )

    attn_part = spread(attn_terms)
    mlp_part = spread(mlp_terms)
    attn_sum, mlp_sum = lax.psum((attn_part, mlp_part), "rep")
    gain_stack = jnp.stack([d_q_gain, d_k_gain, d_attn_gain, d_mlp_gain])
    gain_total = lax.psum(gain_stack, ("rep", "grp"))
    gain_mine = lax.dynamic_slice_in_dim(
        gain_total, lax.axis_index("grp") * owned_rows, owned_rows, 1
    )
    return (
        outputs[None],
        d_inputs.astype(jnp.bfloat16)[None],
        attn_sum[:, :width],
        attn_sum[:, width : 2 * width],
        attn_sum[:, 2 * width : 3 * width],
        attn_sum[:, 3 * width : 4 * width],
        mlp_sum[:, :hidden_width],
        mlp_sum[:, hidden_width:],
        attn_sum[:, 4 * width :].T,
        gain_mine[0],
        gain_mine[1],
        gain_mine[2],
        gain_mine[3],
    )


def solution(mesh):
    return jax.shard_map(
        on_device,
        mesh=mesh,
        in_specs=(
            P("rep", "grp", None),
            P("grp", None),
            P("grp", None),
            P("grp", None),
            P("grp", None),
            P("grp", None),
            P("grp", None),
            P(None, "grp"),
            P("grp"),
            P("grp"),
            P("grp"),
            P("grp"),
            P("rep", "grp", None),
        ),
        out_specs=(
            P("rep", "grp", None),
            P("rep", "grp", None),
            P("grp", None),
            P("grp", None),
            P("grp", None),
            P("grp", None),
            P("grp", None),
            P("grp", None),
            P(None, "grp"),
            P("grp"),
            P("grp"),
            P("grp"),
            P("grp"),
        ),
        check_vma=False,
    )
```

profile of v0, /device:TPU:0, one launch (start us, length us, event | category | flops | bytes accessed | tf_op | source)
XLA Modules:
  0.0 7855.7 jit_solution(7950014953726846352)
XLA Ops:
  9.5 128.3 %all-gather.14.cloned.1.call-done = bf16[2048,2048]{1,0:T(8,128)(2,1)} async-done(((bf16[256,2048]{1,0:T(8,128)(2,1)}), bf16[2048,2048]{1,0:T(8,128)(2,1)}) %all-gather.14.cloned.1.call-update) | async-done | bytes 8388624 | tf_op jit(solution)/shard_map/all_gather | solution.py:91
  143.5 17.7 all-gather.1
  161.3 17.3 all-gather
  179.0 84.3 %all-gather.20.cloned.1.call-done = bf16[2048,2048]{1,0:T(8,128)(2,1)} async-done(((bf16[256,2048]{1,0:T(8,128)(2,1)}), bf16[2048,2048]{1,0:T(8,128)(2,1)}) %all-gather.20.cloned.1.call-update) | async-done | bytes 8388624 | tf_op jit(solution)/shard_map/all_gather | solution.py:90
  269.4 119.2 %all-gather.18.cloned.1.call-done = bf16[2048,2048]{1,0:T(8,128)(2,1)} async-done(((bf16[256,2048]{1,0:T(8,128)(2,1)}), bf16[2048,2048]{1,0:T(8,128)(2,1)}) %all-gather.18.cloned.1.call-update) | async-done | bytes 8388624 | tf_op jit(solution)/shard_map/all_gather | solution.py:89
  400.2 17.8 all-gather.2
  436.4 26.4 all-gather.16.cloned.1.call-done
  469.2 69.4 all-gather.22.cloned.1.call-done
  538.6 25.6 while.48
  564.3 99.5 %all-gather.24.cloned.1.call-done = bf16[2048,2048]{1,0:T(8,128)(2,1)} async-done(((bf16[256,2048]{1,0:T(8,128)(2,1)}), bf16[2048,2048]{1,0:T(8,128)(2,1)}) %all-gather.24.cloned.1.call-update) | async-done | bytes 8388624 | tf_op jit(solution)/shard_map/all_gather | solution.py:92
  668.8 632.5 %all-gather.26.cloned.1.call-done = bf16[2048,8192]{1,0:T(8,128)(2,1)} async-done(((bf16[256,8192]{1,0:T(8,128)(2,1)}), bf16[2048,8192]{1,0:T(8,128)(2,1)}) %all-gather.26.cloned.1.call-update) | async-done | bytes 33554448 | tf_op jit(solution)/shard_map/all_gather | solution.py:143
  1301.2 18.0 fusion.55
  1319.2 621.3 %all-gather.28.cloned.1.call-done = bf16[2048,8192]{1,0:T(8,128)(2,1)} async-done(((bf16[256,8192]{1,0:T(8,128)(2,1)}), bf16[2048,8192]{1,0:T(8,128)(2,1)}) %all-gather.28.cloned.1.call-update) | async-done | bytes 33554448 | tf_op jit(solution)/shard_map/all_gather | solution.py:144
  1940.5 19.9 multiply_convert_fusion.4
  1960.4 620.6 %all-gather.30.cloned.1.call-done = bf16[8192,2048]{1,0:T(8,128)(2,1)} async-done(((bf16[8192,256]{1,0:T(8,128)(2,1)}), bf16[8192,2048]{1,0:T(8,128)(2,1)}) %all-gather.30.cloned.1.call-update) | async-done | bytes 33554448 | tf_op jit(solution)/shard_map/all_gather | solution.py:151
  2597.1 19.9 multiply_convert_fusion.3
  2617.0 17.3 fusion.56
  2634.3 19.7 multiply_reduce_fusion.1
  2663.4 30.6 while.49
  2694.0 46.3 while.50
  2752.8 25.7 fusion.58
  2778.5 24.2 fusion.57
  2802.8 89.0 %pad_maximum_fusion = f32[2048,16384]{1,0:T(8,128)} fusion(f32[2048,8192]{1,0:T(8,128)} %fusion.58, f32[2048,8192]{1,0:T(8,128)} %fusion.57), kind=kLoop, calls=%fused_computation.45 | loop fusion | flops 33554432 | bytes 268435456 | tf_op jit(solution)/shard_map/concatenate | solution.py:279
  2895.9 138.9 %reduce-scatter.4.cloned.1.call-done = f32[128,4096]{0,1:T(8,128)} async-done(((f32[1024,4096]{0,1:T(8,128)}), f32[128,4096]{0,1:T(8,128)}) %reduce-scatter.4.cloned.1.call-update) | async-done | bytes 2097168 | tf_op jit(solution)/shard_map/reduce_scatter | solution.py:239
  3053.8 17.9 copy.102
  3083.7 17.9 copy.103
  3109.7 17.7 copy.104
  3169.1 24.4 convolution_dynamic-update-slice_fusion
  3193.6 1951.5 %reduce-scatter.8.cloned.1.call-done = f32[256,16384]{1,0:T(8,128)} async-done(((f32[2048,16384]{1,0:T(8,128)}), f32[256,16384]{1,0:T(8,128)}) %reduce-scatter.8.cloned.1.call-update) | async-done | bytes 16777232 | tf_op jit(solution)/shard_map/reduce_scatter | solution.py:282
  5145.0 2110.4 %reduce-scatter.6.cloned.1.call-done = f32[256,16384]{1,0:T(8,128)} async-done(((f32[2048,16384]{1,0:T(8,128)}), f32[256,16384]{1,0:T(8,128)}) %reduce-scatter.6.cloned.1.call-update) | async-done | bytes 16777232 | tf_op jit(solution)/shard_map/reduce_scatter | solution.py:282
  7256.2 40.9 psum.23
  7314.7 503.2 %all-reduce.7.cloned.1.call-done = (f32[256,16384]{1,0:T(8,128)}, f32[256,16384]{1,0:T(8,128)}) async-done(((f32[256,16384]{1,0:T(8,128)}, f32[256,16384]{1,0:T(8,128)}), (f32[256,16384]{1,0:T(8,128)}, f32[256,16384]{1,0:T(8,128)})) %all-reduce.7.cloned.1.call-update) | async-done | bytes 33554448 | tf_op jit(solution)/shard_map/psum | solution.py:291
  (322 shorter events, 316.4 us)
Async XLA Ops:
  7.2 130.6 %all-gather.14.cloned.1.call-start = ((), (), s32[]{:S(2)}) async-start(), calls=%async_computation.3 | async-start | bytes 9437184 | tf_op jit(solution)/shard_map/all_gather | solution.py:91
  7.9 255.3 %all-gather.20.cloned.1.call-start = ((), (), s32[]{:S(2)}) async-start(), calls=%async_computation.6 | async-start | bytes 9437184 | tf_op jit(solution)/shard_map/all_gather | solution.py:90
  8.7 379.9 %all-gather.18.cloned.1.call-start = ((), (), s32[]{:S(2)}) async-start(), calls=%async_computation.5 | async-start | bytes 9437184 | tf_op jit(solution)/shard_map/all_gather | solution.py:89
  9.4 134.1 %copy-start.42 = (bf16[256]{0:T(256)(128)(2,1)S(1)}, bf16[256]{0:T(256)(128)(2,1)}, u32[]{:S(2)}) copy-start(bf16[256]{0:T(256)(128)(2,1)} %param.28) | copy-start | bytes 1540
  9.4 151.9 %copy-start.43 = (bf16[256]{0:T(256)(128)(2,1)S(1)}, bf16[256]{0:T(256)(128)(2,1)}, u32[]{:S(2)}) copy-start(bf16[256]{0:T(256)(128)(2,1)} %param.27) | copy-start | bytes 1540
  9.4 253.8 %copy-start = (bf16[1,128,2048]{2,1,0:T(8,128)(2,1)S(1)}, bf16[1,128,2048]{2,1,0:T(8,128)(2,1)}, u32[]{:S(2)}) copy-start(bf16[1,128,2048]{2,1,0:T(8,128)(2,1)} %param.19) | copy-start | bytes 1572868
  9.4 453.4 %all-gather.16.cloned.1.call-start = ((), (), s32[]{:S(2)}) async-start(), calls=%async_computation.4 | async-start | bytes 4718592 | tf_op jit(solution)/shard_map/all_gather | solution.py:112
  143.5 395.2 %all-gather.22.cloned.1.call-start = ((), (), s32[]{:S(2)}) async-start(), calls=%async_computation.7 | async-start | bytes 4718592 | tf_op jit(solution)/shard_map/all_gather | solution.py:111
  161.3 106.7 %copy-start.27 = (f32[8,1,256]{2,1,0:T(1,128)}, f32[8,1,256]{2,1,0:T(1,128)S(1)}, u32[]{:S(2)}) copy-start(f32[8,1,256]{2,1,0:T(1,128)S(1)} %convert_element_type.133) | copy-start | bytes 24580
  178.6 215.3 %copy-start.29 = (f32[8,1,256]{2,1,0:T(1,128)}, f32[8,1,256]{2,1,0:T(1,128)S(1)}, u32[]{:S(2)}) copy-start(f32[8,1,256]{2,1,0:T(1,128)S(1)} %convert_element_type.132) | copy-start | bytes 24580
  178.9 215.7 %copy-start.23 = (f32[128,64]{1,0:T(8,128)}, f32[128,64]{1,0:T(8,128)S(1)}, u32[]{:S(2)}) copy-start(f32[128,64]{1,0:T(8,128)S(1)} %get-tuple-element.713) | copy-start | bytes 98308
  178.9 215.7 %copy-start.25 = (f32[128,64]{1,0:T(8,128)}, f32[128,64]{1,0:T(8,128)S(1)}, u32[]{:S(2)}) copy-start(f32[128,64]{1,0:T(8,128)S(1)} %get-tuple-element.714) | copy-start | bytes 98308
  397.3 266.5 %all-gather.24.cloned.1.call-start = ((), (), s32[]{:S(2)}) async-start(), calls=%async_computation.8 | async-start | bytes 9437184 | tf_op jit(solution)/shard_map/all_gather | solution.py:92
  397.8 903.4 %all-gather.26.cloned.1.call-start = ((), (), s32[]{:S(2)}) async-start(), calls=%async_computation.9 | async-start | bytes 37748736 | tf_op jit(solution)/shard_map/all_gather | solution.py:143
  398.6 19.4 copy-start.45
  398.6 1541.9 %all-gather.28.cloned.1.call-start = ((), (), s32[]{:S(2)}) async-start(), calls=%async_computation.10 | async-start | bytes 37748736 | tf_op jit(solution)/shard_map/all_gather | solution.py:144
  399.4 2181.7 %all-gather.30.cloned.1.call-start = ((), (), s32[]{:S(2)}) async-start(), calls=%async_computation.11 | async-start | bytes 37748736 | tf_op jit(solution)/shard_map/all_gather | solution.py:151
  400.1 2634.7 %reduce-scatter.4.cloned.1.call-start = ((), (), s32[]{:S(2)}) async-start(), calls=%async_computation.12 | async-start | bytes 18874368 | tf_op jit(solution)/shard_map/reduce_scatter | solution.py:239
  564.3 104.3 %copy-start.12 = (bf16[4,128,4,128]{1,3,2,0:T(8,128)(2,1)}, bf16[4,128,4,128]{1,3,2,0:T(8,128)(2,1)S(1)}, u32[]{:S(2)}) copy-start(bf16[4,128,4,128]{1,3,2,0:T(8,128)(2,1)S(1)} %get-tuple-element.379) | copy-start | bytes 1572868
  668.8 1271.7 %copy-start.10 = (bf16[128,2048]{1,0:T(8,128)(2,1)}, bf16[128,2048]{1,0:T(8,128)(2,1)S(1)}, u32[]{:S(2)}) copy-start(bf16[128,2048]{1,0:T(8,128)(2,1)S(1)} %fusion.34) | copy-start | bytes 1572868
  2751.8 26.7 copy-start.7
  2751.8 2393.2 %reduce-scatter.8.cloned.1.call-start = ((), (), s32[]{:S(2)}) async-start(), calls=%async_computation.14 | async-start | bytes 150994944 | tf_op jit(solution)/shard_map/reduce_scatter | solution.py:282
  2891.8 4363.7 %reduce-scatter.6.cloned.1.call-start = ((), (), s32[]{:S(2)}) async-start(), calls=%async_computation.13 | async-start | bytes 150994944 | tf_op jit(solution)/shard_map/reduce_scatter | solution.py:282
  2894.5 144.4 %copy-start.24 = (f32[128,64]{1,0:T(8,128)S(1)}, f32[128,64]{1,0:T(8,128)}, u32[]{:S(2)}) copy-start(f32[128,64]{1,0:T(8,128)} %copy-done.23) | copy-start | bytes 98308
  2894.5 144.4 %copy-start.26 = (f32[128,64]{1,0:T(8,128)S(1)}, f32[128,64]{1,0:T(8,128)}, u32[]{:S(2)}) copy-start(f32[128,64]{1,0:T(8,128)} %copy-done.25) | copy-start | bytes 98308
  3053.7 19.5 copy-start.3
  3053.8 19.5 copy-start.28
  3053.8 19.5 copy-start.35
  3127.4 26.8 slice-start
  3127.4 26.8 slice-start.1
  3193.5 4624.4 %all-reduce.7.cloned.1.call-start = ((), (), s32[]{:S(2)}) async-start(), calls=%async_computation.15 | async-start | bytes 67108864 | tf_op jit(solution)/shard_map/psum | solution.py:291
  7255.5 42.3 copy-start.9
  (37 other events, 195.7 us)
Sparse Core Ops, SparseCore 0:
  10.1 127.6 all-gather.13
  139.9 123.2 all-gather.19
  265.4 123.1 all-gather.17
  391.1 71.7 all-gather.15
  465.3 73.2 all-gather.21
  540.6 123.1 all-gather.23
  665.3 635.8 all-gather.25
  1302.8 637.6 all-gather.27
  1942.0 639.0 all-gather.29
  2751.9 282.7 reduce-scatter.3
  3039.0 2105.9 reduce-scatter.7
  5149.1 2106.2 reduce-scatter.5
  7258.3 559.5 all-reduce.6
where the time goes:
time: 7870 us; the launch traced here: 7860 us
  waiting for transfers between devices  7110 us (90%)
  matrix products  300 us (4%)
  local copies, waits for them, and re-layouts  187 us (2%)
  other arithmetic  119 us (2%)
  blocking collectives  111 us (1%)
    reduce_scatter x2, waiting for transfers between devices, spread(): lax.psum_scatter(term_fn(jnp.int32(0), owned_rows * lax.axis_size('grp'))...  4060 us
    all_gather x1, waiting for transfers between devices, on_device(): lax.all_gather(gate_weight, 'grp', axis=0, tiled=True)  632 us
    all_gather x1, waiting for transfers between devices, on_device(): lax.all_gather(up_weight, 'grp', axis=0, tiled=True)  621 us
    all_gather x1, waiting for transfers between devices, on_device(): lax.all_gather(down_weight, 'grp', axis=1, tiled=True)  621 us
    psum x1, waiting for transfers between devices, on_device(): attn_sum, mlp_sum = lax.psum((attn_part, mlp_part), 'rep')  503 us
  transfers between devices with their start and end apart: 13, of which 13 were waited for; matrix products, arithmetic and copies ran while one was open for 5% of the time, Pallas kernels for 0%

commit v1 on v0

--- a/solution.py
+++ b/solution.py
@@ -5,15 +5,331 @@
 
 HEADS = 16
 HEAD = 128
-
-
 EPS = 1e-06
 THETA = 500000.0
 GROUPED = 4
-
-
-def rms_scale(values, gains):
+BF = jnp.bfloat16
+F32 = jnp.float32
+
+
+def dot(left, right, dims=((1,), (0,)), kind=F32):
+    return lax.dot_general(left, right, (dims, ((), ())), preferred_element_type=kind)
+
+
+def dot_right_t(left, right):
+    return dot(left, right, ((1,), (1,)))
+
+
+def dot_left_t(left, right):
+    return dot(left, right, ((0,), (0,)))
+
+
+def shuffle(value, axis, step):
+    return lax.ppermute(value, axis, [(i, i ^ step) for i in range(lax.axis_size(axis))])
+
+
+def gather_pieces(value):
+    count = lax.axis_size("grp")
+    pieces = [None] * count
+    pieces[0] = value
+    for step in range(count - 2, 0, -2):
+        pieces[step] = shuffle(value, "grp", step)
+    for step in [0, *range(count - 2, 0, -2)]:
+        pieces[step + 1] = shuffle(pieces[step], "grp", 1)
+    return pieces
+
+
+def scatter_sum(pieces):
+    count = len(pieces)
+    order = [*range(count - 2, -1, -2)]
+    moved = {step: shuffle(pieces[step + 1].astype(BF), "grp", 1) for step in order}
+    total = None
+    for step in order:
+        paired = pieces[step].astype(F32) + moved[step].astype(F32)
+        if step:
+            paired = shuffle(paired.astype(BF), "grp", step).astype(F32)
+        total = paired if total is None else total + paired
+    return total
+
+
+def exchange(pieces):
+    return [pieces[0]] + [shuffle(pieces[k], "grp", k) for k in range(1, len(pieces))]
+
+
+def group_sum(value):
+    step = 1
+    while step < lax.axis_size("grp"):
+        value = value + shuffle(value, "grp", step)
+        step *= 2
+    return value
+
+
+def across_rep(value):
+    far = shuffle(value, "rep", 2)
+    return [value, shuffle(value, "rep", 1), far, shuffle(far, "rep", 1)]
+
+
+def rep_sum(parts):
+    near = [
+        (parts[j].astype(F32) + shuffle(parts[j ^ 1].astype(BF), "rep", 1).astype(F32)) for j in (0, 2)
+    ]
+    return (near[0] + shuffle(near[1].astype(BF), "rep", 2).astype(F32)).astype(BF)
+
+
+def put(buffer, part, starts):
+    return lax.dynamic_update_slice(buffer, part, starts)
+
+
+def rms(values, gains):
     return values * lax.rsqrt(jnp.mean(values * values, axis=-1, keepdims=True) + EPS) * gains
+
+
+def angles_of(count):
+    freqs = THETA ** (-2.0 * jnp.arange(HEAD // 2, dtype=F32) / HEAD)
+    angles = jnp.arange(count, dtype=jnp.int32).astype(F32)[:, None] * freqs[None, :]
+    return jnp.cos(angles), jnp.sin(angles)
+
+
+def turn(values, cosine, sine):
+    half = HEAD // 2
+    out = []
+    for start in range(0, values.shape[1], HEAD):
+        first, second = values[:, start : start + half], values[:, start + half : start + HEAD]
+        out += [first * cosine - second * sine, second * cosine + first * sine]
+    return jnp.concatenate(out, axis=1)
+
+
+def swiglu(gates, uppers):
+    return jax.nn.silu(gates) * uppers
+
+
+def attend(queries, keys, values):
+    length = queries.shape[0]
+    split = lambda a: a.reshape(length, -1, HEAD)
+    scores = jnp.einsum("qhd,khd->hqk", split(queries), split(keys), preferred_element_type=F32)
+    scores = scores * HEAD ** (-0.5)
+    places = jnp.arange(length, dtype=jnp.int32)
+    scores = jnp.where((places[None, :] <= places[:, None])[None], scores, -1e30)
+    top = jnp.max(scores, axis=-1, keepdims=True)
+    weights = jnp.exp(scores - top)
+    totals = jnp.sum(weights, axis=-1, keepdims=True)
+    probs = (weights / totals).astype(BF)
+    mixed = jnp.einsum("hqk,khd->qhd", probs, split(values), preferred_element_type=F32)
+    return mixed.reshape(length, -1).astype(BF), top + jnp.log(totals)
+
+
+def attend_back(queries, keys, values, lse, grads):
+    length = queries.shape[0]
+    split = lambda a: a.reshape(length, -1, HEAD)
+    scale = HEAD ** (-0.5)
+    q, k, v, do = split(queries), split(keys), split(values), split(grads)
+    scores = jnp.einsum("qhd,khd->hqk", q, k, preferred_element_type=F32) * scale
+    places = jnp.arange(length, dtype=jnp.int32)
+    scores = jnp.where((places[None, :] <= places[:, None])[None], scores, -1e30)
+    probs = jnp.exp(scores - lse)
+    d_probs = jnp.einsum("qhd,khd->hqk", do, v, preferred_element_type=F32)
+    delta = jnp.sum(probs * d_probs, axis=-1, keepdims=True)
+    ds = (probs * (d_probs - delta)).astype(BF)
+    dv = jnp.einsum("hqk,qhd->khd", probs.astype(BF), do, preferred_element_type=F32)
+    dq = jnp.einsum("hqk,khd->qhd", ds, k, preferred_element_type=F32) * scale
+    dk = jnp.einsum("hqk,qhd->khd", ds, q, preferred_element_type=F32) * scale
+    return dq.reshape(length, -1), dk.reshape(length, -1), dv.reshape(length, -1)
+
+
+def by_heads(
+    tokens, q_weight, k_weight, v_weight, o_weight, gate_weight, up_weight, down_weight,
+    q_gain, k_gain, attn_gain, mlp_gain, cotangent,
+):
+    x = tokens[0]
+    count, width = x.shape
+    groups = lax.axis_size("grp")
+    reps = 4
+    me, rep = lax.axis_index("grp"), lax.axis_index("rep")
+    length = count * groups
+    own = width // groups
+    hidden = gate_weight.shape[1]
+    block = hidden // groups
+    part = block // reps
+    sub = own // reps
+    zero = jnp.int32(0)
+    at = [me ^ k for k in range(groups)]
+    of = [rep ^ j for j in range(reps)]
+
+    sends = [
+        jnp.concatenate(
+            [lax.dynamic_slice(w, (rep * sub, at[k] * own), (sub, own)) for w in (q_weight, k_weight, v_weight)],
+            axis=1,
+        )
+        for k in range(groups)
+    ]
+    landed = jnp.zeros((groups, sub, 3 * own), BF)
+    for k, piece in enumerate(exchange(sends)):
+        landed = put(landed, piece[None], (at[k], zero, zero))
+    w_qkv = jnp.zeros((groups, reps, sub, 3 * own), BF)
+    for j, piece in enumerate(across_rep(landed)):
+        w_qkv = put(w_qkv, piece[:, None], (zero, of[j], zero, zero))
+    w_qkv = w_qkv.reshape(width, 3 * own)
+
+    x_all = jnp.zeros((groups, count, width), BF)
+    for k, piece in enumerate(gather_pieces(x)):
+        x_all = put(x_all, piece[None], (at[k], zero, zero))
+    x_all = x_all.reshape(length, width)
+
+    stripe = width // reps
+    gains = jnp.concatenate([attn_gain, mlp_gain])
+    gains = jnp.pad(gains[None], ((0, 15), (0, stripe - 2 * own)))
+    o_part = jnp.concatenate([lax.dynamic_slice(o_weight, (zero, rep * stripe), (own, stripe)), gains])
+    o_mine = jnp.zeros((groups, own, stripe), BF)
+    gain_all = jnp.zeros((groups, 2, own), BF)
+    for k, piece in enumerate(gather_pieces(o_part)):
+        o_mine = put(o_mine, piece[None, :own], (at[k], zero, zero))
+        gain_all = put(gain_all, piece[own, : 2 * own].reshape(1, 2, own), (at[k], zero, zero))
+    w_o = jnp.zeros((width, width), BF)
+    for j, piece in enumerate(across_rep(o_mine.reshape(width, stripe))):
+        w_o = put(w_o, piece, (zero, of[j] * stripe))
+    ga = gain_all[:, 0].reshape(width).astype(F32)
+    gm = gain_all[:, 1].reshape(width).astype(F32)
+
+    sends = []
+    for k in range(groups):
+        start = at[k] * block + rep * part
+        sends.append(
+            jnp.concatenate(
+                [
+                    lax.dynamic_slice(gate_weight, (zero, start), (own, part)),
+                    lax.dynamic_slice(up_weight, (zero, start), (own, part)),
+                    lax.dynamic_slice(down_weight, (start, zero), (part, own)).T,
+                ],
+                axis=1,
+            )
+        )
+    landed_gu = jnp.zeros((groups, own, 2 * part), BF)
+    landed_d = jnp.zeros((groups, own, part), BF)
+    for k, piece in enumerate(exchange(sends)):
+        landed_gu = put(landed_gu, piece[None, :, : 2 * part], (at[k], zero, zero))
+        landed_d = put(landed_d, piece[None, :, 2 * part :], (at[k], zero, zero))
+    gu_parts = across_rep(landed_gu.reshape(width, 2 * part))
+    d_parts = across_rep(landed_d.reshape(width, part))
+    w_gu = jnp.concatenate([p[:, :part] for p in gu_parts] + [p[:, part:] for p in gu_parts], axis=1)
+    w_d = jnp.concatenate(d_parts, axis=1)
+
+    gq, gk = q_gain.astype(F32), k_gain.astype(F32)
+    cosine, sine = angles_of(length)
+    qkv = dot(x_all, w_qkv)
+    q_proj, k_proj = qkv[:, :own], qkv[:, own : 2 * own]
+    values = qkv[:, 2 * own :].astype(BF)
+    squares = jnp.stack([jnp.sum(q_proj * q_proj, axis=1), jnp.sum(k_proj * k_proj, axis=1)])
+    squares = group_sum(squares)
+    q_inv = lax.rsqrt(squares[0] / width + EPS)[:, None]
+    k_inv = lax.rsqrt(squares[1] / width + EPS)[:, None]
+    queries = turn(q_proj * q_inv * gq, cosine, sine).astype(BF)
+    keys = turn(k_proj * k_inv * gk, cosine, sine).astype(BF)
+    attn, lse = attend(queries, keys, values)
+    attn_tok = lax.all_to_all(attn, "grp", 0, 1, tiled=True)
+    a_proj = dot(attn_tok, w_o)
+    middle = x.astype(F32) + rms(a_proj, ga)
+    middle_bf = middle.astype(BF)
+
+    h_all = jnp.concatenate(gather_pieces(middle_bf))
+    gu = dot(h_all, w_gu)
+    gates, uppers = gu[:, :block], gu[:, block:]
+    mixed = swiglu(gates, uppers).astype(BF)
+    y_part = dot_right_t(mixed, w_d).reshape(groups, count, width)
+    y_proj = scatter_sum([y_part[k] for k in range(groups)])
+    outputs = (middle + rms(y_proj, gm)).astype(BF)
+
+    grad_out = cotangent[0].astype(F32)
+    _, pull = jax.vjp(rms, y_proj, gm)
+    dy, d_mlp_gain = pull(grad_out)
+    dy_all = jnp.concatenate(gather_pieces(dy.astype(BF)))
+    d_mixed = dot(dy_all, w_d)
+    _, pull = jax.vjp(swiglu, gates, uppers)
+    d_gu = jnp.concatenate([v.astype(BF) for v in pull(d_mixed)], axis=1)
+    m_part = dot_right_t(d_gu, w_gu).reshape(groups, count, width)
+    d_middle = grad_out + scatter_sum([m_part[k] for k in range(groups)])
+
+    g_gu = dot_left_t(h_all, d_gu).astype(BF)
+    g_d = dot_left_t(dy_all, mixed).astype(BF)
+    sums = rep_sum(
+        [
+            jnp.concatenate(
+                [
+                    g_gu[:, j * part : (j + 1) * part],
+                    g_gu[:, block + j * part : block + (j + 1) * part],
+                    g_d[:, j * part : (j + 1) * part],
+                ],
+                axis=1,
+            )
+            for j in range(reps)
+        ]
+    ).reshape(groups, own, 3 * part)
+    sends = [lax.dynamic_slice(sums, (at[k], zero, zero), (1, own, 3 * part))[0] for k in range(groups)]
+    g_mlp = jnp.zeros((groups, own, 3 * part), BF)
+    for k, piece in enumerate(exchange(sends)):
+        g_mlp = put(g_mlp, piece[None], (at[k], zero, zero))
+    g_mlp = jnp.stack(across_rep(lax.optimization_barrier(g_mlp)))
+    g_mlp = jnp.concatenate([lax.dynamic_slice(g_mlp, (of[j], zero, zero, zero), (1, groups, own, 3 * part)) for j in range(reps)])
+    gate_grad = jnp.transpose(g_mlp[..., :part], (2, 1, 0, 3)).reshape(own, hidden).astype(F32)
+    up_grad = jnp.transpose(g_mlp[..., part : 2 * part], (2, 1, 0, 3)).reshape(own, hidden).astype(F32)
+    down_grad = jnp.transpose(g_mlp[..., 2 * part :], (1, 0, 3, 2)).reshape(hidden, own).astype(F32)
+
+    _, pull = jax.vjp(rms, a_proj, ga)
+    da, d_attn_gain = pull(d_middle)
+    da_bf = da.astype(BF)
+    d_attn = lax.all_to_all(dot_right_t(da_bf, w_o).astype(BF), "grp", 1, 0, tiled=True)
+    dq, dk, dv = attend_back(queries, keys, values, lse, d_attn)
+    dq, dk = turn(dq, cosine, -sine), turn(dk, cosine, -sine)
+    q_unit, k_unit = q_proj * q_inv, k_proj * k_inv
+    d_q_gain, d_k_gain = jnp.sum(dq * q_unit, axis=0), jnp.sum(dk * k_unit, axis=0)
+    dq, dk = dq * gq, dk * gk
+    along = jnp.concatenate(
+        [jnp.sum(dq * q_unit, axis=1), jnp.sum(dk * k_unit, axis=1), d_attn_gain, d_mlp_gain]
+    )
+    along = group_sum(along.reshape(-1, 128)).reshape(-1)
+    q_mean, k_mean = along[:length, None] / width, along[length : 2 * length, None] / width
+    d_qkv = jnp.concatenate(
+        [
+            (q_inv * (dq - q_unit * q_mean)).astype(BF),
+            (k_inv * (dk - k_unit * k_mean)).astype(BF),
+            dv.astype(BF),
+        ],
+        axis=1,
+    )
+    x_part = dot_right_t(d_qkv, w_qkv)
+    d_x = d_middle + scatter_sum(
+        [lax.dynamic_slice(x_part, (at[k] * count, zero), (count, width)) for k in range(groups)]
+    )
+
+    da_all = jnp.zeros((groups, count, width), BF)
+    for k, piece in enumerate(gather_pieces(da_bf)):
+        da_all = put(da_all, piece[None], (at[k], zero, zero))
+    g_o = dot_left_t(attn, da_all.reshape(length, width)).astype(BF)
+    o_sum = rep_sum([lax.dynamic_slice(g_o, (zero, of[j] * stripe), (own, stripe)) for j in range(reps)])
+    o_grad = jnp.zeros((own, width), F32)
+    for j, piece in enumerate(across_rep(lax.optimization_barrier(o_sum))):
+        o_grad = put(o_grad, piece.astype(F32), (zero, of[j] * stripe))
+    g_qkv = dot_left_t(x_all, d_qkv).astype(BF).reshape(groups, reps, sub, 3 * own)
+    sums = rep_sum(
+        [lax.dynamic_slice(g_qkv, (zero, of[j], zero, zero), (groups, 1, sub, 3 * own))[:, 0] for j in range(reps)]
+    )
+    sends = [lax.dynamic_slice(sums, (at[k], zero, zero), (1, sub, 3 * own))[0] for k in range(groups)]
+    landed = jnp.zeros((groups, sub, 3 * own), BF)
+    for k, piece in enumerate(exchange(sends)):
+        landed = put(landed, piece[None], (at[k], zero, zero))
+    g_qkv = jnp.zeros((reps, groups, sub, 3 * own), BF)
+    for j, piece in enumerate(across_rep(lax.optimization_barrier(landed))):
+        g_qkv = put(g_qkv, piece[None], (of[j], zero, zero, zero))
+    q_grad, k_grad, v_grad = (
+        jnp.transpose(g_qkv[..., i * own : (i + 1) * own], (0, 2, 1, 3)).reshape(own, width).astype(F32)
+        for i in range(3)
+    )
+
+    post = lax.dynamic_slice(along[2 * length :].reshape(2, width), (zero, me * own), (2, own))
+    gain_sums = lax.psum(jnp.concatenate([jnp.stack([d_q_gain, d_k_gain]), post]), "rep")
+    return (
+        outputs[None], d_x.astype(BF)[None], q_grad, k_grad, v_grad, o_grad, gate_grad, up_grad, down_grad,
+        gain_sums[0], gain_sums[1], gain_sums[2], gain_sums[3],
+    )
 
 
 def rotary(values, places):
@@ -31,26 +347,6 @@
     return turned.reshape(count, HEADS * HEAD)
 
 
-def swiglu(gates, uppers):
-    return jax.nn.silu(gates) * uppers
-
-
-def dot_plain(left, right):
-    return jnp.dot(left, right, preferred_element_type=jnp.float32)
-
-
-def dot_right_t(left, right):
-    return lax.dot_general(
-        left, right, (((1,), (1,)), ((), ())), preferred_element_type=jnp.float32
-    )
-
-
-def dot_left_t(left, right):
-    return lax.dot_general(
-        left, right, (((0,), (0,)), ((), ())), preferred_element_type=jnp.float32
-    )
-
-
 def head_slice(matrix, index):
     piece = lax.dynamic_slice_in_dim(matrix, index * GROUPED * HEAD, GROUPED * HEAD, 1)
     return piece.reshape(matrix.shape[0], GROUPED, HEAD)
@@ -60,7 +356,7 @@
     return jnp.moveaxis(stacked, 0, 1).reshape(count, HEADS * HEAD)
 
 
-def on_device(
+def by_tokens(
     tokens,
     q_weight,
     k_weight,
@@ -78,7 +374,6 @@
     inputs = tokens[0]
     rows = inputs.shape[0]
     width = inputs.shape[1]
-    hidden_width = gate_weight.shape[1]
     groups = lax.axis_size("grp")
     length = rows * groups
     query_places = lax.axis_index("grp") * rows + jnp.arange(rows, dtype=jnp.int32)
@@ -97,12 +392,12 @@
     gq_full = gq_bf.astype(jnp.float32)
     gk_full = gk_bf.astype(jnp.float32)
     ga_full = ga_bf.astype(jnp.float32)
-    q_proj = dot_plain(inputs, wq_fwd)
-    k_proj = dot_plain(inputs, wk_fwd)
-    v_proj = dot_plain(inputs, wv_fwd)
+    q_proj = dot(inputs, wq_fwd)
+    k_proj = dot(inputs, wk_fwd)
+    v_proj = dot(inputs, wv_fwd)
 
     def turn_query(values, gains):
-        return rotary(rms_scale(values, gains), places)
+        return rotary(rms(values, gains), places)
 
     queries = turn_query(q_proj, gq_full).astype(jnp.bfloat16)
     keys_own = turn_query(k_proj, gk_full).astype(jnp.bfloat16)
@@ -136,8 +431,8 @@
     mixed_all, log_totals = lax.map(forward_group, group_ids)
     log_totals = log_totals.reshape(HEADS, rows)
     attn_bf = heads_back(mixed_all, rows).astype(jnp.bfloat16)
-    a_proj = dot_plain(attn_bf, wo_gathered)
-    middle = inputs.astype(jnp.float32) + rms_scale(a_proj, ga_full)
+    a_proj = dot(attn_bf, wo_gathered)
+    middle = inputs.astype(jnp.float32) + rms(a_proj, ga_full)
     middle_bf = middle.astype(jnp.bfloat16)
     wg_fwd, wu_fwd, gm_bf = (
         lax.all_gather(gate_weight, "grp", axis=0, tiled=True),
@@ -145,13 +440,13 @@
         lax.all_gather(mlp_gain, "grp", axis=0, tiled=True),
     )
     gm_full = gm_bf.astype(jnp.float32)
-    gates = dot_plain(middle_bf, wg_fwd)
-    uppers = dot_plain(middle_bf, wu_fwd)
+    gates = dot(middle_bf, wg_fwd)
+    uppers = dot(middle_bf, wu_fwd)
     hidden = swiglu(gates, uppers).astype(jnp.bfloat16)
-    y_proj = dot_plain(hidden, lax.all_gather(down_weight, "grp", axis=1, tiled=True))
-    outputs = (middle + rms_scale(y_proj, gm_full)).astype(jnp.bfloat16)
+    y_proj = dot(hidden, lax.all_gather(down_weight, "grp", axis=1, tiled=True))
+    outputs = (middle + rms(y_proj, gm_full)).astype(jnp.bfloat16)
     grad_out = cotangent[0].astype(jnp.float32)
-    unused_y, pull_mlp = jax.vjp(rms_scale, y_proj, gm_full)
+    unused_y, pull_mlp = jax.vjp(rms, y_proj, gm_full)
     dy_proj, d_mlp_gain = pull_mlp(grad_out)
     dy_bf = dy_proj.astype(jnp.bfloat16)
     down_full = lax.all_gather(down_weight, "grp", axis=1, tiled=True)
@@ -164,7 +459,7 @@
         dg_bf, lax.all_gather(gate_weight, "grp", axis=0, tiled=True)
     ) + dot_right_t(du_bf, lax.all_gather(up_weight, "grp", axis=0, tiled=True))
     d_middle = grad_out + block
-    unused_a, pull_attn = jax.vjp(rms_scale, a_proj, ga_full)
+    unused_a, pull_attn = jax.vjp(rms, a_proj, ga_full)
     da_proj, d_attn_gain = pull_attn(d_middle)
     da_bf = da_proj.astype(jnp.bfloat16)
     wq_full, wk_full, wv_full, wo_full = (
@@ -262,33 +557,16 @@
         + dot_right_t(dv_bf, wv_full)
     )
     owned_rows = width // groups
-
-    def attn_terms(start, count):
-        return jnp.concatenate(
-            [
-                dot_left_t(inputs, dq_bf),
-                dot_left_t(inputs, dk_bf),
-                dot_left_t(inputs, dv_bf),
-                dot_left_t(attn_bf, da_bf),
-                dot_left_t(dy_bf, hidden),
-            ],
-            axis=1,
-        )
-
-    def mlp_terms(start, count):
-        return jnp.concatenate([dot_left_t(middle_bf, dg_bf), dot_left_t(middle_bf, du_bf)], axis=1)
-
-    def spread(term_fn):
-        return lax.psum_scatter(
-            term_fn(jnp.int32(0), owned_rows * lax.axis_size("grp")),
-            "grp",
-            scatter_dimension=0,
-            tiled=True,
-        )
-
-    attn_part = spread(attn_terms)
-    mlp_part = spread(mlp_terms)
-    attn_sum, mlp_sum = lax.psum((attn_part, mlp_part), "rep")
+    pairs = (
+        (inputs, dq_bf), (inputs, dk_bf), (inputs, dv_bf), (attn_bf, da_bf),
+        (middle_bf, dg_bf), (middle_bf, du_bf), (dy_bf, hidden),
+    )
+    weight_sums = []
+    for left, right in pairs:
+        if weight_sums:
+            left, right, weight_sums[-1] = lax.optimization_barrier((left, right, weight_sums[-1]))
+        share = lax.psum_scatter(dot_left_t(left, right), "grp", scatter_dimension=0, tiled=True)
+        weight_sums.append(lax.psum(share, "rep"))
     gain_stack = jnp.stack([d_q_gain, d_k_gain, d_attn_gain, d_mlp_gain])
     gain_total = lax.psum(gain_stack, ("rep", "grp"))
     gain_mine = lax.dynamic_slice_in_dim(
@@ -297,13 +575,8 @@
     return (
         outputs[None],
         d_inputs.astype(jnp.bfloat16)[None],
-        attn_sum[:, :width],
-        attn_sum[:, width : 2 * width],
-        attn_sum[:, 2 * width : 3 * width],
-        attn_sum[:, 3 * width : 4 * width],
-        mlp_sum[:, :hidden_width],
-        mlp_sum[:, hidden_width:],
-        attn_sum[:, 4 * width :].T,
+        *weight_sums[:6],
+        weight_sums[6].T,
         gain_mine[0],
         gain_mine[1],
         gain_mine[2],
@@ -312,38 +585,14 @@
 
 
 def solution(mesh):
+    rows = P("grp", None)
+    seq = P("rep", "grp", None)
+    gain = P("grp")
+    whole_heads = HEADS % mesh.shape["grp"] == 0 and mesh.shape["rep"] == 4
     return jax.shard_map(
-        on_device,
+        by_heads if whole_heads else by_tokens,
         mesh=mesh,
-        in_specs=(
-            P("rep", "grp", None),
-            P("grp", None),
-            P("grp", None),
-            P("grp", None),
-            P("grp", None),
-            P("grp", None),
-            P("grp", None),
-            P(None, "grp"),
-            P("grp"),
-            P("grp"),
-            P("grp"),
-            P("grp"),
-            P("rep", "grp", None),
-        ),
-        out_specs=(
-            P("rep", "grp", None),
-            P("rep", "grp", None),
-            P("grp", None),
-            P("grp", None),
-            P("grp", None),
-            P("grp", None),
-            P("grp", None),
-            P("grp", None),
-            P(None, "grp"),
-            P("grp"),
-            P("grp"),
-            P("grp"),
-            P("grp"),
-        ),
+        in_specs=(seq, *[rows] * 6, P(None, "grp"), *[gain] * 4, seq),
+        out_specs=(seq, seq, *[rows] * 6, P(None, "grp"), *[gain] * 4),
         check_vma=False,
     )

time: 7870 us -> 1240 us (0.16)
  waiting for transfers between devices: 7110 us -> 590 us
  starting transfers between devices: 0.92 us -> 204 us
  matrix products: 300 us -> 105 us
    reduce_scatter x3 -> x0, waiting for transfers between devices: 4200 us -> none  [the longest x2 4060 us: spread(): lax.psum_scatter(term_fn(jnp.int32(0), owned_rows * lax.axis_size('grp'))...]
    all_gather x9 -> x0, waiting for transfers between devices: 2400 us -> none  [the longest x1 632 us: on_device(): lax.all_gather(gate_weight, 'grp', axis=0, tiled=True)]
    ppermute x0 -> x120, waiting for transfers between devices: none -> 587 us  [shuffle(): lax.ppermute(value, axis, [(i, i ^ step) for i in range(lax.axis_size(axi...]
    psum x1 -> x0, waiting for transfers between devices: 503 us -> none  [on_device(): attn_sum, mlp_sum = lax.psum((attn_part, mlp_part), 'rep')]
    ppermute x0 -> x120, starting transfers between devices: none -> 197 us  [shuffle(): lax.ppermute(value, axis, [(i, i ^ step) for i in range(lax.axis_size(axi...]
    dot_general x53 -> x18, matrix products: 300 us -> 105 us  [the longest x12 92 us: dot(): lax.dot_general(left, right, (dims, ((), ())), preferred_element_type=kind)]
    concatenate x3 -> x21, other arithmetic: 101 us -> 14 us  [the longest x1 4.92 us: by_heads(): jnp.concatenate([lax.dynamic_slice(g_mlp, (of[j], zero, zero, zero), (1,...]
  transfers between devices with their start and end apart: 13 -> 122, of which waited for: 13 -> 61; matrix products, arithmetic and copies ran while one was open for 5% -> 19% of each run, Pallas kernels for 0% -> 0%
where the time goes in v1:
time: 1240 us; the launch traced here: 1230 us
  waiting for transfers between devices  590 us (48%)
  starting transfers between devices  204 us (16%)
  local copies, waits for them, and re-layouts  196 us (16%)
  matrix products  105 us (8%)
  other arithmetic  64.1 us (5%)
  blocking collectives  63.7 us (5%)
    ppermute x120, waiting for transfers between devices, shuffle(): lax.ppermute(value, axis, [(i, i ^ step) for i in range(lax.axis_size(axi...  587 us
    ppermute x120, starting transfers between devices, shuffle(): lax.ppermute(value, axis, [(i, i ^ step) for i in range(lax.axis_size(axi...  197 us
    dot_general x12, matrix products, dot(): lax.dot_general(left, right, (dims, ((), ())), preferred_element_type=kind)  92 us
    psum x1, blocking collectives, by_heads(): lax.psum(jnp.concatenate([jnp.stack([d_q_gain, d_k_gain]), post]), 'rep')  63.7 us
    dynamic_update_slice x80, local copies, waits for them, and re-layouts, put(): return lax.dynamic_update_slice(buffer, part, starts)  61.9 us
    unnamed x216, local copies, waits for them, and re-layouts  55.8 us
  transfers between devices with their start and end apart: 122, of which 61 were waited for; matrix products, arithmetic and copies ran while one was open for 19% of the time, Pallas kernels for 0%

profile of v1, /device:TPU:0, one launch (start us, length us, event | category | flops | bytes accessed | tf_op | source)
XLA Modules:
  0.0 1225.5 jit_solution(16679962195540700012)
XLA Ops:
  128.8 13.4 %collective-permute-done.40 = bf16[256,768]{1,0:T(8,128)(2,1)S(1)} collective-permute-done((bf16[256,768]{1,0:T(8,128)(2,1)S(1)}, bf16[256,768]{1,0:T(8,128)(2,1)S(1)}, u32[]{:S(2)}, u32[]{:S(2)}) %collective-permute-start.40) | collective-permute-done | bytes 393248 | tf_op jit(solution)/shard_map/ppermute | solution.py:28
  144.4 20.2 %collective-permute-done.41 = bf16[256,768]{1,0:T(8,128)(2,1)S(1)} collective-permute-done((bf16[256,768]{1,0:T(8,128)(2,1)S(1)}, bf16[256,768]{1,0:T(8,128)(2,1)S(1)}, u32[]{:S(2)}, u32[]{:S(2)}) %collective-permute-start.41) | collective-permute-done | bytes 393248 | tf_op jit(solution)/shard_map/ppermute | solution.py:28
  222.7 10.6 collective-permute-done.2
  267.3 16.2 %collective-permute-start.18 = (f32[2,1024]{1,0:T(2,128)S(1)}, f32[2,1024]{1,0:T(2,128)S(1)}, u32[]{:S(2)}, u32[]{:S(2)}) collective-permute-start(f32[2,1024]{1,0:T(2,128)S(1)} %fusion.136), channel_id=1, source_target_pairs={{0,2},{1,3},{2,0},{3,1},{4,6},{5,7},{6,4},{7,5},{8,10},{9,11},{10,... | collective-permute-start | bytes 24584 | tf_op jit(solution)/shard_map/ppermute | solution.py:28
  305.1 30.6 %collective-permute-done.28 = bf16[2048,512]{1,0:T(8,128)(2,1)} collective-permute-done((bf16[2048,512]{1,0:T(8,128)(2,1)}, bf16[2048,512]{1,0:T(8,128)(2,1)}, u32[]{:S(2)}, u32[]{:S(2)}) %collective-permute-start.28) | collective-permute-done | bytes 2097184 | tf_op jit(solution)/shard_map/ppermute | solution.py:28
  356.4 15.4 %collective-permute-start.31 = (bf16[128,2048]{1,0:T(8,128)(2,1)S(1)}, bf16[128,2048]{1,0:T(8,128)(2,1)S(1)}, u32[]{:S(2)}, u32[]{:S(2)}) collective-permute-start(bf16[128,2048]{1,0:T(8,128)(2,1)S(1)} %get-tuple-element.57), channel_id=1, source_target_pairs={{0,2},{1,3},{2,0},{3,1},{4,6},{5,7},{6,4},{7,5},{8,10},{9,11},{10,... | collective-permute-start | bytes 1572872 | tf_op jit(solution)/shard_map/ppermute | solution.py:28
  378.7 13.6 %collective-permute-done.31 = bf16[128,2048]{1,0:T(8,128)(2,1)S(1)} collective-permute-done((bf16[128,2048]{1,0:T(8,128)(2,1)S(1)}, bf16[128,2048]{1,0:T(8,128)(2,1)S(1)}, u32[]{:S(2)}, u32[]{:S(2)}) %collective-permute-start.31) | collective-permute-done | bytes 524320 | tf_op jit(solution)/shard_map/ppermute | solution.py:28
  393.7 18.7 %collective-permute-done.33 = bf16[128,2048]{1,0:T(8,128)(2,1)S(1)} collective-permute-done((bf16[128,2048]{1,0:T(8,128)(2,1)S(1)}, bf16[128,2048]{1,0:T(8,128)(2,1)S(1)}, u32[]{:S(2)}, u32[]{:S(2)}) %collective-permute-start.33) | collective-permute-done | bytes 524320 | tf_op jit(solution)/shard_map/ppermute | solution.py:28
  414.7 12.6 %collective-permute-done.34 = bf16[128,2048]{1,0:T(8,128)(2,1)S(1)} collective-permute-done((bf16[128,2048]{1,0:T(8,128)(2,1)S(1)}, bf16[128,2048]{1,0:T(8,128)(2,1)S(1)}, u32[]{:S(2)}, u32[]{:S(2)}) %collective-permute-start.34) | collective-permute-done | bytes 524320 | tf_op jit(solution)/shard_map/ppermute | solution.py:28
  460.2 10.8 collective-permute-done.50
  471.0 11.2 collective-permute-done.52
  482.2 11.2 collective-permute-done.54
  510.7 25.2 %collective-permute-done.53 = bf16[128,2048]{1,0:T(8,128)(2,1)S(1)} collective-permute-done((bf16[128,2048]{1,0:T(8,128)(2,1)S(1)}, bf16[128,2048]{1,0:T(8,128)(2,1)S(1)}, u32[]{:S(2)}, u32[]{:S(2)}) %collective-permute-start.53) | collective-permute-done | bytes 524320 | tf_op jit(solution)/shard_map/ppermute | solution.py:28
  543.5 18.4 %collective-permute-done.58 = bf16[128,2048]{1,0:T(8,128)(2,1)} collective-permute-done((bf16[128,2048]{1,0:T(8,128)(2,1)}, bf16[128,2048]{1,0:T(8,128)(2,1)}, u32[]{:S(2)}, u32[]{:S(2)}) %collective-permute-start.58) | collective-permute-done | bytes 524320 | tf_op jit(solution)/shard_map/ppermute | solution.py:28
  563.3 13.2 %collective-permute-done.60 = bf16[128,2048]{1,0:T(8,128)(2,1)} collective-permute-done((bf16[128,2048]{1,0:T(8,128)(2,1)}, bf16[128,2048]{1,0:T(8,128)(2,1)}, u32[]{:S(2)}, u32[]{:S(2)}) %collective-permute-start.60) | collective-permute-done | bytes 524320 | tf_op jit(solution)/shard_map/ppermute | solution.py:28
  600.9 11.2 fusion.4
  612.1 14.2 %fusion.152 = (bf16[1024,2048]{1,0:T(8,128)(2,1)S(1)}, f32[1024,2048]{1,0:T(8,128)}) fusion(bf16[2048,2048]{1,0:T(8,128)(2,1)} %copy-done.44, bf16[1024,1024]{1,0:T(8,128)(2,1)} %get-tuple-element.68, bf16[1024,1024]{1,0:T(8,128)(2,1)S(1)} %get-tuple-element.67), kind=kOutput, calls=%fused_computation.424 | convolution fusion | flops 8600420352 | bytes 25165824 | tf_op jit(solution)/shard_map/dot_general | solution.py:16
  626.2 11.6 convolution_convert_fusion
  653.0 11.2 collective-permute-done.66
  664.2 11.2 collective-permute-done.68
  694.8 25.1 %collective-permute-done.67 = bf16[128,2048]{1,0:T(8,128)(2,1)S(1)} collective-permute-done((bf16[128,2048]{1,0:T(8,128)(2,1)S(1)}, bf16[128,2048]{1,0:T(8,128)(2,1)S(1)}, u32[]{:S(2)}, u32[]{:S(2)}) %collective-permute-start.67) | collective-permute-done | bytes 524320 | tf_op jit(solution)/shard_map/ppermute | solution.py:28
  772.9 11.3 collective-permute-done.72
  814.6 63.7 %psum.7 = f32[4,256]{1,0:T(4,128)S(1)} all-reduce(f32[4,256]{1,0:T(4,128)S(1)} %pad_maximum_fusion.32), channel_id=1, replica_groups=mesh['rep'=4,'grp'=8] {'rep'}, use_global_device_ids=true, to_apply=%region_15.16 | all-reduce | flops 1024 | bytes 8192 | tf_op jit(solution)/shard_map/psum | solution.py:328
  909.2 13.4 %collective-permute-done.110 = bf16[256,768]{1,0:T(8,128)(2,1)S(1)} collective-permute-done((bf16[256,768]{1,0:T(8,128)(2,1)S(1)}, bf16[256,768]{1,0:T(8,128)(2,1)S(1)}, u32[]{:S(2)}, u32[]{:S(2)}) %collective-permute-start.110) | collective-permute-done | bytes 393248 | tf_op jit(solution)/shard_map/ppermute | solution.py:28
  924.5 16.6 %collective-permute-done.112 = bf16[256,768]{1,0:T(8,128)(2,1)S(1)} collective-permute-done((bf16[256,768]{1,0:T(8,128)(2,1)S(1)}, bf16[256,768]{1,0:T(8,128)(2,1)S(1)}, u32[]{:S(2)}, u32[]{:S(2)}) %collective-permute-start.112) | collective-permute-done | bytes 393248 | tf_op jit(solution)/shard_map/ppermute | solution.py:28
  941.3 17.0 %collective-permute-done.113 = bf16[256,768]{1,0:T(8,128)(2,1)S(1)} collective-permute-done((bf16[256,768]{1,0:T(8,128)(2,1)S(1)}, bf16[256,768]{1,0:T(8,128)(2,1)S(1)}, u32[]{:S(2)}, u32[]{:S(2)}) %collective-permute-start.113) | collective-permute-done | bytes 393248 | tf_op jit(solution)/shard_map/ppermute | solution.py:28
  958.4 11.7 collective-permute-done.114
  971.7 11.0 collective-permute-done.116
  998.0 62.3 %collective-permute-done.103 = bf16[256,512]{1,0:T(8,128)(2,1)S(1)} collective-permute-done((bf16[256,512]{1,0:T(8,128)(2,1)S(1)}, bf16[256,512]{1,0:T(8,128)(2,1)S(1)}, u32[]{:S(2)}, u32[]{:S(2)}) %collective-permute-start.103) | collective-permute-done | bytes 262176 | tf_op jit(solution)/shard_map/ppermute | solution.py:28
  1063.1 11.2 collective-permute-done.83
  1081.0 13.5 %collective-permute-start.85 = (bf16[64,768]{1,0:T(8,128)(2,1)S(1)}, bf16[64,768]{1,0:T(8,128)(2,1)S(1)}, u32[]{:S(2)}, u32[]{:S(2)}) collective-permute-start(bf16[64,768]{1,0:T(8,128)(2,1)S(1)} %get-tuple-element.193), channel_id=1, source_target_pairs={{0,2},{1,3},{2,0},{3,1},{4,6},{5,7},{6,4},{7,5},{8,10},{9,11},{10,... | collective-permute-start | bytes 294920 | tf_op jit(solution)/shard_map/ppermute | solution.py:28
  1135.9 12.8 %collective-permute-done.77 = bf16[128,2048]{1,0:T(8,128)(2,1)S(1)} collective-permute-done((bf16[128,2048]{1,0:T(8,128)(2,1)S(1)}, bf16[128,2048]{1,0:T(8,128)(2,1)S(1)}, u32[]{:S(2)}, u32[]{:S(2)}) %collective-permute-start.77) | collective-permute-done | bytes 524320 | tf_op jit(solution)/shard_map/ppermute | solution.py:28
  (667 shorter events, 651.7 us)
Async XLA Ops:
  6.3 76.6 %collective-permute-start.20 = (bf16[272,512]{1,0:T(8,128)(2,1)}, bf16[272,512]{1,0:T(8,128)(2,1)}, u32[]{:S(2)}, u32[]{:S(2)}) collective-permute-start(bf16[272,512]{1,0:T(8,128)(2,1)} %fusion.74), channel_id=1, source_target_pairs={{0,1},{1,0},{2,3},{3,2},{4,5},{5,4},{6,7},{7,6},{8,9},{9,8},{10,11... | collective-permute-start | bytes 835592 | tf_op jit(solution)/shard_map/ppermute | solution.py:28
  9.3 75.6 %collective-permute-start.21 = (bf16[272,512]{1,0:T(8,128)(2,1)}, bf16[272,512]{1,0:T(8,128)(2,1)}, u32[]{:S(2)}, u32[]{:S(2)}) collective-permute-start(bf16[272,512]{1,0:T(8,128)(2,1)} %fusion.74), channel_id=1, source_target_pairs={{0,2},{1,3},{2,0},{3,1},{4,6},{5,7},{6,4},{7,5},{8,10},{9,11},{10,... | collective-permute-start | bytes 835592 | tf_op jit(solution)/shard_map/ppermute | solution.py:28
  10.9 80.1 %collective-permute-start.23 = (bf16[272,512]{1,0:T(8,128)(2,1)}, bf16[272,512]{1,0:T(8,128)(2,1)}, u32[]{:S(2)}, u32[]{:S(2)}) collective-permute-start(bf16[272,512]{1,0:T(8,128)(2,1)} %fusion.74), channel_id=1, source_target_pairs={{0,4},{1,5},{2,6},{3,7},{4,0},{5,1},{6,2},{7,3},{8,12},{9,13},{10,... | collective-permute-start | bytes 835592 | tf_op jit(solution)/shard_map/ppermute | solution.py:28
  13.5 79.3 %collective-permute-start.25 = (bf16[272,512]{1,0:T(8,128)(2,1)}, bf16[272,512]{1,0:T(8,128)(2,1)}, u32[]{:S(2)}, u32[]{:S(2)}) collective-permute-start(bf16[272,512]{1,0:T(8,128)(2,1)} %fusion.74), channel_id=1, source_target_pairs={{0,6},{1,7},{2,4},{3,5},{4,2},{5,3},{6,0},{7,1},{8,14},{9,15},{10,... | collective-permute-start | bytes 835592 | tf_op jit(solution)/shard_map/ppermute | solution.py:28
  80.3 104.3 %collective-permute-start = (bf16[128,2048]{1,0:T(8,128)(2,1)S(1)}, bf16[128,2048]{1,0:T(8,128)(2,1)}, u32[]{:S(2)}, u32[]{:S(2)}) collective-permute-start(bf16[128,2048]{1,0:T(8,128)(2,1)S(1)} %bitcast.383), channel_id=1, source_target_pairs={{0,1},{1,0},{2,3},{3,2},{4,5},{5,4},{6,7},{7,6},{8,9},{9,8},{10,11... | collective-permute-start | bytes 1572872 | tf_op jit(solution)/shard_map/ppermute | solution.py:28
  82.9 105.1 %collective-permute-start.1 = (bf16[128,2048]{1,0:T(8,128)(2,1)S(1)}, bf16[128,2048]{1,0:T(8,128)(2,1)}, u32[]{:S(2)}, u32[]{:S(2)}) collective-permute-start(bf16[128,2048]{1,0:T(8,128)(2,1)S(1)} %bitcast.384), channel_id=1, source_target_pairs={{0,2},{1,3},{2,0},{3,1},{4,6},{5,7},{6,4},{7,5},{8,10},{9,11},{10,... | collective-permute-start | bytes 1572872 | tf_op jit(solution)/shard_map/ppermute | solution.py:28
  84.9 135.7 %collective-permute-start.3 = (bf16[128,2048]{1,0:T(8,128)(2,1)S(1)}, bf16[128,2048]{1,0:T(8,128)(2,1)S(1)}, u32[]{:S(2)}, u32[]{:S(2)}) collective-permute-start(bf16[128,2048]{1,0:T(8,128)(2,1)S(1)} %bitcast.385), channel_id=1, source_target_pairs={{0,4},{1,5},{2,6},{3,7},{4,0},{5,1},{6,2},{7,3},{8,12},{9,13},{10,... | collective-permute-start | bytes 1572872 | tf_op jit(solution)/shard_map/ppermute | solution.py:28
  167.8 54.3 %collective-permute-start.5 = (bf16[128,2048]{1,0:T(8,128)(2,1)S(1)}, bf16[128,2048]{1,0:T(8,128)(2,1)}, u32[]{:S(2)}, u32[]{:S(2)}) collective-permute-start(bf16[128,2048]{1,0:T(8,128)(2,1)S(1)} %bitcast.386), channel_id=1, source_target_pairs={{0,6},{1,7},{2,4},{3,5},{4,2},{5,3},{6,0},{7,1},{8,14},{9,15},{10,... | collective-permute-start | bytes 1572872 | tf_op jit(solution)/shard_map/ppermute | solution.py:28
  212.7 123.1 %collective-permute-start.44 = (bf16[2048,512]{1,0:T(8,128)(2,1)}, bf16[2048,512]{1,0:T(8,128)(2,1)}, u32[]{:S(2)}, u32[]{:S(2)}) collective-permute-start(bf16[2048,512]{1,0:T(8,128)(2,1)} %bitcast.60), channel_id=1, source_target_pairs={{0,8},{8,0},{16,24},{24,16},{1,9},{9,1},{17,25},{25,17},{2,10},{10... | collective-permute-start | bytes 6291464 | tf_op jit(solution)/shard_map/ppermute | solution.py:28
  219.9 75.8 %collective-permute-start.45 = (bf16[2048,512]{1,0:T(8,128)(2,1)}, bf16[2048,512]{1,0:T(8,128)(2,1)}, u32[]{:S(2)}, u32[]{:S(2)}) collective-permute-start(bf16[2048,512]{1,0:T(8,128)(2,1)} %bitcast.60), channel_id=1, source_target_pairs={{0,16},{8,24},{16,0},{24,8},{1,17},{9,25},{17,1},{25,9},{2,18},{10... | collective-permute-start | bytes 6291464 | tf_op jit(solution)/shard_map/ppermute | solution.py:28
  220.6 172.5 %collective-permute-start.48 = (bf16[2048,256]{1,0:T(8,128)(2,1)}, bf16[2048,256]{1,0:T(8,128)(2,1)}, u32[]{:S(2)}, u32[]{:S(2)}) collective-permute-start(bf16[2048,256]{1,0:T(8,128)(2,1)} %bitcast.70), channel_id=1, source_target_pairs={{0,16},{8,24},{16,0},{24,8},{1,17},{9,25},{17,1},{25,9},{2,18},{10... | collective-permute-start | bytes 3145736 | tf_op jit(solution)/shard_map/ppermute | solution.py:28
  255.3 84.9 %collective-permute-start.27 = (bf16[2048,512]{1,0:T(8,128)(2,1)}, bf16[2048,512]{1,0:T(8,128)(2,1)}, u32[]{:S(2)}, u32[]{:S(2)}) collective-permute-start(bf16[2048,512]{1,0:T(8,128)(2,1)} %bitcast.43), channel_id=1, source_target_pairs={{0,8},{8,0},{16,24},{24,16},{1,9},{9,1},{17,25},{25,17},{2,10},{10... | collective-permute-start | bytes 6291464 | tf_op jit(solution)/shard_map/ppermute | solution.py:28
  289.7 46.0 %collective-permute-start.28 = (bf16[2048,512]{1,0:T(8,128)(2,1)}, bf16[2048,512]{1,0:T(8,128)(2,1)}, u32[]{:S(2)}, u32[]{:S(2)}) collective-permute-start(bf16[2048,512]{1,0:T(8,128)(2,1)} %bitcast.43), channel_id=1, source_target_pairs={{0,16},{8,24},{16,0},{24,8},{1,17},{9,25},{17,1},{25,9},{2,18},{10... | collective-permute-start | bytes 6291464 | tf_op jit(solution)/shard_map/ppermute | solution.py:28
  295.7 50.6 %collective-permute-start.46 = (bf16[2048,512]{1,0:T(8,128)(2,1)}, bf16[2048,512]{1,0:T(8,128)(2,1)S(1)}, u32[]{:S(2)}, u32[]{:S(2)}) collective-permute-start(bf16[2048,512]{1,0:T(8,128)(2,1)} %collective-permute-done.45), channel_id=1, source_target_pairs={{0,8},{8,0},{16,24},{24,16},{1,9},{9,1},{17,25},{25,17},{2,10},{10... | collective-permute-start | bytes 6291464 | tf_op jit(solution)/shard_map/ppermute | solution.py:28
  301.4 49.8 %all-to-all-start = ((bf16[8,128,256]{1,2,0:T(8,128)(2,1)}), bf16[8,128,256]{1,2,0:T(8,128)(2,1)S(1)}, u32[]{:S(2)}, u32[]{:S(2)}) async-start(bf16[8,128,256]{1,2,0:T(8,128)(2,1)} %copy.193), calls=%async_computation | async-start | bytes 1048576 | tf_op jit(solution)/shard_map/all_to_all | solution.py:228
  393.1 54.9 %collective-permute-start.47 = (bf16[2048,256]{1,0:T(8,128)(2,1)}, bf16[2048,256]{1,0:T(8,128)(2,1)S(1)}, u32[]{:S(2)}, u32[]{:S(2)}) collective-permute-start(bf16[2048,256]{1,0:T(8,128)(2,1)} %bitcast.70), channel_id=1, source_target_pairs={{0,8},{8,0},{16,24},{24,16},{1,9},{9,1},{17,25},{25,17},{2,10},{10... | collective-permute-start | bytes 3145736 | tf_op jit(solution)/shard_map/ppermute | solution.py:28
  393.2 54.8 %collective-permute-start.49 = (bf16[2048,256]{1,0:T(8,128)(2,1)}, bf16[2048,256]{1,0:T(8,128)(2,1)S(1)}, u32[]{:S(2)}, u32[]{:S(2)}) collective-permute-start(bf16[2048,256]{1,0:T(8,128)(2,1)} %collective-permute-done.48), channel_id=1, source_target_pairs={{0,8},{8,0},{16,24},{24,16},{1,9},{9,1},{17,25},{25,17},{2,10},{10... | collective-permute-start | bytes 3145736 | tf_op jit(solution)/shard_map/ppermute | solution.py:28
  738.5 155.6 %collective-permute-start.107 = (bf16[2048,768]{0,1:T(8,128)(2,1)}, bf16[2048,768]{0,1:T(8,128)(2,1)}, u32[]{:S(2)}, u32[]{:S(2)}) collective-permute-start(bf16[2048,768]{0,1:T(8,128)(2,1)} %pad_maximum_fusion.4), channel_id=1, source_target_pairs={{0,8},{8,0},{16,24},{24,16},{1,9},{9,1},{17,25},{25,17},{2,10},{10... | collective-permute-start | bytes 9437192 | tf_op jit(solution)/shard_map/ppermute | solution.py:28
  740.9 63.2 %collective-permute-start.108 = (bf16[2048,768]{0,1:T(8,128)(2,1)}, bf16[2048,768]{0,1:T(8,128)(2,1)}, u32[]{:S(2)}, u32[]{:S(2)}) collective-permute-start(bf16[2048,768]{0,1:T(8,128)(2,1)} %pad_maximum_fusion.5), channel_id=1, source_target_pairs={{0,8},{8,0},{16,24},{24,16},{1,9},{9,1},{17,25},{25,17},{2,10},{10... | collective-permute-start | bytes 9437192 | tf_op jit(solution)/shard_map/ppermute | solution.py:28
  786.4 98.3 %collective-permute-start.96 = (bf16[128,2048]{1,0:T(8,128)(2,1)}, bf16[128,2048]{1,0:T(8,128)(2,1)}, u32[]{:S(2)}, u32[]{:S(2)}) collective-permute-start(bf16[128,2048]{1,0:T(8,128)(2,1)} %collective-permute-done.95), channel_id=1, source_target_pairs={{0,1},{1,0},{2,3},{3,2},{4,5},{5,4},{6,7},{7,6},{8,9},{9,8},{10,11... | collective-permute-start | bytes 1572872 | tf_op jit(solution)/shard_map/ppermute | solution.py:28
  787.9 100.6 %collective-permute-start.98 = (bf16[128,2048]{1,0:T(8,128)(2,1)}, bf16[128,2048]{1,0:T(8,128)(2,1)S(1)}, u32[]{:S(2)}, u32[]{:S(2)}) collective-permute-start(bf16[128,2048]{1,0:T(8,128)(2,1)} %collective-permute-done.97), channel_id=1, source_target_pairs={{0,1},{1,0},{2,3},{3,2},{4,5},{5,4},{6,7},{7,6},{8,9},{9,8},{10,11... | collective-permute-start | bytes 1572872 | tf_op jit(solution)/shard_map/ppermute | solution.py:28
  794.5 97.2 %collective-permute-start.100 = (bf16[128,2048]{1,0:T(8,128)(2,1)}, bf16[128,2048]{1,0:T(8,128)(2,1)S(1)}, u32[]{:S(2)}, u32[]{:S(2)}) collective-permute-start(bf16[128,2048]{1,0:T(8,128)(2,1)} %collective-permute-done.99), channel_id=1, source_target_pairs={{0,1},{1,0},{2,3},{3,2},{4,5},{5,4},{6,7},{7,6},{8,9},{9,8},{10,11... | collective-permute-start | bytes 1572872 | tf_op jit(solution)/shard_map/ppermute | solution.py:28
  808.3 85.8 %collective-permute-start.109 = (bf16[2048,768]{0,1:T(8,128)(2,1)}, bf16[2048,768]{0,1:T(8,128)(2,1)}, u32[]{:S(2)}, u32[]{:S(2)}) collective-permute-start(bf16[2048,768]{0,1:T(8,128)(2,1)} %add_convert_fusion.1), channel_id=1, source_target_pairs={{0,16},{8,24},{16,0},{24,8},{1,17},{9,25},{17,1},{25,9},{2,18},{10... | collective-permute-start | bytes 9437192 | tf_op jit(solution)/shard_map/ppermute | solution.py:28
  884.7 101.0 %collective-permute-start.82 = (bf16[8,64,768]{2,1,0:T(8,128)(2,1)}, bf16[8,64,768]{2,1,0:T(8,128)(2,1)}, u32[]{:S(2)}, u32[]{:S(2)}) collective-permute-start(bf16[8,64,768]{2,1,0:T(8,128)(2,1)} %get-tuple-element.138), channel_id=1, source_target_pairs={{0,8},{8,0},{16,24},{24,16},{1,9},{9,1},{17,25},{25,17},{2,10},{10... | collective-permute-start | bytes 2359304 | tf_op jit(solution)/shard_map/ppermute | solution.py:28
  888.5 98.8 %collective-permute-start.74 = (bf16[128,2048]{1,0:T(8,128)(2,1)}, bf16[128,2048]{1,0:T(8,128)(2,1)}, u32[]{:S(2)}, u32[]{:S(2)}) collective-permute-start(bf16[128,2048]{1,0:T(8,128)(2,1)} %get-tuple-element.80), channel_id=1, source_target_pairs={{0,1},{1,0},{2,3},{3,2},{4,5},{5,4},{6,7},{7,6},{8,9},{9,8},{10,11... | collective-permute-start | bytes 1572872 | tf_op jit(solution)/shard_map/ppermute | solution.py:28
  891.7 96.1 %collective-permute-start.76 = (bf16[128,2048]{1,0:T(8,128)(2,1)}, bf16[128,2048]{1,0:T(8,128)(2,1)}, u32[]{:S(2)}, u32[]{:S(2)}) collective-permute-start(bf16[128,2048]{1,0:T(8,128)(2,1)} %get-tuple-element.83), channel_id=1, source_target_pairs={{0,1},{1,0},{2,3},{3,2},{4,5},{5,4},{6,7},{7,6},{8,9},{9,8},{10,11... | collective-permute-start | bytes 1572872 | tf_op jit(solution)/shard_map/ppermute | solution.py:28
  983.5 139.1 %collective-permute-start.118 = (bf16[8,256,768]{2,1,0:T(8,128)(2,1)S(1)}, bf16[8,256,768]{2,1,0:T(8,128)(2,1)S(1)}, u32[]{:S(2)}, u32[]{:S(2)}) collective-permute-start(bf16[8,256,768]{2,1,0:T(8,128)(2,1)S(1)} %bitcast_dynamic-update-slice_fusion.22), channel_id=1, source_target_pairs={{0,16},{8,24},{16,0},{24,8},{1,17},{9,25},{17,1},{25,9},{2,18},{10... | collective-permute-start | bytes 9437192 | tf_op jit(solution)/shard_map/ppermute | solution.py:28
  985.8 77.3 %collective-permute-start.81 = (bf16[8,64,768]{2,1,0:T(8,128)(2,1)S(1)}, bf16[8,64,768]{2,1,0:T(8,128)(2,1)S(1)}, u32[]{:S(2)}, u32[]{:S(2)}) collective-permute-start(bf16[8,64,768]{2,1,0:T(8,128)(2,1)S(1)} %copy-done.34), channel_id=1, source_target_pairs={{0,8},{8,0},{16,24},{24,16},{1,9},{9,1},{17,25},{25,17},{2,10},{10... | collective-permute-start | bytes 2359304 | tf_op jit(solution)/shard_map/ppermute | solution.py:28
  987.8 72.5 %collective-permute-start.103 = (bf16[256,512]{1,0:T(8,128)(2,1)S(1)}, bf16[256,512]{1,0:T(8,128)(2,1)S(1)}, u32[]{:S(2)}, u32[]{:S(2)}) collective-permute-start(bf16[256,512]{1,0:T(8,128)(2,1)S(1)} %add_convert_fusion.8), channel_id=1, source_target_pairs={{0,16},{8,24},{16,0},{24,8},{1,17},{9,25},{17,1},{25,9},{2,18},{10... | collective-permute-start | bytes 786440 | tf_op jit(solution)/shard_map/ppermute | solution.py:28
  994.4 79.9 %collective-permute-start.83 = (bf16[8,64,768]{2,1,0:T(8,128)(2,1)S(1)}, bf16[8,64,768]{2,1,0:T(8,128)(2,1)S(1)}, u32[]{:S(2)}, u32[]{:S(2)}) collective-permute-start(bf16[8,64,768]{2,1,0:T(8,128)(2,1)S(1)} %fusion.11), channel_id=1, source_target_pairs={{0,16},{8,24},{16,0},{24,8},{1,17},{9,25},{17,1},{25,9},{2,18},{10... | collective-permute-start | bytes 2359304 | tf_op jit(solution)/shard_map/ppermute | solution.py:28
  997.6 117.6 %collective-permute-start.80 = (bf16[128,2048]{1,0:T(8,128)(2,1)S(1)}, bf16[128,2048]{1,0:T(8,128)(2,1)S(1)}, u32[]{:S(2)}, u32[]{:S(2)}) collective-permute-start(bf16[128,2048]{1,0:T(8,128)(2,1)S(1)} %copy-done.39), channel_id=1, source_target_pairs={{0,1},{1,0},{2,3},{3,2},{4,5},{5,4},{6,7},{7,6},{8,9},{9,8},{10,11... | collective-permute-start | bytes 1572872 | tf_op jit(solution)/shard_map/ppermute | solution.py:28
  1060.3 66.1 %collective-permute-start.75 = (bf16[128,2048]{1,0:T(8,128)(2,1)S(1)}, bf16[128,2048]{1,0:T(8,128)(2,1)S(1)}, u32[]{:S(2)}, u32[]{:S(2)}) collective-permute-start(bf16[128,2048]{1,0:T(8,128)(2,1)S(1)} %get-tuple-element.77), channel_id=1, source_target_pairs={{0,6},{1,7},{2,4},{3,5},{4,2},{5,3},{6,0},{7,1},{8,14},{9,15},{10,... | collective-permute-start | bytes 1572872 | tf_op jit(solution)/shard_map/ppermute | solution.py:28
  (181 other events, 4172.2 us)

commit v2 on v1

--- a/solution.py
+++ b/solution.py
@@ -1,6 +1,8 @@
 import jax
 import jax.numpy as jnp
 from jax import lax
+from jax.experimental import pallas as pl
+from jax.experimental.pallas import tpu as pltpu
 from jax.sharding import PartitionSpec as P
 
 HEADS = 16
@@ -28,32 +30,46 @@
     return lax.ppermute(value, axis, [(i, i ^ step) for i in range(lax.axis_size(axis))])
 
 
-def gather_pieces(value):
+def tie(value, *others):
+    return lax.optimization_barrier((value, *others))[0]
+
+
+def gather_pieces(value, *meanwhile):
     count = lax.axis_size("grp")
+    top = count - 2
     pieces = [None] * count
     pieces[0] = value
-    for step in range(count - 2, 0, -2):
+    pieces[top] = shuffle(value, "grp", top)
+    for step in range(2, count // 2, 2):
         pieces[step] = shuffle(value, "grp", step)
-    for step in [0, *range(count - 2, 0, -2)]:
-        pieces[step + 1] = shuffle(pieces[step], "grp", 1)
+    pieces[1] = shuffle(value, "grp", 1)
+    for step in range(count // 2, top, 2):
+        pieces[step] = shuffle(pieces[top], "grp", step ^ top)
+    steps = [*range(2, count // 2, 2), top, *range(count // 2, top, 2)]
+    for step in steps:
+        held = meanwhile if step == steps[-1] else ()
+        pieces[step + 1] = shuffle(tie(pieces[step], *held) if held else pieces[step], "grp", 1)
     return pieces
 
 
-def scatter_sum(pieces):
-    count = len(pieces)
-    order = [*range(count - 2, -1, -2)]
-    moved = {step: shuffle(pieces[step + 1].astype(BF), "grp", 1) for step in order}
-    total = None
-    for step in order:
-        paired = pieces[step].astype(F32) + moved[step].astype(F32)
-        if step:
-            paired = shuffle(paired.astype(BF), "grp", step).astype(F32)
-        total = paired if total is None else total + paired
-    return total
-
-
-def exchange(pieces):
-    return [pieces[0]] + [shuffle(pieces[k], "grp", k) for k in range(1, len(pieces))]
+def scatter_sum(pieces, *meanwhile):
+    steps = [*range(len(pieces) - 2, 0, -2)]
+    cut = pieces[0].shape[1] * 3 // 4
+    left = [p[:, :cut] for p in pieces]
+    right = [p[:, cut:] for p in pieces]
+    odd = shuffle(jnp.stack([left[k + 1].astype(BF) for k in steps]), "grp", 1)
+    far = [shuffle(jnp.stack([right[k].astype(BF), right[k + 1].astype(BF)]), "grp", k) for k in steps]
+    paired = [left[k].astype(F32) + odd[i].astype(F32) for i, k in enumerate(steps)]
+    moved = [shuffle(p.astype(BF), "grp", k) for p, k in zip(paired, steps)]
+    both = [right[i].astype(F32) + sum(f[i].astype(F32) for f in far) for i in (0, 1)]
+    last = jnp.concatenate([left[1].astype(BF), both[1].astype(BF)], axis=1)
+    last = shuffle(tie(last, *meanwhile) if meanwhile else last, "grp", 1)
+    total_left = left[0].astype(F32) + sum(m.astype(F32) for m in moved)
+    return jnp.concatenate([total_left, both[0]], axis=1) + last.astype(F32), last
+
+
+def to_columns(blocks):
+    return lax.all_to_all(blocks, "grp", 0, 0, tiled=True)
 
 
 def group_sum(value):
@@ -64,16 +80,101 @@
     return value
 
 
-def across_rep(value):
-    far = shuffle(value, "rep", 2)
-    return [value, shuffle(value, "rep", 1), far, shuffle(far, "rep", 1)]
-
-
-def rep_sum(parts):
-    near = [
-        (parts[j].astype(F32) + shuffle(parts[j ^ 1].astype(BF), "rep", 1).astype(F32)) for j in (0, 2)
-    ]
-    return (near[0] + shuffle(near[1].astype(BF), "rep", 2).astype(F32)).astype(BF)
+def rep_near(value):
+    return shuffle(value, "rep", 1)
+
+
+def rep_far(value):
+    return shuffle(value, "rep", 2)
+
+
+def near_send(parts):
+    return rep_near(jnp.stack([parts[1], parts[3]]))
+
+
+def far_send(parts, near):
+    return rep_far((parts[2].astype(F32) + near[1].astype(F32)).astype(BF))
+
+
+def rep_total(parts, near, far):
+    return (parts[0].astype(F32) + near[0].astype(F32) + far.astype(F32)).astype(BF)
+
+
+def lay_kernel(rep_ref, here_ref, there_ref, *out_refs):
+    del rep_ref
+    wide = here_ref.shape[3] // len(out_refs)
+    here = pl.program_id(0) % 2 == 0
+    for i, out_ref in enumerate(out_refs):
+        for g in range(here_ref.shape[1]):
+            piece = jnp.where(
+                here,
+                here_ref[0, g, :, i * wide : (i + 1) * wide].astype(F32),
+                there_ref[0, g, :, i * wide : (i + 1) * wide].astype(F32),
+            )
+            out_ref[:, g * wide : (g + 1) * wide] = piece
+
+
+def lay_rows(rep, here, there):
+    _, groups, rows, wide = here.shape
+    width = groups * wide // 4
+    spec = pl.BlockSpec((1, groups, rows, wide), lambda j, rep_ref: (j // 2, 0, 0, 0))
+    out = pl.BlockSpec((rows, width), lambda j, rep_ref: (rep_ref[0] ^ j, 0))
+    return pl.pallas_call(
+        lay_kernel,
+        grid_spec=pltpu.PrefetchScalarGridSpec(
+            num_scalar_prefetch=1, grid=(4,), in_specs=[spec, spec], out_specs=[out] * 4
+        ),
+        out_shape=[jax.ShapeDtypeStruct((4 * rows, width), F32)] * 4,
+        cost_estimate=pl.CostEstimate(flops=0, bytes_accessed=here.size * 12, transcendentals=0),
+    )(rep[None], here, there)
+
+
+def cut_kernel(rep_ref, gate_ref, up_ref, down_ref, gate_out, up_out, down_out):
+    del rep_ref
+    gate_out[0] = gate_ref[...]
+    up_out[0] = up_ref[...]
+    down_out[0] = down_ref[...].T
+
+
+def cut(rep, gate, up, down, groups, reps):
+    rows, part = gate.shape[0], gate.shape[1] // (groups * reps)
+    wide = pl.BlockSpec((rows, part), lambda g, rep_ref: (0, g * reps + rep_ref[0]))
+    tall = pl.BlockSpec((part, rows), lambda g, rep_ref: (g * reps + rep_ref[0], 0))
+    out = pl.BlockSpec((1, rows, part), lambda g, rep_ref: (g, 0, 0))
+    return pl.pallas_call(
+        cut_kernel,
+        grid_spec=pltpu.PrefetchScalarGridSpec(
+            num_scalar_prefetch=1, grid=(groups,), in_specs=[wide, wide, tall], out_specs=[out] * 3
+        ),
+        out_shape=[jax.ShapeDtypeStruct((groups, rows, part), BF)] * 3,
+        cost_estimate=pl.CostEstimate(flops=0, bytes_accessed=groups * rows * part * 12, transcendentals=0),
+    )(rep[None], gate, up, down)
+
+
+def widen_kernel(x_ref, o_ref):
+    for r in range(x_ref.shape[0]):
+        wide = x_ref.shape[3]
+        o_ref[:, r * wide : (r + 1) * wide] = x_ref[r, 0].astype(F32)
+
+
+def widen_turned_kernel(x_ref, o_ref):
+    for r in range(x_ref.shape[0]):
+        tall = x_ref.shape[3]
+        o_ref[r * tall : (r + 1) * tall, :] = x_ref[r, 0].astype(F32).T
+
+
+def widen(parts, turned):
+    reps, count, rows, wide = parts.shape
+    out = (rows, reps * wide) if not turned else (reps * wide, rows)
+    full = (rows, reps * count * wide) if not turned else (reps * count * wide, rows)
+    return pl.pallas_call(
+        widen_turned_kernel if turned else widen_kernel,
+        grid=(count,),
+        in_specs=[pl.BlockSpec((reps, 1, rows, wide), lambda s: (0, s, 0, 0))],
+        out_specs=pl.BlockSpec(out, (lambda s: (s, 0)) if turned else (lambda s: (0, s))),
+        out_shape=jax.ShapeDtypeStruct(full, F32),
+        cost_estimate=pl.CostEstimate(flops=0, bytes_accessed=parts.size * 6, transcendentals=0),
+    )(parts)
 
 
 def put(buffer, part, starts):
@@ -155,63 +256,36 @@
     at = [me ^ k for k in range(groups)]
     of = [rep ^ j for j in range(reps)]
 
-    sends = [
-        jnp.concatenate(
-            [lax.dynamic_slice(w, (rep * sub, at[k] * own), (sub, own)) for w in (q_weight, k_weight, v_weight)],
-            axis=1,
-        )
-        for k in range(groups)
-    ]
-    landed = jnp.zeros((groups, sub, 3 * own), BF)
-    for k, piece in enumerate(exchange(sends)):
-        landed = put(landed, piece[None], (at[k], zero, zero))
+    qkv_rows = jnp.concatenate(
+        [
+            lax.dynamic_slice(w, (rep * sub, zero), (sub, width)).reshape(sub, groups, own)
+            for w in (q_weight, k_weight, v_weight)
+        ],
+        axis=2,
+    )
+    gains = jnp.pad(jnp.concatenate([attn_gain, mlp_gain])[None], ((0, 7), (0, own)))
+    gains = jnp.broadcast_to(gains[None], (groups, 8, 3 * own))
+    landed = to_columns(jnp.concatenate([jnp.transpose(qkv_rows, (1, 0, 2)), gains], axis=1))
+    gain_all = landed[:, sub, : 2 * own].astype(F32).reshape(groups, 2, own)
+    ga, gm = gain_all[:, 0].reshape(width), gain_all[:, 1].reshape(width)
+    mine = landed[:, :sub]
+    far = rep_far(mine)
+    x_pieces = gather_pieces(x, far)
+    near = rep_near(jnp.stack([mine, far]))
     w_qkv = jnp.zeros((groups, reps, sub, 3 * own), BF)
-    for j, piece in enumerate(across_rep(landed)):
+    for j, piece in enumerate([mine, near[0], far, near[1]]):
         w_qkv = put(w_qkv, piece[:, None], (zero, of[j], zero, zero))
     w_qkv = w_qkv.reshape(width, 3 * own)
 
     x_all = jnp.zeros((groups, count, width), BF)
-    for k, piece in enumerate(gather_pieces(x)):
+    for k, piece in enumerate(x_pieces):
         x_all = put(x_all, piece[None], (at[k], zero, zero))
     x_all = x_all.reshape(length, width)
 
-    stripe = width // reps
-    gains = jnp.concatenate([attn_gain, mlp_gain])
-    gains = jnp.pad(gains[None], ((0, 15), (0, stripe - 2 * own)))
-    o_part = jnp.concatenate([lax.dynamic_slice(o_weight, (zero, rep * stripe), (own, stripe)), gains])
-    o_mine = jnp.zeros((groups, own, stripe), BF)
-    gain_all = jnp.zeros((groups, 2, own), BF)
-    for k, piece in enumerate(gather_pieces(o_part)):
-        o_mine = put(o_mine, piece[None, :own], (at[k], zero, zero))
-        gain_all = put(gain_all, piece[own, : 2 * own].reshape(1, 2, own), (at[k], zero, zero))
-    w_o = jnp.zeros((width, width), BF)
-    for j, piece in enumerate(across_rep(o_mine.reshape(width, stripe))):
-        w_o = put(w_o, piece, (zero, of[j] * stripe))
-    ga = gain_all[:, 0].reshape(width).astype(F32)
-    gm = gain_all[:, 1].reshape(width).astype(F32)
-
-    sends = []
-    for k in range(groups):
-        start = at[k] * block + rep * part
-        sends.append(
-            jnp.concatenate(
-                [
-                    lax.dynamic_slice(gate_weight, (zero, start), (own, part)),
-                    lax.dynamic_slice(up_weight, (zero, start), (own, part)),
-                    lax.dynamic_slice(down_weight, (start, zero), (part, own)).T,
-                ],
-                axis=1,
-            )
-        )
-    landed_gu = jnp.zeros((groups, own, 2 * part), BF)
-    landed_d = jnp.zeros((groups, own, part), BF)
-    for k, piece in enumerate(exchange(sends)):
-        landed_gu = put(landed_gu, piece[None, :, : 2 * part], (at[k], zero, zero))
-        landed_d = put(landed_d, piece[None, :, 2 * part :], (at[k], zero, zero))
-    gu_parts = across_rep(landed_gu.reshape(width, 2 * part))
-    d_parts = across_rep(landed_d.reshape(width, part))
-    w_gu = jnp.concatenate([p[:, :part] for p in gu_parts] + [p[:, part:] for p in gu_parts], axis=1)
-    w_d = jnp.concatenate(d_parts, axis=1)
+    sends = cut(rep, gate_weight, up_weight, down_weight, groups, reps)
+
+    def spread(blocks):
+        return lax.all_gather(blocks.reshape(width, part), "rep", axis=1, tiled=True)
 
     gq, gk = q_gain.astype(F32), k_gain.astype(F32)
     cosine, sine = angles_of(length)
@@ -225,59 +299,69 @@
     queries = turn(q_proj * q_inv * gq, cosine, sine).astype(BF)
     keys = turn(k_proj * k_inv * gk, cosine, sine).astype(BF)
     attn, lse = attend(queries, keys, values)
-    attn_tok = lax.all_to_all(attn, "grp", 0, 1, tiled=True)
-    a_proj = dot(attn_tok, w_o)
+    gu_landed = tie(to_columns(tie(jnp.concatenate(sends[:2], axis=2), x_all)), attn)
+    w_gate, w_up = spread(gu_landed[..., :part]), spread(gu_landed[..., part:])
+    a_part = dot(attn, o_weight)
+    a_proj, _ = scatter_sum(
+        [lax.dynamic_slice(a_part, (at[k] * count, zero), (count, width)) for k in range(groups)]
+    )
+    w_down = spread(tie(to_columns(tie(sends[2], attn)), a_proj))
     middle = x.astype(F32) + rms(a_proj, ga)
     middle_bf = middle.astype(BF)
 
-    h_all = jnp.concatenate(gather_pieces(middle_bf))
-    gu = dot(h_all, w_gu)
-    gates, uppers = gu[:, :block], gu[:, block:]
-    mixed = swiglu(gates, uppers).astype(BF)
-    y_part = dot_right_t(mixed, w_d).reshape(groups, count, width)
-    y_proj = scatter_sum([y_part[k] for k in range(groups)])
+    def halves(pieces):
+        return jnp.concatenate(pieces[0::2]), jnp.concatenate(pieces[1::2])
+
+    def whole(even, odd):
+        even, odd = (v.reshape(groups // 2, count, width) for v in (even, odd))
+        return [(even, odd)[k % 2][k // 2] for k in range(groups)]
+
+    h_halves = halves(gather_pieces(middle_bf, w_gate))
+    gates = [dot(h, w_gate) for h in h_halves]
+    uppers = [dot(h, w_up) for h in h_halves]
+    mixed = [swiglu(g, u).astype(BF) for g, u in zip(gates, uppers)]
+    y_proj, _ = scatter_sum(whole(*[dot_right_t(m, w_down) for m in mixed]))
     outputs = (middle + rms(y_proj, gm)).astype(BF)
 
     grad_out = cotangent[0].astype(F32)
     _, pull = jax.vjp(rms, y_proj, gm)
     dy, d_mlp_gain = pull(grad_out)
-    dy_all = jnp.concatenate(gather_pieces(dy.astype(BF)))
-    d_mixed = dot(dy_all, w_d)
-    _, pull = jax.vjp(swiglu, gates, uppers)
-    d_gu = jnp.concatenate([v.astype(BF) for v in pull(d_mixed)], axis=1)
-    m_part = dot_right_t(d_gu, w_gu).reshape(groups, count, width)
-    d_middle = grad_out + scatter_sum([m_part[k] for k in range(groups)])
-
-    g_gu = dot_left_t(h_all, d_gu).astype(BF)
-    g_d = dot_left_t(dy_all, mixed).astype(BF)
-    sums = rep_sum(
-        [
-            jnp.concatenate(
-                [
-                    g_gu[:, j * part : (j + 1) * part],
-                    g_gu[:, block + j * part : block + (j + 1) * part],
-                    g_d[:, j * part : (j + 1) * part],
-                ],
-                axis=1,
-            )
-            for j in range(reps)
-        ]
-    ).reshape(groups, own, 3 * part)
-    sends = [lax.dynamic_slice(sums, (at[k], zero, zero), (1, own, 3 * part))[0] for k in range(groups)]
-    g_mlp = jnp.zeros((groups, own, 3 * part), BF)
-    for k, piece in enumerate(exchange(sends)):
-        g_mlp = put(g_mlp, piece[None], (at[k], zero, zero))
-    g_mlp = jnp.stack(across_rep(lax.optimization_barrier(g_mlp)))
-    g_mlp = jnp.concatenate([lax.dynamic_slice(g_mlp, (of[j], zero, zero, zero), (1, groups, own, 3 * part)) for j in range(reps)])
-    gate_grad = jnp.transpose(g_mlp[..., :part], (2, 1, 0, 3)).reshape(own, hidden).astype(F32)
-    up_grad = jnp.transpose(g_mlp[..., part : 2 * part], (2, 1, 0, 3)).reshape(own, hidden).astype(F32)
-    down_grad = jnp.transpose(g_mlp[..., 2 * part :], (1, 0, 3, 2)).reshape(hidden, own).astype(F32)
+    dy_halves = halves(gather_pieces(dy.astype(BF)))
+    d_gates, d_uppers, m_halves = [], [], []
+    for g, u, d in zip(gates, uppers, dy_halves):
+        _, pull = jax.vjp(swiglu, g, u)
+        d_gate, d_upper = (v.astype(BF) for v in pull(dot(d, w_down)))
+        d_gates.append(d_gate)
+        d_uppers.append(d_upper)
+        m_halves.append(dot_right_t(d_gate, w_gate) + dot_right_t(d_upper, w_up))
+    d_middle, _ = scatter_sum(whole(*m_halves))
+    d_middle = grad_out + d_middle
+
+    def weight_sum(left, right, later):
+        both = [dot_left_t(a, b) for a, b in zip(left, right)]
+        both = tie((both[0] + both[1]).astype(BF), later)
+        return lax.psum_scatter(both, "rep", scatter_dimension=1, tiled=True)
+
+    def to_place(sums, before, after):
+        return tie(to_columns(tie(sums.reshape(groups, own, part), before)), after)
+
+    def to_rows(sums, turned):
+        return widen(lax.all_gather(lax.optimization_barrier(sums), "rep", axis=0), turned)
 
     _, pull = jax.vjp(rms, a_proj, ga)
     da, d_attn_gain = pull(d_middle)
     da_bf = da.astype(BF)
-    d_attn = lax.all_to_all(dot_right_t(da_bf, w_o).astype(BF), "grp", 1, 0, tiled=True)
+    sum_down = weight_sum(dy_halves, mixed, da_bf)
+    sum_gate = weight_sum(h_halves, d_gates, da_bf)
+    sum_up = weight_sum(h_halves, d_uppers, da_bf)
+    da_pieces = gather_pieces(da_bf)
+    da_all = jnp.zeros((groups, count, width), BF)
+    for k, piece in enumerate(da_pieces):
+        da_all = put(da_all, piece[None], (at[k], zero, zero))
+    da_all = da_all.reshape(length, width)
+    d_attn = dot_right_t(da_all, o_weight).astype(BF)
     dq, dk, dv = attend_back(queries, keys, values, lse, d_attn)
+    down_grad = to_rows(to_place(sum_down, da_all, dq), True)
     dq, dk = turn(dq, cosine, -sine), turn(dk, cosine, -sine)
     q_unit, k_unit = q_proj * q_inv, k_proj * k_inv
     d_q_gain, d_k_gain = jnp.sum(dq * q_unit, axis=0), jnp.sum(dk * k_unit, axis=0)
@@ -296,36 +380,33 @@
         axis=1,
     )
     x_part = dot_right_t(d_qkv, w_qkv)
-    d_x = d_middle + scatter_sum(
-        [lax.dynamic_slice(x_part, (at[k] * count, zero), (count, width)) for k in range(groups)]
-    )
-
-    da_all = jnp.zeros((groups, count, width), BF)
-    for k, piece in enumerate(gather_pieces(da_bf)):
-        da_all = put(da_all, piece[None], (at[k], zero, zero))
-    g_o = dot_left_t(attn, da_all.reshape(length, width)).astype(BF)
-    o_sum = rep_sum([lax.dynamic_slice(g_o, (zero, of[j] * stripe), (own, stripe)) for j in range(reps)])
-    o_grad = jnp.zeros((own, width), F32)
-    for j, piece in enumerate(across_rep(lax.optimization_barrier(o_sum))):
-        o_grad = put(o_grad, piece.astype(F32), (zero, of[j] * stripe))
+    gate_grad = to_rows(to_place(sum_gate, along, x_part), False)
+
     g_qkv = dot_left_t(x_all, d_qkv).astype(BF).reshape(groups, reps, sub, 3 * own)
-    sums = rep_sum(
-        [lax.dynamic_slice(g_qkv, (zero, of[j], zero, zero), (groups, 1, sub, 3 * own))[:, 0] for j in range(reps)]
-    )
-    sends = [lax.dynamic_slice(sums, (at[k], zero, zero), (1, sub, 3 * own))[0] for k in range(groups)]
-    landed = jnp.zeros((groups, sub, 3 * own), BF)
-    for k, piece in enumerate(exchange(sends)):
-        landed = put(landed, piece[None], (at[k], zero, zero))
-    g_qkv = jnp.zeros((reps, groups, sub, 3 * own), BF)
-    for j, piece in enumerate(across_rep(lax.optimization_barrier(landed))):
-        g_qkv = put(g_qkv, piece[None], (of[j], zero, zero, zero))
-    q_grad, k_grad, v_grad = (
-        jnp.transpose(g_qkv[..., i * own : (i + 1) * own], (0, 2, 1, 3)).reshape(own, width).astype(F32)
-        for i in range(3)
-    )
+    g_o = dot_left_t(attn, tie(da_all, dq)).astype(BF).reshape(reps, sub, groups, own)
+    g_all = jnp.concatenate([g_qkv, jnp.transpose(g_o, (2, 0, 1, 3))], axis=3)
+    parts = [
+        lax.dynamic_slice(g_all, (zero, of[j], zero, zero), (groups, 1, sub, 4 * own))[:, 0] for j in range(reps)
+    ]
+    near = near_send(parts)
+    far = far_send(parts, near)
+    d_x, _ = scatter_sum(
+        [lax.dynamic_slice(x_part, (at[k] * count, zero), (count, width)) for k in range(groups)], far
+    )
+    up_grad = to_rows(to_place(sum_up, x_part, d_x), False)
+    sums = rep_total(parts, near, far)
+    rows_of = tie(to_columns(sums[..., : 3 * own]), d_x)
+    d_x = d_middle + tie(d_x, down_grad)
+    mine = jnp.concatenate([rows_of, sums[..., 3 * own :]], axis=2)
+    mine = tie(mine, down_grad)
+    far = rep_far(mine)
+    here = tie(jnp.stack([mine, far]), gate_grad)
+    q_grad, k_grad, v_grad, o_grad = lay_rows(rep, here, rep_near(here))
 
     post = lax.dynamic_slice(along[2 * length :].reshape(2, width), (zero, me * own), (2, own))
-    gain_sums = lax.psum(jnp.concatenate([jnp.stack([d_q_gain, d_k_gain]), post]), "rep")
+    gain_sums = jnp.concatenate([jnp.stack([d_q_gain, d_k_gain]), post])
+    for step in (1, 2):
+        gain_sums = gain_sums + shuffle(gain_sums, "rep", step)
     return (
         outputs[None], d_x.astype(BF)[None], q_grad, k_grad, v_grad, o_grad, gate_grad, up_grad, down_grad,
         gain_sums[0], gain_sums[1], gain_sums[2], gain_sums[3],

time: 1240 us -> 895 us (0.72)
  waiting for transfers between devices: 590 us -> 409 us
  local copies, waits for them, and re-layouts: 196 us -> 60.2 us
  blocking collectives: 63.7 us -> 0 us
  Pallas kernels: 0 us -> 35.6 us
  matrix products: 105 us -> 121 us
  between operations: 3.46 us -> 16.2 us
    ppermute x120 -> x74, waiting for transfers between devices: 587 us -> 381 us  [shuffle(): lax.ppermute(value, axis, [(i, i ^ step) for i in range(lax.axis_size(axi...]
    psum x1 -> x0, blocking collectives: 63.7 us -> none  [by_heads(): lax.psum(jnp.concatenate([jnp.stack([d_q_gain, d_k_gain]), post]), 'rep')]
    dynamic_update_slice x80 -> x19, local copies, waits for them, and re-layouts: 61.9 us -> 16.9 us  [put(): return lax.dynamic_update_slice(buffer, part, starts)]
    ppermute x120 -> x74, starting transfers between devices: 197 us -> 154 us  [shuffle(): lax.ppermute(value, axis, [(i, i ^ step) for i in range(lax.axis_size(axi...]
    pallas_call x0 -> x5, Pallas kernels: none -> 35.6 us  [the longest x3 22.5 us: widen(): pl.pallas_call(widen_turned_kernel if turned else widen_kernel, grid=(cou...]
    unnamed x216 -> x200, local copies, waits for them, and re-layouts: 55.8 us -> 22.7 us
    convert_element_type x5 -> x1, local copies, waits for them, and re-layouts: 32.1 us -> 0.02 us  [by_heads(): gain_all = landed[:, sub, :2 * own].astype(F32).reshape(groups, 2, own)]
    all_to_all x2 -> x7, starting transfers between devices: 7.29 us -> 38.4 us  [to_columns(): return lax.all_to_all(blocks, 'grp', 0, 0, tiled=True)]
  transfers between devices with their start and end apart: 122 -> 90, of which waited for: 61 -> 35; matrix products, arithmetic and copies ran while one was open for 19% -> 20% of each run, Pallas kernels for 0% -> 3%
where the time goes in v2:
time: 895 us; the launch traced here: 888 us
  waiting for transfers between devices  409 us (46%)
  starting transfers between devices  194 us (22%)
  matrix products  121 us (14%)
  local copies, waits for them, and re-layouts  60.2 us (7%)
  other arithmetic  52.4 us (6%)
  Pallas kernels  35.6 us (4%)
  between operations  16.2 us (2%)
    ppermute x74, waiting for transfers between devices, shuffle(): lax.ppermute(value, axis, [(i, i ^ step) for i in range(lax.axis_size(axi...  381 us
    ppermute x74, starting transfers between devices, shuffle(): lax.ppermute(value, axis, [(i, i ^ step) for i in range(lax.axis_size(axi...  154 us
    dot_general x24, matrix products, dot(): lax.dot_general(left, right, (dims, ((), ())), preferred_element_type=kind)  104 us
    all_to_all x7, starting transfers between devices, to_columns(): return lax.all_to_all(blocks, 'grp', 0, 0, tiled=True)  38.4 us
    all_to_all x7, waiting for transfers between devices, to_columns(): return lax.all_to_all(blocks, 'grp', 0, 0, tiled=True)  27.4 us
    unnamed x200, local copies, waits for them, and re-layouts  22.7 us
    pallas_call x3, Pallas kernels, widen(): pl.pallas_call(widen_turned_kernel if turned else widen_kernel, grid=(cou...  22.5 us
  transfers between devices with their start and end apart: 90, of which 35 were waited for; matrix products, arithmetic and copies ran while one was open for 20% of the time, Pallas kernels for 3%

profile of v2, /device:TPU:0, one launch (start us, length us, event | category | flops | bytes accessed | tf_op | source)
XLA Modules:
  0.0 888.2 jit_solution(14797146689344081052)
XLA Ops:
  11.5 7.3 all-to-all-start
  34.8 15.0 %collective-permute-done.3 = bf16[128,2048]{1,0:T(8,128)(2,1)S(1)} collective-permute-done((bf16[128,2048]{1,0:T(8,128)(2,1)S(1)}, bf16[128,2048]{1,0:T(8,128)(2,1)S(1)}, u32[]{:S(2)}, u32[]{:S(2)}) %collective-permute-start.3) | collective-permute-done | bytes 524320 | tf_op jit(solution)/shard_map/ppermute | solution.py:30
  49.9 14.3 %collective-permute-start.4 = (bf16[128,2048]{1,0:T(8,128)(2,1)S(1)}, bf16[128,2048]{1,0:T(8,128)(2,1)}, u32[]{:S(2)}, u32[]{:S(2)}) collective-permute-start(bf16[128,2048]{1,0:T(8,128)(2,1)S(1)} %collective-permute-done.3), channel_id=1, source_target_pairs={{0,2},{1,3},{2,0},{3,1},{4,6},{5,7},{6,4},{7,5},{8,10},{9,11},{10,... | collective-permute-start | bytes 1572872 | tf_op jit(solution)/shard_map/ppermute | solution.py:30
  70.6 17.2 %collective-permute-done.2 = bf16[128,2048]{1,0:T(8,128)(2,1)} collective-permute-done((bf16[128,2048]{1,0:T(8,128)(2,1)S(1)}, bf16[128,2048]{1,0:T(8,128)(2,1)}, u32[]{:S(2)}, u32[]{:S(2)}) %collective-permute-start.2) | collective-permute-done | bytes 524320 | tf_op jit(solution)/shard_map/ppermute | solution.py:30
  93.9 7.6 collective-permute-done.6
  124.2 29.7 %collective-permute-done.10 = f32[2,1024]{1,0:T(2,128)S(1)} collective-permute-done((f32[2,1024]{1,0:T(2,128)S(1)}, f32[2,1024]{1,0:T(2,128)S(1)}, u32[]{:S(2)}, u32[]{:S(2)}) %collective-permute-start.10) | collective-permute-done | bytes 8224 | tf_op jit(solution)/shard_map/ppermute | solution.py:30
  160.1 8.4 collective-permute-done.11
  200.2 17.5 %collective-permute-done.12 = bf16[3,128,1536]{2,1,0:T(8,128)(2,1)S(1)} collective-permute-done((bf16[3,128,1536]{2,1,0:T(8,128)(2,1)S(1)}, bf16[3,128,1536]{2,1,0:T(8,128)(2,1)S(1)}, u32[]{:S(2)}, u32[]{:S(2)}) %collective-permute-start.12) | collective-permute-done | bytes 1179680 | tf_op jit(solution)/shard_map/ppermute | solution.py:30
  232.2 32.2 %collective-permute-done.14 = bf16[128,1536]{1,0:T(8,128)(2,1)S(1)} collective-permute-done((bf16[128,1536]{1,0:T(8,128)(2,1)S(1)}, bf16[128,1536]{1,0:T(8,128)(2,1)S(1)}, u32[]{:S(2)}, u32[]{:S(2)}) %collective-permute-start.14) | collective-permute-done | bytes 393248 | tf_op jit(solution)/shard_map/ppermute | solution.py:30
  278.4 7.5 collective-permute-done.20
  288.4 10.8 %collective-permute-done.21 = bf16[128,2048]{1,0:T(8,128)(2,1)} collective-permute-done((bf16[128,2048]{1,0:T(8,128)(2,1)S(1)}, bf16[128,2048]{1,0:T(8,128)(2,1)}, u32[]{:S(2)}, u32[]{:S(2)}) %collective-permute-start.21) | collective-permute-done | bytes 524320 | tf_op jit(solution)/shard_map/ppermute | solution.py:30
  319.4 7.5 multiply_convert_fusion.4
  351.6 14.6 %collective-permute-done.27 = bf16[3,128,1536]{2,1,0:T(8,128)(2,1)S(1)} collective-permute-done((bf16[3,128,1536]{2,1,0:T(8,128)(2,1)S(1)}, bf16[3,128,1536]{2,1,0:T(8,128)(2,1)S(1)}, u32[]{:S(2)}, u32[]{:S(2)}) %collective-permute-start.27) | collective-permute-done | bytes 1179680 | tf_op jit(solution)/shard_map/ppermute | solution.py:30
  371.6 7.3 collective-permute-done.30
  378.9 18.2 %collective-permute-done.29 = bf16[128,1536]{1,0:T(8,128)(2,1)S(1)} collective-permute-done((bf16[128,1536]{1,0:T(8,128)(2,1)S(1)}, bf16[128,1536]{1,0:T(8,128)(2,1)S(1)}, u32[]{:S(2)}, u32[]{:S(2)}) %collective-permute-start.29) | collective-permute-done | bytes 393248 | tf_op jit(solution)/shard_map/ppermute | solution.py:30
  401.4 16.4 %collective-permute-start.35 = (bf16[128,2048]{1,0:T(8,128)(2,1)S(1)}, bf16[128,2048]{1,0:T(8,128)(2,1)S(1)}, u32[]{:S(2)}, u32[]{:S(2)}) collective-permute-start(bf16[128,2048]{1,0:T(8,128)(2,1)S(1)} %get-tuple-element.145), channel_id=1, source_target_pairs={{0,2},{1,3},{2,0},{3,1},{4,6},{5,7},{6,4},{7,5},{8,10},{9,11},{10,... | collective-permute-start | bytes 1572872 | tf_op jit(solution)/shard_map/ppermute | solution.py:30
  418.1 11.2 %collective-permute-start.37 = (bf16[128,2048]{1,0:T(8,128)(2,1)S(1)}, bf16[128,2048]{1,0:T(8,128)(2,1)S(1)}, u32[]{:S(2)}, u32[]{:S(2)}) collective-permute-start(bf16[128,2048]{1,0:T(8,128)(2,1)S(1)} %collective-permute-done.36), channel_id=1, source_target_pairs={{0,2},{1,3},{2,0},{3,1},{4,6},{5,7},{6,4},{7,5},{8,10},{9,11},{10,... | collective-permute-start | bytes 1572872 | tf_op jit(solution)/shard_map/ppermute | solution.py:30
  431.3 7.4 collective-permute-done.37
  484.0 14.8 %collective-permute-done.42 = bf16[3,128,1536]{2,1,0:T(8,128)(2,1)} collective-permute-done((bf16[3,128,1536]{2,1,0:T(8,128)(2,1)}, bf16[3,128,1536]{2,1,0:T(8,128)(2,1)}, u32[]{:S(2)}, u32[]{:S(2)}) %collective-permute-start.42) | collective-permute-done | bytes 1179680 | tf_op jit(solution)/shard_map/ppermute | solution.py:30
  513.2 19.5 %collective-permute-done.44 = bf16[128,1536]{1,0:T(8,128)(2,1)S(1)} collective-permute-done((bf16[128,1536]{1,0:T(8,128)(2,1)S(1)}, bf16[128,1536]{1,0:T(8,128)(2,1)S(1)}, u32[]{:S(2)}, u32[]{:S(2)}) %collective-permute-start.44) | collective-permute-done | bytes 393248 | tf_op jit(solution)/shard_map/ppermute | solution.py:30
  565.6 9.2 %collective-permute-done.53 = bf16[128,2048]{1,0:T(8,128)(2,1)S(1)} collective-permute-done((bf16[128,2048]{1,0:T(8,128)(2,1)S(1)}, bf16[128,2048]{1,0:T(8,128)(2,1)S(1)}, u32[]{:S(2)}, u32[]{:S(2)}) %collective-permute-start.53) | collective-permute-done | bytes 524320 | tf_op jit(solution)/shard_map/ppermute | solution.py:30
  592.4 14.5 %collective-permute-done.52 = bf16[128,2048]{1,0:T(8,128)(2,1)S(1)} collective-permute-done((bf16[128,2048]{1,0:T(8,128)(2,1)S(1)}, bf16[128,2048]{1,0:T(8,128)(2,1)S(1)}, u32[]{:S(2)}, u32[]{:S(2)}) %collective-permute-start.52) | collective-permute-done | bytes 524320 | tf_op jit(solution)/shard_map/ppermute | solution.py:30
  637.2 8.9 %all-to-all-done.3 = bf16[8,256,256]{2,1,0:T(8,128)(2,1)} async-done(((bf16[8,256,256]{2,1,0:T(8,128)(2,1)}), bf16[8,256,256]{2,1,0:T(8,128)(2,1)}, u32[]{:S(2)}, u32[]{:S(2)}) %all-to-all-start.3) | async-done | bytes 1048608 | tf_op jit(solution)/shard_map/all_to_all | solution.py:72
  671.8 18.2 %collective-permute-done.59 = f32[48,128]{1,0:T(8,128)S(1)} collective-permute-done((f32[48,128]{1,0:T(8,128)S(1)}, f32[48,128]{1,0:T(8,128)S(1)}, u32[]{:S(2)}, u32[]{:S(2)}) %collective-permute-start.59) | collective-permute-done | bytes 24608 | tf_op jit(solution)/shard_map/ppermute | solution.py:30
  726.2 17.7 %collective-permute-done.60 = bf16[3,128,1536]{2,1,0:T(8,128)(2,1)} collective-permute-done((bf16[3,128,1536]{2,1,0:T(8,128)(2,1)}, bf16[3,128,1536]{2,1,0:T(8,128)(2,1)}, u32[]{:S(2)}, u32[]{:S(2)}) %collective-permute-start.60) | collective-permute-done | bytes 1179680 | tf_op jit(solution)/shard_map/ppermute | solution.py:30
  759.2 28.1 %collective-permute-done.62 = bf16[128,1536]{1,0:T(8,128)(2,1)S(1)} collective-permute-done((bf16[128,1536]{1,0:T(8,128)(2,1)S(1)}, bf16[128,1536]{1,0:T(8,128)(2,1)S(1)}, u32[]{:S(2)}, u32[]{:S(2)}) %collective-permute-start.62) | collective-permute-done | bytes 393248 | tf_op jit(solution)/shard_map/ppermute | solution.py:30
  793.9 9.2 %all-to-all-start.4 = ((bf16[8,64,768]{2,1,0:T(8,128)(2,1)}), bf16[8,64,768]{2,1,0:T(8,128)(2,1)}, u32[]{:S(2)}, u32[]{:S(2)}) async-start(bf16[8,64,768]{2,1,0:T(8,128)(2,1)} %slice.779), calls=%async_computation.5 | async-start | bytes 1572864 | tf_op jit(solution)/shard_map/all_to_all | solution.py:72
  804.2 18.5 %all-to-all-done.4 = bf16[8,64,768]{2,1,0:T(8,128)(2,1)} async-done(((bf16[8,64,768]{2,1,0:T(8,128)(2,1)}), bf16[8,64,768]{2,1,0:T(8,128)(2,1)}, u32[]{:S(2)}, u32[]{:S(2)}) %all-to-all-start.4) | async-done | bytes 786464 | tf_op jit(solution)/shard_map/all_to_all | solution.py:72
  824.0 7.8 shard_map.229
  833.6 7.3 shard_map.230
  840.9 14.4 %collective-permute-done.70 = bf16[8,64,1024]{2,1,0:T(8,128)(2,1)} collective-permute-done((bf16[8,64,1024]{2,1,0:T(8,128)(2,1)S(1)}, bf16[8,64,1024]{2,1,0:T(8,128)(2,1)}, u32[]{:S(2)}, u32[]{:S(2)}) %collective-permute-start.70) | collective-permute-done | bytes 1048608 | tf_op jit(solution)/shard_map/ppermute | solution.py:30
  866.1 7.4 shard_map.232
  (547 shorter events, 426.6 us)
Async XLA Ops:
  11.5 56.6 %all-to-all-start = ((bf16[8,72,768]{2,1,0:T(8,128)(2,1)}), bf16[8,72,768]{2,1,0:T(8,128)(2,1)S(1)}, u32[]{:S(2)}, u32[]{:S(2)}) async-start(bf16[8,72,768]{2,1,0:T(8,128)(2,1)} %copy.61), calls=%async_computation | async-start | bytes 1769472 | tf_op jit(solution)/shard_map/all_to_all | solution.py:72
  22.6 42.9 %collective-permute-start.1 = (bf16[128,2048]{1,0:T(8,128)(2,1)S(1)}, bf16[128,2048]{1,0:T(8,128)(2,1)S(1)}, u32[]{:S(2)}, u32[]{:S(2)}) collective-permute-start(bf16[128,2048]{1,0:T(8,128)(2,1)S(1)} %bitcast.369), channel_id=1, source_target_pairs={{0,2},{1,3},{2,0},{3,1},{4,6},{5,7},{6,4},{7,5},{8,10},{9,11},{10,... | collective-permute-start | bytes 1572872 | tf_op jit(solution)/shard_map/ppermute | solution.py:30
  22.6 43.6 %collective-permute-start = (bf16[128,2048]{1,0:T(8,128)(2,1)S(1)}, bf16[128,2048]{1,0:T(8,128)(2,1)}, u32[]{:S(2)}, u32[]{:S(2)}) collective-permute-start(bf16[128,2048]{1,0:T(8,128)(2,1)S(1)} %bitcast.370), channel_id=1, source_target_pairs={{0,1},{1,0},{2,3},{3,2},{4,5},{5,4},{6,7},{7,6},{8,9},{9,8},{10,11... | collective-permute-start | bytes 1572872 | tf_op jit(solution)/shard_map/ppermute | solution.py:30
  49.9 39.9 %collective-permute-start.4 = (bf16[128,2048]{1,0:T(8,128)(2,1)S(1)}, bf16[128,2048]{1,0:T(8,128)(2,1)}, u32[]{:S(2)}, u32[]{:S(2)}) collective-permute-start(bf16[128,2048]{1,0:T(8,128)(2,1)S(1)} %collective-permute-done.3), channel_id=1, source_target_pairs={{0,2},{1,3},{2,0},{3,1},{4,6},{5,7},{6,4},{7,5},{8,10},{9,11},{10,... | collective-permute-start | bytes 1572872 | tf_op jit(solution)/shard_map/ppermute | solution.py:30
  64.2 38.9 %collective-permute-start.7 = (bf16[128,2048]{1,0:T(8,128)(2,1)S(1)}, bf16[128,2048]{1,0:T(8,128)(2,1)}, u32[]{:S(2)}, u32[]{:S(2)}) collective-permute-start(bf16[128,2048]{1,0:T(8,128)(2,1)S(1)} %collective-permute-done.3), channel_id=1, source_target_pairs={{0,1},{1,0},{2,3},{3,2},{4,5},{5,4},{6,7},{7,6},{8,9},{9,8},{10,11... | collective-permute-start | bytes 1572872 | tf_op jit(solution)/shard_map/ppermute | solution.py:30
  117.0 62.7 %all-to-all-start.1 = ((bf16[8,256,512]{2,1,0:T(8,128)(2,1)}), bf16[8,256,512]{2,1,0:T(8,128)(2,1)S(1)}, u32[]{:S(2)}, u32[]{:S(2)}) async-start(bf16[8,256,512]{2,1,0:T(8,128)(2,1)} %pad_maximum_fusion.1), calls=%async_computation.1 | async-start | bytes 4194304 | tf_op jit(solution)/shard_map/all_to_all | solution.py:72
  121.9 187.7 %all-gather.10.cloned.1.call-start = ((), (), s32[]{:S(2)}) async-start(), calls=%async_computation.10 | async-start | bytes 5242880 | tf_op jit(solution)/shard_map/all_gather | solution.py:288
  181.3 138.1 %all-gather.12.cloned.1.call-start = ((), (), s32[]{:S(2)}) async-start(), calls=%async_computation.11 | async-start | bytes 5242880 | tf_op jit(solution)/shard_map/all_gather | solution.py:288
  185.0 32.7 %collective-permute-start.12 = (bf16[3,128,1536]{2,1,0:T(8,128)(2,1)S(1)}, bf16[3,128,1536]{2,1,0:T(8,128)(2,1)S(1)}, u32[]{:S(2)}, u32[]{:S(2)}) collective-permute-start(bf16[3,128,1536]{2,1,0:T(8,128)(2,1)S(1)} %pad_maximum_fusion.7), channel_id=1, source_target_pairs={{0,1},{1,0},{2,3},{3,2},{4,5},{5,4},{6,7},{7,6},{8,9},{9,8},{10,11... | collective-permute-start | bytes 3538952 | tf_op jit(solution)/shard_map/ppermute | solution.py:30
  188.8 33.5 %collective-permute-start.18 = (bf16[2,128,512]{2,1,0:T(8,128)(2,1)}, bf16[2,128,512]{2,1,0:T(8,128)(2,1)}, u32[]{:S(2)}, u32[]{:S(2)}) collective-permute-start(bf16[2,128,512]{2,1,0:T(8,128)(2,1)} %pad_maximum_fusion.27), channel_id=1, source_target_pairs={{0,2},{1,3},{2,0},{3,1},{4,6},{5,7},{6,4},{7,5},{8,10},{9,11},{10,... | collective-permute-start | bytes 786440 | tf_op jit(solution)/shard_map/ppermute | solution.py:30
  189.5 34.6 %collective-permute-start.17 = (bf16[2,128,512]{2,1,0:T(8,128)(2,1)}, bf16[2,128,512]{2,1,0:T(8,128)(2,1)}, u32[]{:S(2)}, u32[]{:S(2)}) collective-permute-start(bf16[2,128,512]{2,1,0:T(8,128)(2,1)} %pad_maximum_fusion.26), channel_id=1, source_target_pairs={{0,4},{1,5},{2,6},{3,7},{4,0},{5,1},{6,2},{7,3},{8,12},{9,13},{10,... | collective-permute-start | bytes 786440 | tf_op jit(solution)/shard_map/ppermute | solution.py:30
  194.7 71.2 %all-to-all-start.2 = ((bf16[8,256,256]{2,1,0:T(8,128)(2,1)}), bf16[8,256,256]{2,1,0:T(8,128)(2,1)}, u32[]{:S(2)}, u32[]{:S(2)}) async-start(bf16[8,256,256]{2,1,0:T(8,128)(2,1)} %get-tuple-element.46), calls=%async_computation.2 | async-start | bytes 2097152 | tf_op jit(solution)/shard_map/all_to_all | solution.py:72
  198.9 138.0 %all-gather.14.cloned.1.call-start = ((), (), s32[]{:S(2)}) async-start(), calls=%async_computation.12 | async-start | bytes 5242880 | tf_op jit(solution)/shard_map/all_gather | solution.py:288
  219.7 44.6 %collective-permute-start.14 = (bf16[128,1536]{1,0:T(8,128)(2,1)S(1)}, bf16[128,1536]{1,0:T(8,128)(2,1)S(1)}, u32[]{:S(2)}, u32[]{:S(2)}) collective-permute-start(bf16[128,1536]{1,0:T(8,128)(2,1)S(1)} %get-tuple-element.88), channel_id=1, source_target_pairs={{0,4},{1,5},{2,6},{3,7},{4,0},{5,1},{6,2},{7,3},{8,12},{9,13},{10,... | collective-permute-start | bytes 1179656 | tf_op jit(solution)/shard_map/ppermute | solution.py:30
  222.2 42.1 %collective-permute-start.13 = (bf16[128,1536]{1,0:T(8,128)(2,1)S(1)}, bf16[128,1536]{1,0:T(8,128)(2,1)S(1)}, u32[]{:S(2)}, u32[]{:S(2)}) collective-permute-start(bf16[128,1536]{1,0:T(8,128)(2,1)S(1)} %get-tuple-element.86), channel_id=1, source_target_pairs={{0,6},{1,7},{2,4},{3,5},{4,2},{5,3},{6,0},{7,1},{8,14},{9,15},{10,... | collective-permute-start | bytes 1179656 | tf_op jit(solution)/shard_map/ppermute | solution.py:30
  225.8 39.8 %collective-permute-start.19 = (bf16[128,2048]{1,0:T(8,128)(2,1)S(1)}, bf16[128,2048]{1,0:T(8,128)(2,1)S(1)}, u32[]{:S(2)}, u32[]{:S(2)}) collective-permute-start(bf16[128,2048]{1,0:T(8,128)(2,1)S(1)} %pad_maximum_fusion.19), channel_id=1, source_target_pairs={{0,1},{1,0},{2,3},{3,2},{4,5},{5,4},{6,7},{7,6},{8,9},{9,8},{10,11... | collective-permute-start | bytes 1572872 | tf_op jit(solution)/shard_map/ppermute | solution.py:30
  265.9 352.0 %reduce-scatter.4.cloned.1.call-start = ((), (), s32[]{:S(2)}) async-start(), calls=%async_computation.13 | async-start | bytes 5242880 | tf_op jit(solution)/shard_map/reduce_scatter | solution.py:343
  429.2 33.5 %collective-permute-start.41 = (bf16[128,2048]{1,0:T(8,128)(2,1)S(1)}, bf16[128,2048]{1,0:T(8,128)(2,1)S(1)}, u32[]{:S(2)}, u32[]{:S(2)}) collective-permute-start(bf16[128,2048]{1,0:T(8,128)(2,1)S(1)} %collective-permute-done.36), channel_id=1, source_target_pairs={{0,1},{1,0},{2,3},{3,2},{4,5},{5,4},{6,7},{7,6},{8,9},{9,8},{10,11... | collective-permute-start | bytes 1572872 | tf_op jit(solution)/shard_map/ppermute | solution.py:30
  538.1 122.1 %reduce-scatter.6.cloned.1.call-start = ((), (), s32[]{:S(2)}) async-start(), calls=%async_computation.14 | async-start | bytes 5242880 | tf_op jit(solution)/shard_map/reduce_scatter | solution.py:343
  548.1 173.7 %reduce-scatter.8.cloned.1.call-start = ((), (), s32[]{:S(2)}) async-start(), calls=%async_computation.15 | async-start | bytes 5242880 | tf_op jit(solution)/shard_map/reduce_scatter | solution.py:343
  580.8 36.3 %collective-permute-start.56 = (bf16[128,2048]{1,0:T(8,128)(2,1)S(1)}, bf16[128,2048]{1,0:T(8,128)(2,1)S(1)}, u32[]{:S(2)}, u32[]{:S(2)}) collective-permute-start(bf16[128,2048]{1,0:T(8,128)(2,1)S(1)} %collective-permute-done.53), channel_id=1, source_target_pairs={{0,1},{1,0},{2,3},{3,2},{4,5},{5,4},{6,7},{7,6},{8,9},{9,8},{10,11... | collective-permute-start | bytes 1572872 | tf_op jit(solution)/shard_map/ppermute | solution.py:30
  622.2 201.7 %all-gather.16.cloned.1.call-start = ((), (), s32[]{:S(2)}) async-start(), calls=%async_computation.16 | async-start | bytes 5242880 | tf_op jit(solution)/shard_map/all_gather | solution.py:349
  660.1 37.6 %all-to-all-start.5 = ((bf16[8,256,256]{2,1,0:T(8,128)(2,1)}), bf16[8,256,256]{2,1,0:T(8,128)(2,1)}, u32[]{:S(2)}, u32[]{:S(2)}) async-start(bf16[8,256,256]{2,1,0:T(8,128)(2,1)} %bitcast.392), calls=%async_computation.7 | async-start | bytes 2097152 | tf_op jit(solution)/shard_map/all_to_all | solution.py:72
  664.4 169.2 %all-gather.18.cloned.1.call-start = ((), (), s32[]{:S(2)}) async-start(), calls=%async_computation.17 | async-start | bytes 5242880 | tf_op jit(solution)/shard_map/all_gather | solution.py:349
  709.2 40.4 %collective-permute-start.66 = (bf16[2,128,512]{2,1,0:T(8,128)(2,1)}, bf16[2,128,512]{2,1,0:T(8,128)(2,1)}, u32[]{:S(2)}, u32[]{:S(2)}) collective-permute-start(bf16[2,128,512]{2,1,0:T(8,128)(2,1)} %pad_maximum_fusion.36), channel_id=1, source_target_pairs={{0,2},{1,3},{2,0},{3,1},{4,6},{5,7},{6,4},{7,5},{8,10},{9,11},{10,... | collective-permute-start | bytes 786440 | tf_op jit(solution)/shard_map/ppermute | solution.py:30
  710.4 33.5 %collective-permute-start.60 = (bf16[3,128,1536]{2,1,0:T(8,128)(2,1)}, bf16[3,128,1536]{2,1,0:T(8,128)(2,1)}, u32[]{:S(2)}, u32[]{:S(2)}) collective-permute-start(bf16[3,128,1536]{2,1,0:T(8,128)(2,1)} %pad_maximum_fusion.10), channel_id=1, source_target_pairs={{0,1},{1,0},{2,3},{3,2},{4,5},{5,4},{6,7},{7,6},{8,9},{9,8},{10,11... | collective-permute-start | bytes 3538952 | tf_op jit(solution)/shard_map/ppermute | solution.py:30
  712.3 37.3 %collective-permute-start.65 = (bf16[2,128,512]{2,1,0:T(8,128)(2,1)}, bf16[2,128,512]{2,1,0:T(8,128)(2,1)}, u32[]{:S(2)}, u32[]{:S(2)}) collective-permute-start(bf16[2,128,512]{2,1,0:T(8,128)(2,1)} %pad_maximum_fusion.35), channel_id=1, source_target_pairs={{0,4},{1,5},{2,6},{3,7},{4,0},{5,1},{6,2},{7,3},{8,12},{9,13},{10,... | collective-permute-start | bytes 786440 | tf_op jit(solution)/shard_map/ppermute | solution.py:30
  717.2 40.6 %collective-permute-start.68 = (bf16[8,64,1024]{2,1,0:T(8,128)(2,1)}, bf16[8,64,1024]{2,1,0:T(8,128)(2,1)}, u32[]{:S(2)}, u32[]{:S(2)}) collective-permute-start(bf16[8,64,1024]{2,1,0:T(8,128)(2,1)} %fusion.14), channel_id=1, source_target_pairs={{0,16},{8,24},{16,0},{24,8},{1,17},{9,25},{17,1},{25,9},{2,18},{10... | collective-permute-start | bytes 3145736 | tf_op jit(solution)/shard_map/ppermute | solution.py:30
  721.8 67.9 %all-to-all-start.6 = ((bf16[8,256,256]{2,1,0:T(8,128)(2,1)}), bf16[8,256,256]{2,1,0:T(8,128)(2,1)}, u32[]{:S(2)}, u32[]{:S(2)}) async-start(bf16[8,256,256]{2,1,0:T(8,128)(2,1)} %bitcast.391), calls=%async_computation.9 | async-start | bytes 2097152 | tf_op jit(solution)/shard_map/all_to_all | solution.py:72
  726.1 140.0 %all-gather.20.cloned.1.call-start = ((), (), s32[]{:S(2)}) async-start(), calls=%async_computation.18 | async-start | bytes 5242880 | tf_op jit(solution)/shard_map/all_gather | solution.py:349
  749.6 37.7 %collective-permute-start.62 = (bf16[128,1536]{1,0:T(8,128)(2,1)S(1)}, bf16[128,1536]{1,0:T(8,128)(2,1)S(1)}, u32[]{:S(2)}, u32[]{:S(2)}) collective-permute-start(bf16[128,1536]{1,0:T(8,128)(2,1)S(1)} %get-tuple-element.85), channel_id=1, source_target_pairs={{0,4},{1,5},{2,6},{3,7},{4,0},{5,1},{6,2},{7,3},{8,12},{9,13},{10,... | collective-permute-start | bytes 1179656 | tf_op jit(solution)/shard_map/ppermute | solution.py:30
  749.6 37.7 %collective-permute-start.61 = (bf16[128,1536]{1,0:T(8,128)(2,1)S(1)}, bf16[128,1536]{1,0:T(8,128)(2,1)S(1)}, u32[]{:S(2)}, u32[]{:S(2)}) collective-permute-start(bf16[128,1536]{1,0:T(8,128)(2,1)S(1)} %get-tuple-element.83), channel_id=1, source_target_pairs={{0,6},{1,7},{2,4},{3,5},{4,2},{5,3},{6,0},{7,1},{8,14},{9,15},{10,... | collective-permute-start | bytes 1179656 | tf_op jit(solution)/shard_map/ppermute | solution.py:30
  (154 other events, 2551.0 us)
Sparse Core Ops, SparseCore 0:
  181.4 33.7 all-gather.9
  217.4 35.0 all-gather.11
  266.0 40.4 all-gather.13
  538.2 47.4 reduce-scatter.3
  588.2 44.4 reduce-scatter.5
  635.1 44.4 reduce-scatter.7
  681.3 34.4 all-gather.15
  717.4 48.1 all-gather.17
  789.8 39.2 all-gather.19

commit v3 on v2

--- a/solution.py
+++ b/solution.py
@@ -53,19 +53,22 @@
 
 
 def scatter_sum(pieces, *meanwhile):
-    steps = [*range(len(pieces) - 2, 0, -2)]
-    cut = pieces[0].shape[1] * 3 // 4
-    left = [p[:, :cut] for p in pieces]
-    right = [p[:, cut:] for p in pieces]
-    odd = shuffle(jnp.stack([left[k + 1].astype(BF) for k in steps]), "grp", 1)
-    far = [shuffle(jnp.stack([right[k].astype(BF), right[k + 1].astype(BF)]), "grp", k) for k in steps]
-    paired = [left[k].astype(F32) + odd[i].astype(F32) for i, k in enumerate(steps)]
-    moved = [shuffle(p.astype(BF), "grp", k) for p, k in zip(paired, steps)]
-    both = [right[i].astype(F32) + sum(f[i].astype(F32) for f in far) for i in (0, 1)]
-    last = jnp.concatenate([left[1].astype(BF), both[1].astype(BF)], axis=1)
-    last = shuffle(tie(last, *meanwhile) if meanwhile else last, "grp", 1)
-    total_left = left[0].astype(F32) + sum(m.astype(F32) for m in moved)
-    return jnp.concatenate([total_left, both[0]], axis=1) + last.astype(F32), last
+    count = len(pieces)
+    top = count - 2
+    odd = {k: shuffle(pieces[k + 1].astype(BF), "grp", 1) for k in range(count // 2, top, 2)}
+    odd |= {k: shuffle(pieces[k + 1].astype(BF), "grp", 1) for k in (top, *range(2, count // 2, 2), 0)}
+    paired = {k: pieces[k].astype(F32) + odd[k].astype(F32) for k in range(count // 2, top, 2)}
+    passed = [shuffle(v.astype(BF), "grp", k ^ top) for k, v in paired.items()]
+    held = tie(odd[top], *passed) if passed else odd[top]
+    farthest = pieces[top].astype(F32) + held.astype(F32) + sum(v.astype(F32) for v in passed)
+    farthest = shuffle(farthest.astype(BF), "grp", top)
+    total = pieces[0].astype(F32)
+    last = []
+    for k in range(2, count // 2, 2):
+        held = tie(odd[k], *passed, *meanwhile)
+        last.append(shuffle((pieces[k].astype(F32) + held.astype(F32)).astype(BF), "grp", k))
+        total += last[-1].astype(F32)
+    return total + farthest.astype(F32) + odd[0].astype(F32), last
 
 
 def to_columns(blocks):
@@ -270,7 +273,7 @@
     ga, gm = gain_all[:, 0].reshape(width), gain_all[:, 1].reshape(width)
     mine = landed[:, :sub]
     far = rep_far(mine)
-    x_pieces = gather_pieces(x, far)
+    x_pieces = gather_pieces(x)
     near = rep_near(jnp.stack([mine, far]))
     w_qkv = jnp.zeros((groups, reps, sub, 3 * own), BF)
     for j, piece in enumerate([mine, near[0], far, near[1]]):
@@ -299,48 +302,50 @@
     queries = turn(q_proj * q_inv * gq, cosine, sine).astype(BF)
     keys = turn(k_proj * k_inv * gk, cosine, sine).astype(BF)
     attn, lse = attend(queries, keys, values)
-    gu_landed = tie(to_columns(tie(jnp.concatenate(sends[:2], axis=2), x_all)), attn)
+    gu_landed = tie(to_columns(tie(jnp.concatenate(sends[:2], axis=2), x_pieces[groups - 1])), squares)
     w_gate, w_up = spread(gu_landed[..., :part]), spread(gu_landed[..., part:])
-    a_part = dot(attn, o_weight)
+    a_part = dot(attn, o_weight).astype(BF)
     a_proj, _ = scatter_sum(
         [lax.dynamic_slice(a_part, (at[k] * count, zero), (count, width)) for k in range(groups)]
     )
-    w_down = spread(tie(to_columns(tie(sends[2], attn)), a_proj))
+    w_down = spread(tie(to_columns(tie(sends[2], gu_landed)), attn))
     middle = x.astype(F32) + rms(a_proj, ga)
     middle_bf = middle.astype(BF)
 
     def halves(pieces):
         return jnp.concatenate(pieces[0::2]), jnp.concatenate(pieces[1::2])
 
-    def whole(even, odd):
-        even, odd = (v.reshape(groups // 2, count, width) for v in (even, odd))
-        return [(even, odd)[k % 2][k // 2] for k in range(groups)]
+    def whole(*parts):
+        parts = [v.reshape(-1, count, width) for v in parts]
+        return [parts[k % len(parts)][k // len(parts)] for k in range(groups)]
 
     h_halves = halves(gather_pieces(middle_bf, w_gate))
     gates = [dot(h, w_gate) for h in h_halves]
     uppers = [dot(h, w_up) for h in h_halves]
     mixed = [swiglu(g, u).astype(BF) for g, u in zip(gates, uppers)]
-    y_proj, _ = scatter_sum(whole(*[dot_right_t(m, w_down) for m in mixed]))
+    y_proj, _ = scatter_sum(whole(*[dot_right_t(m, w_down).astype(BF) for m in mixed]))
     outputs = (middle + rms(y_proj, gm)).astype(BF)
 
     grad_out = cotangent[0].astype(F32)
     _, pull = jax.vjp(rms, y_proj, gm)
     dy, d_mlp_gain = pull(grad_out)
-    dy_halves = halves(gather_pieces(dy.astype(BF)))
+    dy_pieces = gather_pieces(dy.astype(BF))
+    dy_halves = halves([tie(dy_pieces[0], dy_pieces[groups - 1]), *dy_pieces[1:]])
     d_gates, d_uppers, m_halves = [], [], []
     for g, u, d in zip(gates, uppers, dy_halves):
         _, pull = jax.vjp(swiglu, g, u)
         d_gate, d_upper = (v.astype(BF) for v in pull(dot(d, w_down)))
         d_gates.append(d_gate)
         d_uppers.append(d_upper)
-        m_halves.append(dot_right_t(d_gate, w_gate) + dot_right_t(d_upper, w_up))
+        m_halves.append((dot_right_t(d_gate, w_gate) + dot_right_t(d_upper, w_up)).astype(BF))
     d_middle, _ = scatter_sum(whole(*m_halves))
     d_middle = grad_out + d_middle
 
-    def weight_sum(left, right, later):
-        both = [dot_left_t(a, b) for a, b in zip(left, right)]
-        both = tie((both[0] + both[1]).astype(BF), later)
-        return lax.psum_scatter(both, "rep", scatter_dimension=1, tiled=True)
+    def weight_part(left, right):
+        return sum(dot_left_t(a, b) for a, b in zip(left, right)).astype(BF)
+
+    def over_rep(part_sum):
+        return lax.psum_scatter(part_sum, "rep", scatter_dimension=1, tiled=True)
 
     def to_place(sums, before, after):
         return tie(to_columns(tie(sums.reshape(groups, own, part), before)), after)
@@ -348,12 +353,14 @@
     def to_rows(sums, turned):
         return widen(lax.all_gather(lax.optimization_barrier(sums), "rep", axis=0), turned)
 
+    g_down = weight_part(dy_halves, mixed)
+    g_gate, g_up = weight_part(h_halves, d_gates), weight_part(h_halves, d_uppers)
+    sum_down = over_rep(tie(g_down, *m_halves))
+    d_middle = tie(d_middle, sum_down, g_gate, g_up)
     _, pull = jax.vjp(rms, a_proj, ga)
     da, d_attn_gain = pull(d_middle)
     da_bf = da.astype(BF)
-    sum_down = weight_sum(dy_halves, mixed, da_bf)
-    sum_gate = weight_sum(h_halves, d_gates, da_bf)
-    sum_up = weight_sum(h_halves, d_uppers, da_bf)
+    sum_gate, sum_up = over_rep(g_gate), over_rep(g_up)
     da_pieces = gather_pieces(da_bf)
     da_all = jnp.zeros((groups, count, width), BF)
     for k, piece in enumerate(da_pieces):
@@ -361,7 +368,6 @@
     da_all = da_all.reshape(length, width)
     d_attn = dot_right_t(da_all, o_weight).astype(BF)
     dq, dk, dv = attend_back(queries, keys, values, lse, d_attn)
-    down_grad = to_rows(to_place(sum_down, da_all, dq), True)
     dq, dk = turn(dq, cosine, -sine), turn(dk, cosine, -sine)
     q_unit, k_unit = q_proj * q_inv, k_proj * k_inv
     d_q_gain, d_k_gain = jnp.sum(dq * q_unit, axis=0), jnp.sum(dk * k_unit, axis=0)
@@ -379,10 +385,9 @@
         ],
         axis=1,
     )
-    x_part = dot_right_t(d_qkv, w_qkv)
-    gate_grad = to_rows(to_place(sum_gate, along, x_part), False)
-
-    g_qkv = dot_left_t(x_all, d_qkv).astype(BF).reshape(groups, reps, sub, 3 * own)
+    x_part = dot_right_t(d_qkv, w_qkv).astype(BF)
+
+    g_qkv = dot_left_t(tie(x_all, x_part), d_qkv).astype(BF).reshape(groups, reps, sub, 3 * own)
     g_o = dot_left_t(attn, tie(da_all, dq)).astype(BF).reshape(reps, sub, groups, own)
     g_all = jnp.concatenate([g_qkv, jnp.transpose(g_o, (2, 0, 1, 3))], axis=3)
     parts = [
@@ -390,17 +395,20 @@
     ]
     near = near_send(parts)
     far = far_send(parts, near)
-    d_x, _ = scatter_sum(
-        [lax.dynamic_slice(x_part, (at[k] * count, zero), (count, width)) for k in range(groups)], far
-    )
-    up_grad = to_rows(to_place(sum_up, x_part, d_x), False)
+    d_x, last = scatter_sum(
+        [lax.dynamic_slice(x_part, (at[k] * count, zero), (count, width)) for k in range(groups)]
+    )
+    near_place = da_pieces[groups - 4]
+    down_grad = to_rows(to_place(sum_down, near_place, d_attn), True)
+    gate_grad = to_rows(to_place(sum_gate, near_place, x_part), False)
+    up_grad = to_rows(to_place(sum_up, dq, x_part), False)
     sums = rep_total(parts, near, far)
-    rows_of = tie(to_columns(sums[..., : 3 * own]), d_x)
-    d_x = d_middle + tie(d_x, down_grad)
+    rows_of = to_columns(tie(sums[..., : 3 * own], *last))
+    d_x = d_middle + d_x
     mine = jnp.concatenate([rows_of, sums[..., 3 * own :]], axis=2)
-    mine = tie(mine, down_grad)
+    mine = tie(lax.optimization_barrier(mine), gate_grad)
     far = rep_far(mine)
-    here = tie(jnp.stack([mine, far]), gate_grad)
+    here = tie(jnp.stack([mine, far]), down_grad, gate_grad, up_grad)
     q_grad, k_grad, v_grad, o_grad = lay_rows(rep, here, rep_near(here))
 
     post = lax.dynamic_slice(along[2 * length :].reshape(2, width), (zero, me * own), (2, own))
@@ -669,7 +677,7 @@
     rows = P("grp", None)
     seq = P("rep", "grp", None)
     gain = P("grp")
-    whole_heads = HEADS % mesh.shape["grp"] == 0 and mesh.shape["rep"] == 4
+    whole_heads = HEADS % mesh.shape["grp"] == 0 and mesh.shape["grp"] >= 4 and mesh.shape["rep"] == 4
     return jax.shard_map(
         by_heads if whole_heads else by_tokens,
         mesh=mesh,

time: 895 us -> 786 us (0.88)
  starting transfers between devices: 194 us -> 120 us
  waiting for transfers between devices: 409 us -> 353 us
  blocking collectives: 0 us -> 26.8 us
    ppermute x74 -> x70, starting transfers between devices: 154 us -> 90.6 us  [shuffle(): lax.ppermute(value, axis, [(i, i ^ step) for i in range(lax.axis_size(axi...]
    ppermute x74 -> x70, waiting for transfers between devices: 381 us -> 337 us  [shuffle(): lax.ppermute(value, axis, [(i, i ^ step) for i in range(lax.axis_size(axi...]
    all_to_all x0 -> x1, blocking collectives: none -> 26.8 us  [to_columns(): return lax.all_to_all(blocks, 'grp', 0, 0, tiled=True)]
    all_to_all x7 -> x6, waiting for transfers between devices: 27.4 us -> 16 us  [to_columns(): return lax.all_to_all(blocks, 'grp', 0, 0, tiled=True)]
    all_to_all x7 -> x6, starting transfers between devices: 38.4 us -> 27.7 us  [to_columns(): return lax.all_to_all(blocks, 'grp', 0, 0, tiled=True)]
    another operation x26 -> x2, local copies, waits for them, and re-layouts: 10.1 us -> 1.03 us
    unnamed x200 -> x205, local copies, waits for them, and re-layouts: 22.7 us -> 27.3 us
  transfers between devices with their start and end apart: 90 -> 85, of which waited for: 35 -> 47; matrix products, arithmetic and copies ran while one was open for 20% -> 21% of each run, Pallas kernels for 3% -> 4%
where the time goes in v3:
time: 786 us; the launch traced here: 771 us
  waiting for transfers between devices  353 us (45%)
  starting transfers between devices  120 us (15%)
  matrix products  113 us (14%)
  local copies, waits for them, and re-layouts  59.3 us (8%)
  other arithmetic  47.4 us (6%)
  Pallas kernels  35.5 us (5%)
  blocking collectives  26.8 us (3%)
  between operations  16.3 us (2%)
    ppermute x70, waiting for transfers between devices, shuffle(): lax.ppermute(value, axis, [(i, i ^ step) for i in range(lax.axis_size(axi...  337 us
    dot_general x24, matrix products, dot(): lax.dot_general(left, right, (dims, ((), ())), preferred_element_type=kind)  96.3 us
    ppermute x70, starting transfers between devices, shuffle(): lax.ppermute(value, axis, [(i, i ^ step) for i in range(lax.axis_size(axi...  90.6 us
    all_to_all x6, starting transfers between devices, to_columns(): return lax.all_to_all(blocks, 'grp', 0, 0, tiled=True)  27.7 us
    unnamed x205, local copies, waits for them, and re-layouts  27.3 us
    all_to_all x1, blocking collectives, to_columns(): return lax.all_to_all(blocks, 'grp', 0, 0, tiled=True)  26.8 us
    pallas_call x3, Pallas kernels, widen(): pl.pallas_call(widen_turned_kernel if turned else widen_kernel, grid=(cou...  22.4 us
    all_to_all x6, waiting for transfers between devices, to_columns(): return lax.all_to_all(blocks, 'grp', 0, 0, tiled=True)  16 us
  transfers between devices with their start and end apart: 85, of which 47 were waited for; matrix products, arithmetic and copies ran while one was open for 21% of the time, Pallas kernels for 4%

profile of v3, /device:TPU:0, one launch (start us, length us, event | category | flops | bytes accessed | tf_op | source)
XLA Modules:
  0.0 770.9 jit_solution(4640061811127739476)
XLA Ops:
  11.5 7.3 all-to-all-start
  33.8 16.1 %collective-permute-done.3 = bf16[128,2048]{1,0:T(8,128)(2,1)S(1)} collective-permute-done((bf16[128,2048]{1,0:T(8,128)(2,1)S(1)}, bf16[128,2048]{1,0:T(8,128)(2,1)S(1)}, u32[]{:S(2)}, u32[]{:S(2)}) %collective-permute-start.3) | collective-permute-done | bytes 524320 | tf_op jit(solution)/shard_map/ppermute | solution.py:30
  49.9 14.3 %collective-permute-start.4 = (bf16[128,2048]{1,0:T(8,128)(2,1)S(1)}, bf16[128,2048]{1,0:T(8,128)(2,1)}, u32[]{:S(2)}, u32[]{:S(2)}) collective-permute-start(bf16[128,2048]{1,0:T(8,128)(2,1)S(1)} %collective-permute-done.3), channel_id=1, source_target_pairs={{0,2},{1,3},{2,0},{3,1},{4,6},{5,7},{6,4},{7,5},{8,10},{9,11},{10,... | collective-permute-start | bytes 1572872 | tf_op jit(solution)/shard_map/ppermute | solution.py:30
  67.4 11.7 %collective-permute-done.6 = bf16[128,2048]{1,0:T(8,128)(2,1)S(1)} collective-permute-done((bf16[128,2048]{1,0:T(8,128)(2,1)S(1)}, bf16[128,2048]{1,0:T(8,128)(2,1)S(1)}, u32[]{:S(2)}, u32[]{:S(2)}) %collective-permute-start.6) | collective-permute-done | bytes 524320 | tf_op jit(solution)/shard_map/ppermute | solution.py:30
  88.5 12.2 %collective-permute-done.2 = bf16[128,2048]{1,0:T(8,128)(2,1)} collective-permute-done((bf16[128,2048]{1,0:T(8,128)(2,1)}, bf16[128,2048]{1,0:T(8,128)(2,1)}, u32[]{:S(2)}, u32[]{:S(2)}) %collective-permute-start.2) | collective-permute-done | bytes 524320 | tf_op jit(solution)/shard_map/ppermute | solution.py:30
  105.7 10.8 %collective-permute-done.5 = bf16[128,2048]{1,0:T(8,128)(2,1)} collective-permute-done((bf16[128,2048]{1,0:T(8,128)(2,1)}, bf16[128,2048]{1,0:T(8,128)(2,1)}, u32[]{:S(2)}, u32[]{:S(2)}) %collective-permute-start.5) | collective-permute-done | bytes 524320 | tf_op jit(solution)/shard_map/ppermute | solution.py:30
  162.6 14.1 %collective-permute-done.13 = bf16[128,2048]{1,0:T(8,128)(2,1)S(1)} collective-permute-done((bf16[128,2048]{1,0:T(8,128)(2,1)S(1)}, bf16[128,2048]{1,0:T(8,128)(2,1)S(1)}, u32[]{:S(2)}, u32[]{:S(2)}) %collective-permute-start.13) | collective-permute-done | bytes 524320 | tf_op jit(solution)/shard_map/ppermute | solution.py:30
  180.3 12.0 %collective-permute-done.12 = bf16[128,2048]{1,0:T(8,128)(2,1)} collective-permute-done((bf16[128,2048]{1,0:T(8,128)(2,1)}, bf16[128,2048]{1,0:T(8,128)(2,1)}, u32[]{:S(2)}, u32[]{:S(2)}) %collective-permute-start.12) | collective-permute-done | bytes 524320 | tf_op jit(solution)/shard_map/ppermute | solution.py:30
  192.3 10.9 %collective-permute-done.16 = bf16[128,2048]{1,0:T(8,128)(2,1)} collective-permute-done((bf16[128,2048]{1,0:T(8,128)(2,1)}, bf16[128,2048]{1,0:T(8,128)(2,1)}, u32[]{:S(2)}, u32[]{:S(2)}) %collective-permute-start.16) | collective-permute-done | bytes 524320 | tf_op jit(solution)/shard_map/ppermute | solution.py:30
  212.0 6.7 collective-permute-done.17
  219.5 10.4 %collective-permute-done.15 = bf16[128,2048]{1,0:T(8,128)(2,1)} collective-permute-done((bf16[128,2048]{1,0:T(8,128)(2,1)}, bf16[128,2048]{1,0:T(8,128)(2,1)}, u32[]{:S(2)}, u32[]{:S(2)}) %collective-permute-start.15) | collective-permute-done | bytes 524320 | tf_op jit(solution)/shard_map/ppermute | solution.py:30
  234.4 12.2 %collective-permute-done.19 = bf16[128,2048]{1,0:T(8,128)(2,1)S(1)} collective-permute-done((bf16[128,2048]{1,0:T(8,128)(2,1)S(1)}, bf16[128,2048]{1,0:T(8,128)(2,1)S(1)}, u32[]{:S(2)}, u32[]{:S(2)}) %collective-permute-start.19) | collective-permute-done | bytes 524320 | tf_op jit(solution)/shard_map/ppermute | solution.py:30
  268.7 7.6 multiply_convert_fusion.4
  295.2 20.7 %collective-permute-done.27 = bf16[128,2048]{1,0:T(8,128)(2,1)S(1)} collective-permute-done((bf16[128,2048]{1,0:T(8,128)(2,1)S(1)}, bf16[128,2048]{1,0:T(8,128)(2,1)S(1)}, u32[]{:S(2)}, u32[]{:S(2)}) %collective-permute-start.27) | collective-permute-done | bytes 524320 | tf_op jit(solution)/shard_map/ppermute | solution.py:30
  330.4 9.0 %collective-permute-done.32 = bf16[128,2048]{1,0:T(8,128)(2,1)S(1)} collective-permute-done((bf16[128,2048]{1,0:T(8,128)(2,1)S(1)}, bf16[128,2048]{1,0:T(8,128)(2,1)S(1)}, u32[]{:S(2)}, u32[]{:S(2)}) %collective-permute-start.32) | collective-permute-done | bytes 524320 | tf_op jit(solution)/shard_map/ppermute | solution.py:30
  354.5 9.3 %collective-permute-done.33 = bf16[128,2048]{1,0:T(8,128)(2,1)S(1)} collective-permute-done((bf16[128,2048]{1,0:T(8,128)(2,1)S(1)}, bf16[128,2048]{1,0:T(8,128)(2,1)S(1)}, u32[]{:S(2)}, u32[]{:S(2)}) %collective-permute-start.33) | collective-permute-done | bytes 524320 | tf_op jit(solution)/shard_map/ppermute | solution.py:30
  394.9 7.1 multiply_convert_fusion.1
  424.1 11.5 %collective-permute-done.41 = bf16[128,2048]{1,0:T(8,128)(2,1)S(1)} collective-permute-done((bf16[128,2048]{1,0:T(8,128)(2,1)S(1)}, bf16[128,2048]{1,0:T(8,128)(2,1)S(1)}, u32[]{:S(2)}, u32[]{:S(2)}) %collective-permute-start.41) | collective-permute-done | bytes 524320 | tf_op jit(solution)/shard_map/ppermute | solution.py:30
  463.3 11.8 %collective-permute-done.43 = bf16[128,2048]{1,0:T(8,128)(2,1)} collective-permute-done((bf16[128,2048]{1,0:T(8,128)(2,1)S(1)}, bf16[128,2048]{1,0:T(8,128)(2,1)}, u32[]{:S(2)}, u32[]{:S(2)}) %collective-permute-start.43) | collective-permute-done | bytes 524320 | tf_op jit(solution)/shard_map/ppermute | solution.py:30
  487.0 8.6 %collective-permute-done.50 = bf16[128,2048]{1,0:T(8,128)(2,1)S(1)} collective-permute-done((bf16[128,2048]{1,0:T(8,128)(2,1)}, bf16[128,2048]{1,0:T(8,128)(2,1)S(1)}, u32[]{:S(2)}, u32[]{:S(2)}) %collective-permute-start.50) | collective-permute-done | bytes 524320 | tf_op jit(solution)/shard_map/ppermute | solution.py:30
  507.1 8.5 %collective-permute-done.49 = bf16[128,2048]{1,0:T(8,128)(2,1)S(1)} collective-permute-done((bf16[128,2048]{1,0:T(8,128)(2,1)S(1)}, bf16[128,2048]{1,0:T(8,128)(2,1)S(1)}, u32[]{:S(2)}, u32[]{:S(2)}) %collective-permute-start.49) | collective-permute-done | bytes 524320 | tf_op jit(solution)/shard_map/ppermute | solution.py:30
  560.3 16.2 %collective-permute-done.56 = f32[48,128]{1,0:T(8,128)S(1)} collective-permute-done((f32[48,128]{1,0:T(8,128)S(1)}, f32[48,128]{1,0:T(8,128)S(1)}, u32[]{:S(2)}, u32[]{:S(2)}) %collective-permute-start.56) | collective-permute-done | bytes 24608 | tf_op jit(solution)/shard_map/ppermute | solution.py:30
  584.1 26.8 %all_to_all.35 = bf16[8,256,256]{2,1,0:T(8,128)(2,1)} all-to-all(bf16[8,256,256]{2,1,0:T(8,128)(2,1)} %bitcast.247), channel_id=1, replica_groups=mesh['rep'=4,'grp'=8] {'grp'}, dimensions={0} | all-to-all | bytes 2097152 | tf_op jit(solution)/shard_map/all_to_all | solution.py:75
  637.3 11.9 %collective-permute-done.58 = bf16[128,2048]{1,0:T(8,128)(2,1)S(1)} collective-permute-done((bf16[128,2048]{1,0:T(8,128)(2,1)S(1)}, bf16[128,2048]{1,0:T(8,128)(2,1)S(1)}, u32[]{:S(2)}, u32[]{:S(2)}) %collective-permute-start.58) | collective-permute-done | bytes 524320 | tf_op jit(solution)/shard_map/ppermute | solution.py:30
  652.8 7.6 collective-permute-done.57
  660.4 7.4 collective-permute-done.61
  672.0 14.8 %collective-permute-done.65 = bf16[8,64,1024]{2,1,0:T(8,128)(2,1)S(1)} collective-permute-done((bf16[8,64,1024]{2,1,0:T(8,128)(2,1)S(1)}, bf16[8,64,1024]{2,1,0:T(8,128)(2,1)S(1)}, u32[]{:S(2)}, u32[]{:S(2)}) %collective-permute-start.65) | collective-permute-done | bytes 1048608 | tf_op jit(solution)/shard_map/ppermute | solution.py:30
  695.7 12.6 %all-to-all-done.3 = bf16[8,64,768]{2,1,0:T(8,128)(2,1)} async-done(((bf16[8,64,768]{2,1,0:T(8,128)(2,1)}), bf16[8,64,768]{2,1,0:T(8,128)(2,1)}, u32[]{:S(2)}, u32[]{:S(2)}) %all-to-all-start.3) | async-done | bytes 786464 | tf_op jit(solution)/shard_map/all_to_all | solution.py:75
  709.6 7.3 shard_map.229
  717.8 7.8 %shard_map.230 = f32[8192,256]{1,0:T(8,128)} custom-call(bf16[4,8,256,256]{3,2,1,0:T(8,128)(2,1)} %bitcast.223), custom_call_target="tpu_custom_call" | custom-call | bytes 12582912 | tf_op jit(solution)/shard_map/pallas_call | solution.py:173
  725.7 7.3 shard_map.231
  757.0 7.0 shard_map.232
  (498 shorter events, 395.2 us)
Async XLA Ops:
  11.5 69.7 %all-to-all-start = ((bf16[8,72,768]{2,1,0:T(8,128)(2,1)}), bf16[8,72,768]{2,1,0:T(8,128)(2,1)S(1)}, u32[]{:S(2)}, u32[]{:S(2)}) async-start(bf16[8,72,768]{2,1,0:T(8,128)(2,1)} %copy.61), calls=%async_computation | async-start | bytes 1769472 | tf_op jit(solution)/shard_map/all_to_all | solution.py:75
  18.8 31.1 %collective-permute-start.3 = (bf16[128,2048]{1,0:T(8,128)(2,1)S(1)}, bf16[128,2048]{1,0:T(8,128)(2,1)S(1)}, u32[]{:S(2)}, u32[]{:S(2)}) collective-permute-start(bf16[128,2048]{1,0:T(8,128)(2,1)S(1)} %bitcast.219), channel_id=1, source_target_pairs={{0,6},{1,7},{2,4},{3,5},{4,2},{5,3},{6,0},{7,1},{8,14},{9,15},{10,... | collective-permute-start | bytes 1572872 | tf_op jit(solution)/shard_map/ppermute | solution.py:30
  22.6 42.9 %collective-permute-start.1 = (bf16[128,2048]{1,0:T(8,128)(2,1)S(1)}, bf16[128,2048]{1,0:T(8,128)(2,1)}, u32[]{:S(2)}, u32[]{:S(2)}) collective-permute-start(bf16[128,2048]{1,0:T(8,128)(2,1)S(1)} %bitcast.220), channel_id=1, source_target_pairs={{0,2},{1,3},{2,0},{3,1},{4,6},{5,7},{6,4},{7,5},{8,10},{9,11},{10,... | collective-permute-start | bytes 1572872 | tf_op jit(solution)/shard_map/ppermute | solution.py:30
  22.6 43.6 %collective-permute-start = (bf16[128,2048]{1,0:T(8,128)(2,1)S(1)}, bf16[128,2048]{1,0:T(8,128)(2,1)S(1)}, u32[]{:S(2)}, u32[]{:S(2)}) collective-permute-start(bf16[128,2048]{1,0:T(8,128)(2,1)S(1)} %bitcast.221), channel_id=1, source_target_pairs={{0,1},{1,0},{2,3},{3,2},{4,5},{5,4},{6,7},{7,6},{8,9},{9,8},{10,11... | collective-permute-start | bytes 1572872 | tf_op jit(solution)/shard_map/ppermute | solution.py:30
  49.9 29.2 %collective-permute-start.4 = (bf16[128,2048]{1,0:T(8,128)(2,1)S(1)}, bf16[128,2048]{1,0:T(8,128)(2,1)}, u32[]{:S(2)}, u32[]{:S(2)}) collective-permute-start(bf16[128,2048]{1,0:T(8,128)(2,1)S(1)} %collective-permute-done.3), channel_id=1, source_target_pairs={{0,2},{1,3},{2,0},{3,1},{4,6},{5,7},{6,4},{7,5},{8,10},{9,11},{10,... | collective-permute-start | bytes 1572872 | tf_op jit(solution)/shard_map/ppermute | solution.py:30
  65.5 35.2 %collective-permute-start.2 = (bf16[128,2048]{1,0:T(8,128)(2,1)}, bf16[128,2048]{1,0:T(8,128)(2,1)}, u32[]{:S(2)}, u32[]{:S(2)}) collective-permute-start(bf16[128,2048]{1,0:T(8,128)(2,1)} %collective-permute-done.1), channel_id=1, source_target_pairs={{0,1},{1,0},{2,3},{3,2},{4,5},{5,4},{6,7},{7,6},{8,9},{9,8},{10,11... | collective-permute-start | bytes 1572872 | tf_op jit(solution)/shard_map/ppermute | solution.py:30
  79.8 36.7 %collective-permute-start.5 = (bf16[128,2048]{1,0:T(8,128)(2,1)}, bf16[128,2048]{1,0:T(8,128)(2,1)}, u32[]{:S(2)}, u32[]{:S(2)}) collective-permute-start(bf16[128,2048]{1,0:T(8,128)(2,1)} %collective-permute-done.4), channel_id=1, source_target_pairs={{0,1},{1,0},{2,3},{3,2},{4,5},{5,4},{6,7},{7,6},{8,9},{9,8},{10,11... | collective-permute-start | bytes 1572872 | tf_op jit(solution)/shard_map/ppermute | solution.py:30
  82.1 53.6 %all-to-all-start.1 = ((bf16[8,256,512]{2,1,0:T(8,128)(2,1)}), bf16[8,256,512]{2,1,0:T(8,128)(2,1)S(1)}, u32[]{:S(2)}, u32[]{:S(2)}) async-start(bf16[8,256,512]{2,1,0:T(8,128)(2,1)} %pad_maximum_fusion.1), calls=%async_computation.1 | async-start | bytes 4194304 | tf_op jit(solution)/shard_map/all_to_all | solution.py:75
  85.7 176.7 %all-gather.10.cloned.1.call-start = ((), (), s32[]{:S(2)}) async-start(), calls=%async_computation.10 | async-start | bytes 5242880 | tf_op jit(solution)/shard_map/all_gather | solution.py:291
  137.2 131.5 %all-gather.12.cloned.1.call-start = ((), (), s32[]{:S(2)}) async-start(), calls=%async_computation.11 | async-start | bytes 5242880 | tf_op jit(solution)/shard_map/all_gather | solution.py:291
  154.9 21.8 %collective-permute-start.13 = (bf16[128,2048]{1,0:T(8,128)(2,1)S(1)}, bf16[128,2048]{1,0:T(8,128)(2,1)S(1)}, u32[]{:S(2)}, u32[]{:S(2)}) collective-permute-start(bf16[128,2048]{1,0:T(8,128)(2,1)S(1)} %get-tuple-element.115), channel_id=1, source_target_pairs={{0,1},{1,0},{2,3},{3,2},{4,5},{5,4},{6,7},{7,6},{8,9},{9,8},{10,11... | collective-permute-start | bytes 1572872 | tf_op jit(solution)/shard_map/ppermute | solution.py:30
  155.8 53.8 %all-to-all-start.2 = ((bf16[8,256,256]{2,1,0:T(8,128)(2,1)}), bf16[8,256,256]{2,1,0:T(8,128)(2,1)S(1)}, u32[]{:S(2)}, u32[]{:S(2)}) async-start(bf16[8,256,256]{2,1,0:T(8,128)(2,1)} %get-tuple-element.54), calls=%async_computation.2 | async-start | bytes 2097152 | tf_op jit(solution)/shard_map/all_to_all | solution.py:75
  160.6 124.6 %all-gather.14.cloned.1.call-start = ((), (), s32[]{:S(2)}) async-start(), calls=%async_computation.12 | async-start | bytes 5242880 | tf_op jit(solution)/shard_map/all_gather | solution.py:291
  160.7 31.6 %collective-permute-start.12 = (bf16[128,2048]{1,0:T(8,128)(2,1)}, bf16[128,2048]{1,0:T(8,128)(2,1)}, u32[]{:S(2)}, u32[]{:S(2)}) collective-permute-start(bf16[128,2048]{1,0:T(8,128)(2,1)} %get-tuple-element.112), channel_id=1, source_target_pairs={{0,1},{1,0},{2,3},{3,2},{4,5},{5,4},{6,7},{7,6},{8,9},{9,8},{10,11... | collective-permute-start | bytes 1572872 | tf_op jit(solution)/shard_map/ppermute | solution.py:30
  178.0 25.2 %collective-permute-start.16 = (bf16[128,2048]{1,0:T(8,128)(2,1)}, bf16[128,2048]{1,0:T(8,128)(2,1)}, u32[]{:S(2)}, u32[]{:S(2)}) collective-permute-start(bf16[128,2048]{1,0:T(8,128)(2,1)} %get-tuple-element.114), channel_id=1, source_target_pairs={{0,1},{1,0},{2,3},{3,2},{4,5},{5,4},{6,7},{7,6},{8,9},{9,8},{10,11... | collective-permute-start | bytes 1572872 | tf_op jit(solution)/shard_map/ppermute | solution.py:30
  180.2 31.8 %collective-permute-start.18 = (bf16[128,2048]{1,0:T(8,128)(2,1)}, bf16[128,2048]{1,0:T(8,128)(2,1)}, u32[]{:S(2)}, u32[]{:S(2)}) collective-permute-start(bf16[128,2048]{1,0:T(8,128)(2,1)} %get-tuple-element.113), channel_id=1, source_target_pairs={{0,1},{1,0},{2,3},{3,2},{4,5},{5,4},{6,7},{7,6},{8,9},{9,8},{10,11... | collective-permute-start | bytes 1572872 | tf_op jit(solution)/shard_map/ppermute | solution.py:30
  210.6 266.7 %reduce-scatter.4.cloned.1.call-start = ((), (), s32[]{:S(2)}) async-start(), calls=%async_computation.13 | async-start | bytes 5242880 | tf_op jit(solution)/shard_map/reduce_scatter | solution.py:348
  252.9 24.5 %collective-permute-start.25 = (bf16[128,2048]{1,0:T(8,128)(2,1)}, bf16[128,2048]{1,0:T(8,128)(2,1)S(1)}, u32[]{:S(2)}, u32[]{:S(2)}) collective-permute-start(bf16[128,2048]{1,0:T(8,128)(2,1)} %collective-permute-done.20), channel_id=1, source_target_pairs={{0,1},{1,0},{2,3},{3,2},{4,5},{5,4},{6,7},{7,6},{8,9},{9,8},{10,11... | collective-permute-start | bytes 1572872 | tf_op jit(solution)/shard_map/ppermute | solution.py:30
  290.5 30.6 %collective-permute-start.26 = (bf16[128,2048]{1,0:T(8,128)(2,1)S(1)}, bf16[128,2048]{1,0:T(8,128)(2,1)S(1)}, u32[]{:S(2)}, u32[]{:S(2)}) collective-permute-start(bf16[128,2048]{1,0:T(8,128)(2,1)S(1)} %get-tuple-element.130), channel_id=1, source_target_pairs={{0,1},{1,0},{2,3},{3,2},{4,5},{5,4},{6,7},{7,6},{8,9},{9,8},{10,11... | collective-permute-start | bytes 1572872 | tf_op jit(solution)/shard_map/ppermute | solution.py:30
  292.5 23.3 %collective-permute-start.27 = (bf16[128,2048]{1,0:T(8,128)(2,1)S(1)}, bf16[128,2048]{1,0:T(8,128)(2,1)S(1)}, u32[]{:S(2)}, u32[]{:S(2)}) collective-permute-start(bf16[128,2048]{1,0:T(8,128)(2,1)S(1)} %get-tuple-element.133), channel_id=1, source_target_pairs={{0,1},{1,0},{2,3},{3,2},{4,5},{5,4},{6,7},{7,6},{8,9},{9,8},{10,11... | collective-permute-start | bytes 1572872 | tf_op jit(solution)/shard_map/ppermute | solution.py:30
  408.7 139.8 %reduce-scatter.6.cloned.1.call-start = ((), (), s32[]{:S(2)}) async-start(), calls=%async_computation.14 | async-start | bytes 5242880 | tf_op jit(solution)/shard_map/reduce_scatter | solution.py:348
  418.6 192.3 %reduce-scatter.8.cloned.1.call-start = ((), (), s32[]{:S(2)}) async-start(), calls=%async_computation.15 | async-start | bytes 5242880 | tf_op jit(solution)/shard_map/reduce_scatter | solution.py:348
  499.9 22.9 %collective-permute-start.53 = (bf16[128,2048]{1,0:T(8,128)(2,1)S(1)}, bf16[128,2048]{1,0:T(8,128)(2,1)S(1)}, u32[]{:S(2)}, u32[]{:S(2)}) collective-permute-start(bf16[128,2048]{1,0:T(8,128)(2,1)S(1)} %collective-permute-done.50), channel_id=1, source_target_pairs={{0,1},{1,0},{2,3},{3,2},{4,5},{5,4},{6,7},{7,6},{8,9},{9,8},{10,11... | collective-permute-start | bytes 1572872 | tf_op jit(solution)/shard_map/ppermute | solution.py:30
  548.6 34.5 %all-to-all-start.4 = ((bf16[8,256,256]{2,1,0:T(8,128)(2,1)}), bf16[8,256,256]{2,1,0:T(8,128)(2,1)S(1)}, u32[]{:S(2)}, u32[]{:S(2)}) async-start(bf16[8,256,256]{2,1,0:T(8,128)(2,1)} %bitcast.248), calls=%async_computation.6 | async-start | bytes 2097152 | tf_op jit(solution)/shard_map/all_to_all | solution.py:75
  552.1 157.5 %all-gather.16.cloned.1.call-start = ((), (), s32[]{:S(2)}) async-start(), calls=%async_computation.16 | async-start | bytes 5242880 | tf_op jit(solution)/shard_map/all_gather | solution.py:354
  552.3 24.2 %collective-permute-start.56 = (f32[48,128]{1,0:T(8,128)S(1)}, f32[48,128]{1,0:T(8,128)S(1)}, u32[]{:S(2)}, u32[]{:S(2)}) collective-permute-start(f32[48,128]{1,0:T(8,128)S(1)} %fusion.183), channel_id=1, source_target_pairs={{0,4},{1,5},{2,6},{3,7},{4,0},{5,1},{6,2},{7,3},{8,12},{9,13},{10,... | collective-permute-start | bytes 73736 | tf_op jit(solution)/shard_map/ppermute | solution.py:30
  584.1 133.8 %all-gather.18.cloned.1.call-start = ((), (), s32[]{:S(2)}) async-start(), calls=%async_computation.17 | async-start | bytes 5242880 | tf_op jit(solution)/shard_map/all_gather | solution.py:354
  615.2 110.4 %all-gather.20.cloned.1.call-start = ((), (), s32[]{:S(2)}) async-start(), calls=%async_computation.18 | async-start | bytes 5242880 | tf_op jit(solution)/shard_map/all_gather | solution.py:354
  628.3 22.2 %collective-permute-start.64 = (bf16[2,8,64,1024]{3,2,1,0:T(8,128)(2,1)}, bf16[2,8,64,1024]{3,2,1,0:T(8,128)(2,1)}, u32[]{:S(2)}, u32[]{:S(2)}) collective-permute-start(bf16[2,8,64,1024]{3,2,1,0:T(8,128)(2,1)} %pad_maximum_fusion.2), channel_id=1, source_target_pairs={{0,8},{8,0},{16,24},{24,16},{1,9},{9,1},{17,25},{25,17},{2,10},{10... | collective-permute-start | bytes 6291464 | tf_op jit(solution)/shard_map/ppermute | solution.py:30
  635.3 25.2 %collective-permute-start.57 = (bf16[128,2048]{1,0:T(8,128)(2,1)S(1)}, bf16[128,2048]{1,0:T(8,128)(2,1)S(1)}, u32[]{:S(2)}, u32[]{:S(2)}) collective-permute-start(bf16[128,2048]{1,0:T(8,128)(2,1)S(1)} %get-tuple-element.102), channel_id=1, source_target_pairs={{0,1},{1,0},{2,3},{3,2},{4,5},{5,4},{6,7},{7,6},{8,9},{9,8},{10,11... | collective-permute-start | bytes 1572872 | tf_op jit(solution)/shard_map/ppermute | solution.py:30
  636.3 31.5 %collective-permute-start.61 = (bf16[128,2048]{1,0:T(8,128)(2,1)S(1)}, bf16[128,2048]{1,0:T(8,128)(2,1)S(1)}, u32[]{:S(2)}, u32[]{:S(2)}) collective-permute-start(bf16[128,2048]{1,0:T(8,128)(2,1)S(1)} %get-tuple-element.104), channel_id=1, source_target_pairs={{0,1},{1,0},{2,3},{3,2},{4,5},{5,4},{6,7},{7,6},{8,9},{9,8},{10,11... | collective-permute-start | bytes 1572872 | tf_op jit(solution)/shard_map/ppermute | solution.py:30
  652.0 34.8 %collective-permute-start.65 = (bf16[8,64,1024]{2,1,0:T(8,128)(2,1)S(1)}, bf16[8,64,1024]{2,1,0:T(8,128)(2,1)S(1)}, u32[]{:S(2)}, u32[]{:S(2)}) collective-permute-start(bf16[8,64,1024]{2,1,0:T(8,128)(2,1)S(1)} %fusion.12), channel_id=1, source_target_pairs={{0,16},{8,24},{16,0},{24,8},{1,17},{9,25},{17,1},{25,9},{2,18},{10... | collective-permute-start | bytes 3145736 | tf_op jit(solution)/shard_map/ppermute | solution.py:30
  (149 other events, 1610.7 us)
Sparse Core Ops, SparseCore 0:
  137.3 34.7 all-gather.9
  174.2 34.9 all-gather.11
  210.8 35.0 all-gather.13
  408.8 47.1 reduce-scatter.3
  458.6 44.5 reduce-scatter.5
  505.5 44.5 reduce-scatter.7
  584.2 32.2 all-gather.15
  618.2 34.5 all-gather.17
  654.4 43.1 all-gather.19

commit v4 on v3

--- a/solution.py
+++ b/solution.py
@@ -120,12 +120,13 @@
 def lay_rows(rep, here, there):
     _, groups, rows, wide = here.shape
     width = groups * wide // 4
-    spec = pl.BlockSpec((1, groups, rows, wide), lambda j, rep_ref: (j // 2, 0, 0, 0))
-    out = pl.BlockSpec((rows, width), lambda j, rep_ref: (rep_ref[0] ^ j, 0))
+    half = rows // 2
+    spec = pl.BlockSpec((1, groups, half, wide), lambda j, h, rep_ref: (j // 2, 0, h, 0))
+    out = pl.BlockSpec((half, width), lambda j, h, rep_ref: ((rep_ref[0] ^ j) * 2 + h, 0))
     return pl.pallas_call(
         lay_kernel,
         grid_spec=pltpu.PrefetchScalarGridSpec(
-            num_scalar_prefetch=1, grid=(4,), in_specs=[spec, spec], out_specs=[out] * 4
+            num_scalar_prefetch=1, grid=(4, 2), in_specs=[spec, spec], out_specs=[out] * 4
         ),
         out_shape=[jax.ShapeDtypeStruct((4 * rows, width), F32)] * 4,
         cost_estimate=pl.CostEstimate(flops=0, bytes_accessed=here.size * 12, transcendentals=0),
@@ -168,13 +169,14 @@
 
 def widen(parts, turned):
     reps, count, rows, wide = parts.shape
-    out = (rows, reps * wide) if not turned else (reps * wide, rows)
+    half = rows // 2
+    out = (half, reps * wide) if not turned else (reps * wide, half)
     full = (rows, reps * count * wide) if not turned else (reps * count * wide, rows)
     return pl.pallas_call(
         widen_turned_kernel if turned else widen_kernel,
-        grid=(count,),
-        in_specs=[pl.BlockSpec((reps, 1, rows, wide), lambda s: (0, s, 0, 0))],
-        out_specs=pl.BlockSpec(out, (lambda s: (s, 0)) if turned else (lambda s: (0, s))),
+        grid=(count, 2),
+        in_specs=[pl.BlockSpec((reps, 1, half, wide), lambda s, h: (0, s, h, 0))],
+        out_specs=pl.BlockSpec(out, (lambda s, h: (s, h)) if turned else (lambda s, h: (h, s))),
         out_shape=jax.ShapeDtypeStruct(full, F32),
         cost_estimate=pl.CostEstimate(flops=0, bytes_accessed=parts.size * 6, transcendentals=0),
     )(parts)

time: 786 us -> 797 us (1.014)
  Pallas kernels: 35.5 us -> 48.2 us
    pallas_call x3, Pallas kernels: 22.4 us -> 33.3 us  [widen(): pl.pallas_call(widen_turned_kernel if turned else widen_kernel, grid=(cou...]
  transfers between devices with their start and end apart: 85 -> 85, of which waited for: 47 -> 46; matrix products, arithmetic and copies ran while one was open for 21% -> 21% of each run, Pallas kernels for 4% -> 5%
where the time goes in v4:
time: 797 us; the launch traced here: 782 us
  waiting for transfers between devices  354 us (44%)
  starting transfers between devices  118 us (15%)
  matrix products  113 us (14%)
  local copies, waits for them, and re-layouts  59.3 us (7%)
  Pallas kernels  48.2 us (6%)
  other arithmetic  47.4 us (6%)
  blocking collectives  26.8 us (3%)
  between operations  16.3 us (2%)
    ppermute x70, waiting for transfers between devices, shuffle(): lax.ppermute(value, axis, [(i, i ^ step) for i in range(lax.axis_size(axi...  337 us
    dot_general x24, matrix products, dot(): lax.dot_general(left, right, (dims, ((), ())), preferred_element_type=kind)  96.3 us
    ppermute x70, starting transfers between devices, shuffle(): lax.ppermute(value, axis, [(i, i ^ step) for i in range(lax.axis_size(axi...  88.8 us
    pallas_call x3, Pallas kernels, widen(): pl.pallas_call(widen_turned_kernel if turned else widen_kernel, grid=(cou...  33.3 us
    all_to_all x6, starting transfers between devices, to_columns(): return lax.all_to_all(blocks, 'grp', 0, 0, tiled=True)  27.7 us
    unnamed x205, local copies, waits for them, and re-layouts  27.3 us
    all_to_all x1, blocking collectives, to_columns(): return lax.all_to_all(blocks, 'grp', 0, 0, tiled=True)  26.8 us
    all_to_all x6, waiting for transfers between devices, to_columns(): return lax.all_to_all(blocks, 'grp', 0, 0, tiled=True)  16 us
  transfers between devices with their start and end apart: 85, of which 46 were waited for; matrix products, arithmetic and copies ran while one was open for 21% of the time, Pallas kernels for 5%

profile of v4, /device:TPU:0, one launch (start us, length us, event | category | flops | bytes accessed | tf_op | source)
XLA Modules:
  0.0 782.3 jit_solution(14362411519695978863)
XLA Ops:
  11.5 7.3 all-to-all-start
  33.8 16.1 %collective-permute-done.3 = bf16[128,2048]{1,0:T(8,128)(2,1)S(1)} collective-permute-done((bf16[128,2048]{1,0:T(8,128)(2,1)S(1)}, bf16[128,2048]{1,0:T(8,128)(2,1)S(1)}, u32[]{:S(2)}, u32[]{:S(2)}) %collective-permute-start.3) | collective-permute-done | bytes 524320 | tf_op jit(solution)/shard_map/ppermute | solution.py:30
  49.9 14.3 %collective-permute-start.4 = (bf16[128,2048]{1,0:T(8,128)(2,1)S(1)}, bf16[128,2048]{1,0:T(8,128)(2,1)}, u32[]{:S(2)}, u32[]{:S(2)}) collective-permute-start(bf16[128,2048]{1,0:T(8,128)(2,1)S(1)} %collective-permute-done.3), channel_id=1, source_target_pairs={{0,2},{1,3},{2,0},{3,1},{4,6},{5,7},{6,4},{7,5},{8,10},{9,11},{10,... | collective-permute-start | bytes 1572872 | tf_op jit(solution)/shard_map/ppermute | solution.py:30
  67.4 11.7 %collective-permute-done.6 = bf16[128,2048]{1,0:T(8,128)(2,1)S(1)} collective-permute-done((bf16[128,2048]{1,0:T(8,128)(2,1)S(1)}, bf16[128,2048]{1,0:T(8,128)(2,1)S(1)}, u32[]{:S(2)}, u32[]{:S(2)}) %collective-permute-start.6) | collective-permute-done | bytes 524320 | tf_op jit(solution)/shard_map/ppermute | solution.py:30
  88.5 12.2 %collective-permute-done.2 = bf16[128,2048]{1,0:T(8,128)(2,1)} collective-permute-done((bf16[128,2048]{1,0:T(8,128)(2,1)}, bf16[128,2048]{1,0:T(8,128)(2,1)}, u32[]{:S(2)}, u32[]{:S(2)}) %collective-permute-start.2) | collective-permute-done | bytes 524320 | tf_op jit(solution)/shard_map/ppermute | solution.py:30
  105.7 10.8 %collective-permute-done.5 = bf16[128,2048]{1,0:T(8,128)(2,1)} collective-permute-done((bf16[128,2048]{1,0:T(8,128)(2,1)}, bf16[128,2048]{1,0:T(8,128)(2,1)}, u32[]{:S(2)}, u32[]{:S(2)}) %collective-permute-start.5) | collective-permute-done | bytes 524320 | tf_op jit(solution)/shard_map/ppermute | solution.py:30
  162.6 14.1 %collective-permute-done.13 = bf16[128,2048]{1,0:T(8,128)(2,1)S(1)} collective-permute-done((bf16[128,2048]{1,0:T(8,128)(2,1)S(1)}, bf16[128,2048]{1,0:T(8,128)(2,1)S(1)}, u32[]{:S(2)}, u32[]{:S(2)}) %collective-permute-start.13) | collective-permute-done | bytes 524320 | tf_op jit(solution)/shard_map/ppermute | solution.py:30
  180.3 12.0 %collective-permute-done.12 = bf16[128,2048]{1,0:T(8,128)(2,1)} collective-permute-done((bf16[128,2048]{1,0:T(8,128)(2,1)}, bf16[128,2048]{1,0:T(8,128)(2,1)}, u32[]{:S(2)}, u32[]{:S(2)}) %collective-permute-start.12) | collective-permute-done | bytes 524320 | tf_op jit(solution)/shard_map/ppermute | solution.py:30
  192.3 10.9 %collective-permute-done.16 = bf16[128,2048]{1,0:T(8,128)(2,1)} collective-permute-done((bf16[128,2048]{1,0:T(8,128)(2,1)}, bf16[128,2048]{1,0:T(8,128)(2,1)}, u32[]{:S(2)}, u32[]{:S(2)}) %collective-permute-start.16) | collective-permute-done | bytes 524320 | tf_op jit(solution)/shard_map/ppermute | solution.py:30
  212.0 6.7 collective-permute-done.17
  219.5 10.4 %collective-permute-done.15 = bf16[128,2048]{1,0:T(8,128)(2,1)} collective-permute-done((bf16[128,2048]{1,0:T(8,128)(2,1)}, bf16[128,2048]{1,0:T(8,128)(2,1)}, u32[]{:S(2)}, u32[]{:S(2)}) %collective-permute-start.15) | collective-permute-done | bytes 524320 | tf_op jit(solution)/shard_map/ppermute | solution.py:30
  234.4 12.2 %collective-permute-done.19 = bf16[128,2048]{1,0:T(8,128)(2,1)S(1)} collective-permute-done((bf16[128,2048]{1,0:T(8,128)(2,1)S(1)}, bf16[128,2048]{1,0:T(8,128)(2,1)S(1)}, u32[]{:S(2)}, u32[]{:S(2)}) %collective-permute-start.19) | collective-permute-done | bytes 524320 | tf_op jit(solution)/shard_map/ppermute | solution.py:30
  268.7 7.6 multiply_convert_fusion.4
  295.2 20.7 %collective-permute-done.27 = bf16[128,2048]{1,0:T(8,128)(2,1)S(1)} collective-permute-done((bf16[128,2048]{1,0:T(8,128)(2,1)S(1)}, bf16[128,2048]{1,0:T(8,128)(2,1)S(1)}, u32[]{:S(2)}, u32[]{:S(2)}) %collective-permute-start.27) | collective-permute-done | bytes 524320 | tf_op jit(solution)/shard_map/ppermute | solution.py:30
  330.4 9.0 %collective-permute-done.32 = bf16[128,2048]{1,0:T(8,128)(2,1)S(1)} collective-permute-done((bf16[128,2048]{1,0:T(8,128)(2,1)S(1)}, bf16[128,2048]{1,0:T(8,128)(2,1)S(1)}, u32[]{:S(2)}, u32[]{:S(2)}) %collective-permute-start.32) | collective-permute-done | bytes 524320 | tf_op jit(solution)/shard_map/ppermute | solution.py:30
  354.5 9.3 %collective-permute-done.33 = bf16[128,2048]{1,0:T(8,128)(2,1)S(1)} collective-permute-done((bf16[128,2048]{1,0:T(8,128)(2,1)S(1)}, bf16[128,2048]{1,0:T(8,128)(2,1)S(1)}, u32[]{:S(2)}, u32[]{:S(2)}) %collective-permute-start.33) | collective-permute-done | bytes 524320 | tf_op jit(solution)/shard_map/ppermute | solution.py:30
  394.9 7.1 multiply_convert_fusion.1
  424.1 11.5 %collective-permute-done.41 = bf16[128,2048]{1,0:T(8,128)(2,1)S(1)} collective-permute-done((bf16[128,2048]{1,0:T(8,128)(2,1)S(1)}, bf16[128,2048]{1,0:T(8,128)(2,1)S(1)}, u32[]{:S(2)}, u32[]{:S(2)}) %collective-permute-start.41) | collective-permute-done | bytes 524320 | tf_op jit(solution)/shard_map/ppermute | solution.py:30
  463.3 11.8 %collective-permute-done.43 = bf16[128,2048]{1,0:T(8,128)(2,1)} collective-permute-done((bf16[128,2048]{1,0:T(8,128)(2,1)S(1)}, bf16[128,2048]{1,0:T(8,128)(2,1)}, u32[]{:S(2)}, u32[]{:S(2)}) %collective-permute-start.43) | collective-permute-done | bytes 524320 | tf_op jit(solution)/shard_map/ppermute | solution.py:30
  487.0 8.6 %collective-permute-done.50 = bf16[128,2048]{1,0:T(8,128)(2,1)S(1)} collective-permute-done((bf16[128,2048]{1,0:T(8,128)(2,1)}, bf16[128,2048]{1,0:T(8,128)(2,1)S(1)}, u32[]{:S(2)}, u32[]{:S(2)}) %collective-permute-start.50) | collective-permute-done | bytes 524320 | tf_op jit(solution)/shard_map/ppermute | solution.py:30
  507.1 8.5 %collective-permute-done.49 = bf16[128,2048]{1,0:T(8,128)(2,1)S(1)} collective-permute-done((bf16[128,2048]{1,0:T(8,128)(2,1)S(1)}, bf16[128,2048]{1,0:T(8,128)(2,1)S(1)}, u32[]{:S(2)}, u32[]{:S(2)}) %collective-permute-start.49) | collective-permute-done | bytes 524320 | tf_op jit(solution)/shard_map/ppermute | solution.py:30
  560.3 16.2 %collective-permute-done.56 = f32[48,128]{1,0:T(8,128)S(1)} collective-permute-done((f32[48,128]{1,0:T(8,128)S(1)}, f32[48,128]{1,0:T(8,128)S(1)}, u32[]{:S(2)}, u32[]{:S(2)}) %collective-permute-start.56) | collective-permute-done | bytes 24608 | tf_op jit(solution)/shard_map/ppermute | solution.py:30
  584.1 26.8 %all_to_all.35 = bf16[8,256,256]{2,1,0:T(8,128)(2,1)} all-to-all(bf16[8,256,256]{2,1,0:T(8,128)(2,1)} %bitcast.247), channel_id=1, replica_groups=mesh['rep'=4,'grp'=8] {'grp'}, dimensions={0} | all-to-all | bytes 2097152 | tf_op jit(solution)/shard_map/all_to_all | solution.py:75
  637.3 11.9 %collective-permute-done.58 = bf16[128,2048]{1,0:T(8,128)(2,1)S(1)} collective-permute-done((bf16[128,2048]{1,0:T(8,128)(2,1)S(1)}, bf16[128,2048]{1,0:T(8,128)(2,1)S(1)}, u32[]{:S(2)}, u32[]{:S(2)}) %collective-permute-start.58) | collective-permute-done | bytes 524320 | tf_op jit(solution)/shard_map/ppermute | solution.py:30
  652.8 7.6 collective-permute-done.57
  660.4 7.4 collective-permute-done.61
  672.0 14.8 %collective-permute-done.65 = bf16[8,64,1024]{2,1,0:T(8,128)(2,1)S(1)} collective-permute-done((bf16[8,64,1024]{2,1,0:T(8,128)(2,1)S(1)}, bf16[8,64,1024]{2,1,0:T(8,128)(2,1)S(1)}, u32[]{:S(2)}, u32[]{:S(2)}) %collective-permute-start.65) | collective-permute-done | bytes 1048608 | tf_op jit(solution)/shard_map/ppermute | solution.py:30
  695.7 12.6 %all-to-all-done.3 = bf16[8,64,768]{2,1,0:T(8,128)(2,1)} async-done(((bf16[8,64,768]{2,1,0:T(8,128)(2,1)}), bf16[8,64,768]{2,1,0:T(8,128)(2,1)}, u32[]{:S(2)}, u32[]{:S(2)}) %all-to-all-start.3) | async-done | bytes 786464 | tf_op jit(solution)/shard_map/all_to_all | solution.py:75
  709.6 10.8 %shard_map.229 = f32[256,8192]{1,0:T(8,128)} custom-call(bf16[4,8,256,256]{3,2,1,0:T(8,128)(2,1)} %bitcast.222), custom_call_target="tpu_custom_call" | custom-call | bytes 12582912 | tf_op jit(solution)/shard_map/pallas_call | solution.py:175
  721.4 11.6 %shard_map.230 = f32[8192,256]{1,0:T(8,128)} custom-call(bf16[4,8,256,256]{3,2,1,0:T(8,128)(2,1)} %bitcast.223), custom_call_target="tpu_custom_call" | custom-call | bytes 12582912 | tf_op jit(solution)/shard_map/pallas_call | solution.py:175
  733.0 10.8 %shard_map.231 = f32[256,8192]{1,0:T(8,128)} custom-call(bf16[4,8,256,256]{3,2,1,0:T(8,128)(2,1)} %bitcast.224), custom_call_target="tpu_custom_call" | custom-call | bytes 12582912 | tf_op jit(solution)/shard_map/pallas_call | solution.py:175
  766.5 8.8 %shard_map.232 = (f32[256,2048]{1,0:T(8,128)}, f32[256,2048]{1,0:T(8,128)}, f32[256,2048]{1,0:T(8,128)}, f32[256,2048]{1,0:T(8,128)}) custom-call(s32[1]{0:T(128)} %bitcast.30.rep_ref, bf16[2,8,64,1024]{3,2,1,0:T(8,128)(2,1)} %pad_maximum_fusion.3.here_ref, bf16[2,8,64,1024]{3,2,1,0:T(8,128)(2,1)} %collective-permute-done.67.there_ref), custom_call_target="tpu_custom_call" | custom-call | bytes 12582912 | tf_op jit(solution)/shard_map/pallas_call | solution.py:126
  (498 shorter events, 393.8 us)
Async XLA Ops:
  11.5 69.7 %all-to-all-start = ((bf16[8,72,768]{2,1,0:T(8,128)(2,1)}), bf16[8,72,768]{2,1,0:T(8,128)(2,1)S(1)}, u32[]{:S(2)}, u32[]{:S(2)}) async-start(bf16[8,72,768]{2,1,0:T(8,128)(2,1)} %copy.61), calls=%async_computation | async-start | bytes 1769472 | tf_op jit(solution)/shard_map/all_to_all | solution.py:75
  18.8 31.1 %collective-permute-start.3 = (bf16[128,2048]{1,0:T(8,128)(2,1)S(1)}, bf16[128,2048]{1,0:T(8,128)(2,1)S(1)}, u32[]{:S(2)}, u32[]{:S(2)}) collective-permute-start(bf16[128,2048]{1,0:T(8,128)(2,1)S(1)} %bitcast.219), channel_id=1, source_target_pairs={{0,6},{1,7},{2,4},{3,5},{4,2},{5,3},{6,0},{7,1},{8,14},{9,15},{10,... | collective-permute-start | bytes 1572872 | tf_op jit(solution)/shard_map/ppermute | solution.py:30
  22.6 42.9 %collective-permute-start.1 = (bf16[128,2048]{1,0:T(8,128)(2,1)S(1)}, bf16[128,2048]{1,0:T(8,128)(2,1)}, u32[]{:S(2)}, u32[]{:S(2)}) collective-permute-start(bf16[128,2048]{1,0:T(8,128)(2,1)S(1)} %bitcast.220), channel_id=1, source_target_pairs={{0,2},{1,3},{2,0},{3,1},{4,6},{5,7},{6,4},{7,5},{8,10},{9,11},{10,... | collective-permute-start | bytes 1572872 | tf_op jit(solution)/shard_map/ppermute | solution.py:30
  22.6 43.6 %collective-permute-start = (bf16[128,2048]{1,0:T(8,128)(2,1)S(1)}, bf16[128,2048]{1,0:T(8,128)(2,1)S(1)}, u32[]{:S(2)}, u32[]{:S(2)}) collective-permute-start(bf16[128,2048]{1,0:T(8,128)(2,1)S(1)} %bitcast.221), channel_id=1, source_target_pairs={{0,1},{1,0},{2,3},{3,2},{4,5},{5,4},{6,7},{7,6},{8,9},{9,8},{10,11... | collective-permute-start | bytes 1572872 | tf_op jit(solution)/shard_map/ppermute | solution.py:30
  49.9 29.2 %collective-permute-start.4 = (bf16[128,2048]{1,0:T(8,128)(2,1)S(1)}, bf16[128,2048]{1,0:T(8,128)(2,1)}, u32[]{:S(2)}, u32[]{:S(2)}) collective-permute-start(bf16[128,2048]{1,0:T(8,128)(2,1)S(1)} %collective-permute-done.3), channel_id=1, source_target_pairs={{0,2},{1,3},{2,0},{3,1},{4,6},{5,7},{6,4},{7,5},{8,10},{9,11},{10,... | collective-permute-start | bytes 1572872 | tf_op jit(solution)/shard_map/ppermute | solution.py:30
  65.5 35.2 %collective-permute-start.2 = (bf16[128,2048]{1,0:T(8,128)(2,1)}, bf16[128,2048]{1,0:T(8,128)(2,1)}, u32[]{:S(2)}, u32[]{:S(2)}) collective-permute-start(bf16[128,2048]{1,0:T(8,128)(2,1)} %collective-permute-done.1), channel_id=1, source_target_pairs={{0,1},{1,0},{2,3},{3,2},{4,5},{5,4},{6,7},{7,6},{8,9},{9,8},{10,11... | collective-permute-start | bytes 1572872 | tf_op jit(solution)/shard_map/ppermute | solution.py:30
  79.8 36.7 %collective-permute-start.5 = (bf16[128,2048]{1,0:T(8,128)(2,1)}, bf16[128,2048]{1,0:T(8,128)(2,1)}, u32[]{:S(2)}, u32[]{:S(2)}) collective-permute-start(bf16[128,2048]{1,0:T(8,128)(2,1)} %collective-permute-done.4), channel_id=1, source_target_pairs={{0,1},{1,0},{2,3},{3,2},{4,5},{5,4},{6,7},{7,6},{8,9},{9,8},{10,11... | collective-permute-start | bytes 1572872 | tf_op jit(solution)/shard_map/ppermute | solution.py:30
  82.1 53.6 %all-to-all-start.1 = ((bf16[8,256,512]{2,1,0:T(8,128)(2,1)}), bf16[8,256,512]{2,1,0:T(8,128)(2,1)S(1)}, u32[]{:S(2)}, u32[]{:S(2)}) async-start(bf16[8,256,512]{2,1,0:T(8,128)(2,1)} %pad_maximum_fusion.1), calls=%async_computation.1 | async-start | bytes 4194304 | tf_op jit(solution)/shard_map/all_to_all | solution.py:75
  85.7 176.7 %all-gather.10.cloned.1.call-start = ((), (), s32[]{:S(2)}) async-start(), calls=%async_computation.10 | async-start | bytes 5242880 | tf_op jit(solution)/shard_map/all_gather | solution.py:293
  137.2 131.5 %all-gather.12.cloned.1.call-start = ((), (), s32[]{:S(2)}) async-start(), calls=%async_computation.11 | async-start | bytes 5242880 | tf_op jit(solution)/shard_map/all_gather | solution.py:293
  155.8 53.8 %all-to-all-start.2 = ((bf16[8,256,256]{2,1,0:T(8,128)(2,1)}), bf16[8,256,256]{2,1,0:T(8,128)(2,1)S(1)}, u32[]{:S(2)}, u32[]{:S(2)}) async-start(bf16[8,256,256]{2,1,0:T(8,128)(2,1)} %get-tuple-element.54), calls=%async_computation.2 | async-start | bytes 2097152 | tf_op jit(solution)/shard_map/all_to_all | solution.py:75
  160.6 124.6 %all-gather.14.cloned.1.call-start = ((), (), s32[]{:S(2)}) async-start(), calls=%async_computation.12 | async-start | bytes 5242880 | tf_op jit(solution)/shard_map/all_gather | solution.py:293
  160.7 31.6 %collective-permute-start.12 = (bf16[128,2048]{1,0:T(8,128)(2,1)}, bf16[128,2048]{1,0:T(8,128)(2,1)}, u32[]{:S(2)}, u32[]{:S(2)}) collective-permute-start(bf16[128,2048]{1,0:T(8,128)(2,1)} %get-tuple-element.112), channel_id=1, source_target_pairs={{0,1},{1,0},{2,3},{3,2},{4,5},{5,4},{6,7},{7,6},{8,9},{9,8},{10,11... | collective-permute-start | bytes 1572872 | tf_op jit(solution)/shard_map/ppermute | solution.py:30
  178.0 25.2 %collective-permute-start.16 = (bf16[128,2048]{1,0:T(8,128)(2,1)}, bf16[128,2048]{1,0:T(8,128)(2,1)}, u32[]{:S(2)}, u32[]{:S(2)}) collective-permute-start(bf16[128,2048]{1,0:T(8,128)(2,1)} %get-tuple-element.114), channel_id=1, source_target_pairs={{0,1},{1,0},{2,3},{3,2},{4,5},{5,4},{6,7},{7,6},{8,9},{9,8},{10,11... | collective-permute-start | bytes 1572872 | tf_op jit(solution)/shard_map/ppermute | solution.py:30
  180.2 31.8 %collective-permute-start.18 = (bf16[128,2048]{1,0:T(8,128)(2,1)}, bf16[128,2048]{1,0:T(8,128)(2,1)}, u32[]{:S(2)}, u32[]{:S(2)}) collective-permute-start(bf16[128,2048]{1,0:T(8,128)(2,1)} %get-tuple-element.113), channel_id=1, source_target_pairs={{0,1},{1,0},{2,3},{3,2},{4,5},{5,4},{6,7},{7,6},{8,9},{9,8},{10,11... | collective-permute-start | bytes 1572872 | tf_op jit(solution)/shard_map/ppermute | solution.py:30
  210.6 266.7 %reduce-scatter.4.cloned.1.call-start = ((), (), s32[]{:S(2)}) async-start(), calls=%async_computation.13 | async-start | bytes 5242880 | tf_op jit(solution)/shard_map/reduce_scatter | solution.py:350
  252.9 24.5 %collective-permute-start.25 = (bf16[128,2048]{1,0:T(8,128)(2,1)}, bf16[128,2048]{1,0:T(8,128)(2,1)S(1)}, u32[]{:S(2)}, u32[]{:S(2)}) collective-permute-start(bf16[128,2048]{1,0:T(8,128)(2,1)} %collective-permute-done.20), channel_id=1, source_target_pairs={{0,1},{1,0},{2,3},{3,2},{4,5},{5,4},{6,7},{7,6},{8,9},{9,8},{10,11... | collective-permute-start | bytes 1572872 | tf_op jit(solution)/shard_map/ppermute | solution.py:30
  290.5 30.6 %collective-permute-start.26 = (bf16[128,2048]{1,0:T(8,128)(2,1)S(1)}, bf16[128,2048]{1,0:T(8,128)(2,1)S(1)}, u32[]{:S(2)}, u32[]{:S(2)}) collective-permute-start(bf16[128,2048]{1,0:T(8,128)(2,1)S(1)} %get-tuple-element.130), channel_id=1, source_target_pairs={{0,1},{1,0},{2,3},{3,2},{4,5},{5,4},{6,7},{7,6},{8,9},{9,8},{10,11... | collective-permute-start | bytes 1572872 | tf_op jit(solution)/shard_map/ppermute | solution.py:30
  292.5 23.3 %collective-permute-start.27 = (bf16[128,2048]{1,0:T(8,128)(2,1)S(1)}, bf16[128,2048]{1,0:T(8,128)(2,1)S(1)}, u32[]{:S(2)}, u32[]{:S(2)}) collective-permute-start(bf16[128,2048]{1,0:T(8,128)(2,1)S(1)} %get-tuple-element.133), channel_id=1, source_target_pairs={{0,1},{1,0},{2,3},{3,2},{4,5},{5,4},{6,7},{7,6},{8,9},{9,8},{10,11... | collective-permute-start | bytes 1572872 | tf_op jit(solution)/shard_map/ppermute | solution.py:30
  408.7 139.8 %reduce-scatter.6.cloned.1.call-start = ((), (), s32[]{:S(2)}) async-start(), calls=%async_computation.14 | async-start | bytes 5242880 | tf_op jit(solution)/shard_map/reduce_scatter | solution.py:350
  418.6 192.3 %reduce-scatter.8.cloned.1.call-start = ((), (), s32[]{:S(2)}) async-start(), calls=%async_computation.15 | async-start | bytes 5242880 | tf_op jit(solution)/shard_map/reduce_scatter | solution.py:350
  499.9 22.9 %collective-permute-start.53 = (bf16[128,2048]{1,0:T(8,128)(2,1)S(1)}, bf16[128,2048]{1,0:T(8,128)(2,1)S(1)}, u32[]{:S(2)}, u32[]{:S(2)}) collective-permute-start(bf16[128,2048]{1,0:T(8,128)(2,1)S(1)} %collective-permute-done.50), channel_id=1, source_target_pairs={{0,1},{1,0},{2,3},{3,2},{4,5},{5,4},{6,7},{7,6},{8,9},{9,8},{10,11... | collective-permute-start | bytes 1572872 | tf_op jit(solution)/shard_map/ppermute | solution.py:30
  548.6 34.5 %all-to-all-start.4 = ((bf16[8,256,256]{2,1,0:T(8,128)(2,1)}), bf16[8,256,256]{2,1,0:T(8,128)(2,1)S(1)}, u32[]{:S(2)}, u32[]{:S(2)}) async-start(bf16[8,256,256]{2,1,0:T(8,128)(2,1)} %bitcast.248), calls=%async_computation.6 | async-start | bytes 2097152 | tf_op jit(solution)/shard_map/all_to_all | solution.py:75
  552.1 157.5 %all-gather.16.cloned.1.call-start = ((), (), s32[]{:S(2)}) async-start(), calls=%async_computation.16 | async-start | bytes 5242880 | tf_op jit(solution)/shard_map/all_gather | solution.py:356
  552.3 24.2 %collective-permute-start.56 = (f32[48,128]{1,0:T(8,128)S(1)}, f32[48,128]{1,0:T(8,128)S(1)}, u32[]{:S(2)}, u32[]{:S(2)}) collective-permute-start(f32[48,128]{1,0:T(8,128)S(1)} %fusion.183), channel_id=1, source_target_pairs={{0,4},{1,5},{2,6},{3,7},{4,0},{5,1},{6,2},{7,3},{8,12},{9,13},{10,... | collective-permute-start | bytes 73736 | tf_op jit(solution)/shard_map/ppermute | solution.py:30
  584.1 137.3 %all-gather.18.cloned.1.call-start = ((), (), s32[]{:S(2)}) async-start(), calls=%async_computation.17 | async-start | bytes 5242880 | tf_op jit(solution)/shard_map/all_gather | solution.py:356
  615.2 117.8 %all-gather.20.cloned.1.call-start = ((), (), s32[]{:S(2)}) async-start(), calls=%async_computation.18 | async-start | bytes 5242880 | tf_op jit(solution)/shard_map/all_gather | solution.py:356
  628.3 22.2 %collective-permute-start.64 = (bf16[2,8,64,1024]{3,2,1,0:T(8,128)(2,1)}, bf16[2,8,64,1024]{3,2,1,0:T(8,128)(2,1)}, u32[]{:S(2)}, u32[]{:S(2)}) collective-permute-start(bf16[2,8,64,1024]{3,2,1,0:T(8,128)(2,1)} %pad_maximum_fusion.2), channel_id=1, source_target_pairs={{0,8},{8,0},{16,24},{24,16},{1,9},{9,1},{17,25},{25,17},{2,10},{10... | collective-permute-start | bytes 6291464 | tf_op jit(solution)/shard_map/ppermute | solution.py:30
  635.3 25.2 %collective-permute-start.57 = (bf16[128,2048]{1,0:T(8,128)(2,1)S(1)}, bf16[128,2048]{1,0:T(8,128)(2,1)S(1)}, u32[]{:S(2)}, u32[]{:S(2)}) collective-permute-start(bf16[128,2048]{1,0:T(8,128)(2,1)S(1)} %get-tuple-element.102), channel_id=1, source_target_pairs={{0,1},{1,0},{2,3},{3,2},{4,5},{5,4},{6,7},{7,6},{8,9},{9,8},{10,11... | collective-permute-start | bytes 1572872 | tf_op jit(solution)/shard_map/ppermute | solution.py:30
  636.3 31.5 %collective-permute-start.61 = (bf16[128,2048]{1,0:T(8,128)(2,1)S(1)}, bf16[128,2048]{1,0:T(8,128)(2,1)S(1)}, u32[]{:S(2)}, u32[]{:S(2)}) collective-permute-start(bf16[128,2048]{1,0:T(8,128)(2,1)S(1)} %get-tuple-element.104), channel_id=1, source_target_pairs={{0,1},{1,0},{2,3},{3,2},{4,5},{5,4},{6,7},{7,6},{8,9},{9,8},{10,11... | collective-permute-start | bytes 1572872 | tf_op jit(solution)/shard_map/ppermute | solution.py:30
  652.0 34.8 %collective-permute-start.65 = (bf16[8,64,1024]{2,1,0:T(8,128)(2,1)S(1)}, bf16[8,64,1024]{2,1,0:T(8,128)(2,1)S(1)}, u32[]{:S(2)}, u32[]{:S(2)}) collective-permute-start(bf16[8,64,1024]{2,1,0:T(8,128)(2,1)S(1)} %fusion.12), channel_id=1, source_target_pairs={{0,16},{8,24},{16,0},{24,8},{1,17},{9,25},{17,1},{25,9},{2,18},{10... | collective-permute-start | bytes 3145736 | tf_op jit(solution)/shard_map/ppermute | solution.py:30
  720.4 23.4 %collective-permute-start.66 = (bf16[8,64,1024]{2,1,0:T(8,128)(2,1)S(1)}, bf16[8,64,1024]{2,1,0:T(8,128)(2,1)}, u32[]{:S(2)}, u32[]{:S(2)}) collective-permute-start(bf16[8,64,1024]{2,1,0:T(8,128)(2,1)S(1)} %pad_maximum_fusion.8), channel_id=1, source_target_pairs={{0,16},{8,24},{16,0},{24,8},{1,17},{9,25},{17,1},{25,9},{2,18},{10... | collective-permute-start | bytes 3145736 | tf_op jit(solution)/shard_map/ppermute | solution.py:30
  (149 other events, 1615.1 us)
Sparse Core Ops, SparseCore 0:
  137.3 34.7 all-gather.9
  174.2 34.9 all-gather.11
  210.8 35.0 all-gather.13
  408.8 47.1 reduce-scatter.3
  458.6 44.5 reduce-scatter.5
  505.5 44.5 reduce-scatter.7
  584.2 32.2 all-gather.15
  618.2 34.5 all-gather.17
  654.4 43.1 all-gather.19
